TPU v7x, 32 devices: a whole 2x2x4 slice. The times are simulated.
32 devices in a mesh: dp: 8 (over z, x), mp: 4 (over y, core).
Axes of the slice: x: 2, y: 2, z: 4, core: 2. Of those that a mesh axis runs over, the one named last changes fastest.
Arguments:
- pixels_in: bfloat16 [6400, 320], P('dp', 'mp'), may hold values from -6 to 6
- cotangent: bfloat16 [6400, 320], P('dp'), may hold values from -6 to 6
- pixel_mask: int32 [6400], P('dp'), may hold values from 0 to 1, as said below
- tile_slot: int32 [8, 2], replicated, may hold values from 0 to 7, as said below
- ln1_gain: float32 [320], replicated, may hold values from 0.5 to 1.5
- ln1_bias: float32 [320], replicated, may hold values from -2 to 2
- w_query: bfloat16 [320, 320], replicated, may hold values from -0.3125 to 0.3125
- b_query: float32 [320], replicated, may hold values from -2 to 2
- w_key: bfloat16 [320, 320], replicated, may hold values from -0.3125 to 0.3125
- w_value: bfloat16 [320, 320], replicated, may hold values from -0.3125 to 0.3125
- b_value: float32 [320], replicated, may hold values from -2 to 2
- w_reduce: bfloat16 [1280, 320], replicated, may hold values from -0.15625 to 0.15625
- b_reduce: float32 [320], replicated, may hold values from -2 to 2
- lnr_gain: float32 [320], replicated, may hold values from 0.5 to 1.5
- lnr_bias: float32 [320], replicated, may hold values from -2 to 2
- w_out: bfloat16 [320, 320], replicated, may hold values from -2.5 to 2.5
- b_out: float32 [320], replicated, may hold values from -2 to 2
- ln2_gain: float32 [320], replicated, may hold values from 0.5 to 1.5
- ln2_bias: float32 [320], replicated, may hold values from -2 to 2
- w_fc1: bfloat16 [320, 1280], P(None, 'mp'), may hold values from -0.3125 to 0.3125
- b_fc1: float32 [1280], P('mp'), may hold values from -2 to 2
- w_depth: float32 [9, 1280], P(None, 'mp'), may hold values from -2 to 2
- b_depth: float32 [1280], P('mp'), may hold values from -2 to 2
- w_fc2: bfloat16 [1280, 320], P('mp'), may hold values from -0.3125 to 0.3125
- b_fc2: float32 [320], replicated, may hold values from -2 to 2
Outputs:
- block_out: bfloat16 [6400, 320], P('dp', 'mp')
- grad_pixels_in: float32 [6400, 320], P('dp', 'mp')
- grad_ln1_gain: float32 [320], replicated
- grad_ln1_bias: float32 [320], replicated
- grad_w_query: float32 [320, 320], replicated
- grad_b_query: float32 [320], replicated
- grad_w_key: float32 [320, 320], replicated
- grad_w_value: float32 [320, 320], replicated
- grad_b_value: float32 [320], replicated
- grad_w_reduce: float32 [1280, 320], replicated
- grad_b_reduce: float32 [320], replicated
- grad_lnr_gain: float32 [320], replicated
- grad_lnr_bias: float32 [320], replicated
- output_weight_gradient: float32 [320, 320], replicated
- grad_b_out: float32 [320], replicated
- grad_ln2_gain: float32 [320], replicated
- grad_ln2_bias: float32 [320], replicated
- grad_w_fc1: float32 [320, 1280], P(None, 'mp')
- grad_b_fc1: float32 [1280], P('mp')
- grad_w_depth: float32 [9, 1280], P(None, 'mp')
- grad_b_depth: float32 [1280], P('mp')
- grad_w_fc2: float32 [1280, 320], P('mp')
- grad_b_fc2: float32 [320], replicated
Inputs may be any that keep to these rules, and one draw needn't show every extreme that they name: `tile_slot`: row d names the crop (below 1) and tile (below 8) of device d; every pair of crop and tile appears exactly once. `pixel_mask`: 1 exactly inside the crop's square of side 64 or 80 at the frame's top-left corner.
All inputs are finite; a program needn't handle non-finite values.
Results may differ from a plain program's by a relative error of at most 0.024.
Values may be sent and summed in bfloat16 or wider, within the bound.
A program may use at most 128 MiB of HBM per device.

v0:
```python
import jax
import jax.numpy as jnp
from jax import lax
from jax.sharding import PartitionSpec as P

HEADS = 5
HEAD_FEATURES = 64
FRAME = 80
TILE_ROWS = 8


EPS = 1e-05
NEG = -1e30


def layer_norm(value, gain, shift):
    mean = jnp.mean(value, axis=-1, keepdims=True)
    centred = value - mean
    spread = jnp.mean(centred * centred, axis=-1, keepdims=True)
    return centred * lax.rsqrt(spread + EPS) * gain + shift


def depth_gelu(padded, kernel, shift):
    rows = padded.shape[0] - 2
    cols = padded.shape[1] - 2
    total = jnp.zeros((rows, cols, padded.shape[2]), jnp.float32) + shift
    for row_off in range(3):
        for col_off in range(3):
            total = (
                total
                + kernel[3 * row_off + col_off]
                * padded[row_off : row_off + rows, col_off : col_off + cols]
            )
    return jax.nn.gelu(total, approximate=False)


def mat(left, right):
    return jnp.dot(left, right, preferred_element_type=jnp.float32)


def pick(weights, table):
    return jnp.einsum(
        "j,jab->ab", weights.astype(table.dtype), table, preferred_element_type=jnp.float32
    )


def head_columns(weight_matrix, select_where):
    wide_layout = weight_matrix.astype(jnp.float32).reshape(
        weight_matrix.shape[0], HEADS, HEAD_FEATURES
    )
    return (
        jnp.einsum("uzx,nz->unx", wide_layout, select_where)
        .reshape(weight_matrix.shape[0], -1)
        .astype(jnp.bfloat16)
    )


def head_rows(weight_matrix, select_where):
    wide_layout = weight_matrix.astype(jnp.float32).reshape(
        HEADS, HEAD_FEATURES, weight_matrix.shape[1]
    )
    return (
        jnp.einsum("hed,sh->sed", wide_layout, select_where)
        .reshape(-1, weight_matrix.shape[1])
        .astype(jnp.bfloat16)
    )


def head_vector(vector_entries, select_where):
    return jnp.einsum(
        "he,sh->se", vector_entries.reshape(HEADS, HEAD_FEATURES), select_where
    ).reshape(-1)


def spread_columns(gradient_value, select_where):
    return jnp.einsum(
        "tvm,vq->tqm",
        gradient_value.reshape(gradient_value.shape[0], -1, HEAD_FEATURES),
        select_where,
    ).reshape(gradient_value.shape[0], -1)


def spread_rows(gradient_value, select_where):
    return jnp.einsum(
        "sed,sh->hed",
        gradient_value.reshape(-1, HEAD_FEATURES, gradient_value.shape[1]),
        select_where,
    ).reshape(-1, gradient_value.shape[1])


def spread_vector(gradient_value, select_where):
    return jnp.einsum("se,sh->he", gradient_value.reshape(-1, HEAD_FEATURES), select_where).reshape(
        -1
    )


def on_device(
    pixels_in,
    cotangent,
    pixel_mask,
    tile_slot,
    ln1_gain,
    ln1_bias,
    w_query,
    b_query,
    w_key,
    w_value,
    b_value,
    w_reduce,
    b_reduce,
    lnr_gain,
    lnr_bias,
    w_out,
    b_out,
    ln2_gain,
    ln2_bias,
    w_fc1,
    b_fc1,
    w_depth,
    b_depth,
    w_fc2,
    b_fc2,
):
    n_dp = lax.axis_size("dp")
    n_mp = lax.axis_size("mp")
    device = lax.axis_index("dp")
    part = lax.axis_index("mp")
    rows = FRAME // TILE_ROWS
    tokens = pixels_in.shape[0]
    cols = tokens // rows
    tiles_col = FRAME // cols
    per_frame = TILE_ROWS * tiles_col
    width = ln1_gain.shape[0]
    share = width // n_mp
    slots = -(-HEADS // n_mp)
    scale = HEAD_FEATURES ** (-0.5)
    maskf = pixel_mask.astype(jnp.float32)[:, None]
    head_ids = part + n_mp * jnp.arange(slots)
    select_where = (head_ids[:, None] == jnp.arange(HEADS)[None, :]).astype(jnp.float32)
    crops = tile_slot[:, 0]
    tiles = tile_slot[:, 1]
    is_me = jnp.arange(n_dp) == device
    own_crop = jnp.sum(jnp.where(is_me, crops, 0))
    own_tile = jnp.sum(jnp.where(is_me, tiles, 0))
    own_row = own_tile // tiles_col
    own_col = own_tile % tiles_col
    tile_row = tiles // tiles_col
    tile_col = tiles % tiles_col

    def beside(drow, dcol):
        hit = (crops == own_crop) & (tile_row == own_row + drow) & (tile_col == own_col + dcol)
        return hit.astype(jnp.float32)

    member = (crops[None, :] == own_crop) & (tiles[None, :] == jnp.arange(per_frame)[:, None])
    crop_devices = jnp.sum(jnp.where(member, jnp.arange(n_dp)[None, :], 0), axis=1)
    whole = lax.all_gather(pixels_in, "mp", axis=1, tiled=True)
    xm = whole.astype(jnp.float32) * maskf
    n1, first_norm_backward = jax.vjp(layer_norm, xm, ln1_gain, ln1_bias)
    n1b = n1.astype(jnp.bfloat16)
    wq = head_columns(w_query, select_where)
    wk = head_columns(w_key, select_where)
    wv = head_columns(w_value, select_where)
    wo = head_rows(w_out, select_where)
    qb = (mat(n1b, wq) + head_vector(b_query, select_where)).astype(jnp.bfloat16)
    patches = (
        n1b.reshape(rows // 2, 2, cols // 2, 2, width)
        .transpose(0, 2, 1, 3, 4)
        .reshape(-1, 4 * width)
    )
    reduced = mat(patches, w_reduce) + b_reduce
    xr, lnr_back = jax.vjp(layer_norm, reduced, lnr_gain, lnr_bias)
    xrb = xr.astype(jnp.bfloat16)
    kb = mat(xrb, wk).astype(jnp.bfloat16)
    vb = (mat(xrb, wv) + head_vector(b_value, select_where)).astype(jnp.bfloat16)
    kmask = (
        pixel_mask.reshape(rows // 2, 2, cols // 2, 2)[:, 0, :, 0].reshape(-1).astype(jnp.bfloat16)
    )
    keys_all, values_all, kmask_all = (
        lax.all_gather(kb, "dp", axis=0, tiled=True),
        lax.all_gather(vb, "dp", axis=0, tiled=True),
        lax.all_gather(kmask, "dp", axis=0, tiled=True),
    )
    per_key = kb.shape[0]
    keys_crop = keys_all.reshape(n_dp, per_key, -1)[crop_devices]
    values_crop = values_all.reshape(n_dp, per_key, -1)[crop_devices]
    usable_crop = kmask_all.reshape(n_dp, per_key)[crop_devices].astype(jnp.float32) > 0.5
    n_blocks = 4
    key_blocks = keys_crop.reshape(n_blocks, -1, slots, HEAD_FEATURES)
    value_blocks = values_crop.reshape(n_blocks, -1, slots, HEAD_FEATURES)
    usable_blocks = usable_crop.reshape(n_blocks, -1)
    queries = qb.reshape(tokens, slots, HEAD_FEATURES)

    def block_scores(key_block, usable_block):
        raw = (
            jnp.einsum("qsd,ksd->sqk", queries, key_block, preferred_element_type=jnp.float32)
            * scale
        )
        return jnp.where(usable_block[None, None, :], raw, NEG)

    def top_step(carry, blocks):
        top, total = carry
        key_block, usable_block = blocks
        scores = block_scores(key_block, usable_block)
        new_top = jnp.maximum(top, jnp.max(scores, axis=-1))
        total = total * jnp.exp(top - new_top) + jnp.sum(
            jnp.exp(scores - new_top[..., None]), axis=-1
        )
        return ((new_top, total), None)

    start = (jnp.full((slots, tokens), NEG, jnp.float32), jnp.zeros((slots, tokens), jnp.float32))
    (top, total), _ = lax.scan(top_step, start, (key_blocks, usable_blocks))
    lse = top + jnp.log(total)

    def out_step(acc, blocks):
        key_block, value_block, usable_block = blocks
        prob = jnp.exp(block_scores(key_block, usable_block) - lse[..., None])
        acc = acc + jnp.einsum(
            "sqk,ksd->qsd",
            prob.astype(jnp.bfloat16),
            value_block,
            preferred_element_type=jnp.float32,
        )
        return (acc, None)

    empty = jnp.zeros((tokens, slots, HEAD_FEATURES), jnp.float32)
    acc, _ = lax.scan(out_step, empty, (key_blocks, value_blocks, usable_blocks))
    ob = acc.reshape(tokens, -1).astype(jnp.bfloat16)
    branch = lax.psum(mat(ob, wo).astype(jnp.bfloat16), "mp").astype(jnp.float32) + b_out
    h1 = xm + branch * maskf
    n2, ln2_back = jax.vjp(layer_norm, h1, ln2_gain, ln2_bias)
    n2b = n2.astype(jnp.bfloat16)
    ub = ((mat(n2b, w_fc1) + b_fc1) * maskf).astype(jnp.bfloat16)
    channels = ub.shape[1]
    tile_u = ub.reshape(rows, cols, channels)
    lines, sides = (
        lax.all_gather(jnp.stack([tile_u[0], tile_u[-1]]), "dp", axis=0, tiled=True),
        lax.all_gather(jnp.stack([tile_u[:, 0], tile_u[:, -1]]), "dp", axis=0, tiled=True),
    )
    lines = lines.reshape(n_dp, 2, cols, channels)
    sides = sides.reshape(n_dp, 2, rows, channels)
    top_lines = lines[:, 0]
    bottom_lines = lines[:, 1]
    left_sides = sides[:, 0]
    right_sides = sides[:, 1]
    upper = jnp.concatenate(
        [
            pick(beside(-1, -1), bottom_lines[:, -1:]),
            pick(beside(-1, 0), bottom_lines),
            pick(beside(-1, 1), bottom_lines[:, :1]),
        ],
        axis=0,
    )
    lower = jnp.concatenate(
        [
            pick(beside(1, -1), top_lines[:, -1:]),
            pick(beside(1, 0), top_lines),
            pick(beside(1, 1), top_lines[:, :1]),
        ],
        axis=0,
    )
    middle = jnp.concatenate(
        [
            pick(beside(0, -1), right_sides)[:, None],
            tile_u.astype(jnp.float32),
            pick(beside(0, 1), left_sides)[:, None],
        ],
        axis=1,
    )
    padded = jnp.concatenate([upper[None], middle, lower[None]], axis=0)
    act, depth_back = jax.vjp(depth_gelu, padded, w_depth, b_depth)
    gb = act.reshape(tokens, channels).astype(jnp.bfloat16)
    ffn_mine = lax.psum_scatter(
        mat(gb, w_fc2).astype(jnp.bfloat16), "mp", scatter_dimension=1, tiled=True
    ).astype(jnp.float32)
    h1_mine = lax.dynamic_slice_in_dim(h1, part * share, share, 1)
    bias_mine = lax.dynamic_slice_in_dim(b_fc2, part * share, share, 0)
    block_result = (h1_mine + (ffn_mine + bias_mine) * maskf).astype(jnp.bfloat16)
    dy = cotangent.astype(jnp.float32)
    dff = dy * maskf
    grad_b_fc2 = jnp.sum(dff, axis=0)
    dfb = dff.astype(jnp.bfloat16)
    grad_w_fc2 = mat(gb.T, dfb)
    dgr = mat(dfb, w_fc2.T).astype(jnp.bfloat16).astype(jnp.float32).reshape(rows, cols, channels)
    dpad, grad_w_depth, grad_b_depth = depth_back(dgr)
    grad_lines, grad_sides = (
        lax.all_gather(
            jnp.stack([dpad[0], dpad[-1]]).astype(jnp.bfloat16), "dp", axis=0, tiled=True
        ).astype(jnp.float32),
        lax.all_gather(
            jnp.stack([dpad[1:-1, 0], dpad[1:-1, -1]]).astype(jnp.bfloat16),
            "dp",
            axis=0,
            tiled=True,
        ).astype(jnp.float32),
    )
    grad_lines = grad_lines.reshape(n_dp, 2, cols + 2, channels)
    grad_sides = grad_sides.reshape(n_dp, 2, rows, channels)
    top_grads = grad_lines[:, 0]
    bottom_grads = grad_lines[:, 1]
    dtile = dpad[1:-1, 1:-1]
    dtile = dtile.at[0].add(pick(beside(-1, 0), bottom_grads[:, 1:-1]))
    dtile = dtile.at[0, 0].add(pick(beside(-1, -1), bottom_grads[:, -1:])[0])
    dtile = dtile.at[0, -1].add(pick(beside(-1, 1), bottom_grads[:, :1])[0])
    dtile = dtile.at[-1].add(pick(beside(1, 0), top_grads[:, 1:-1]))
    dtile = dtile.at[-1, 0].add(pick(beside(1, -1), top_grads[:, -1:])[0])
    dtile = dtile.at[-1, -1].add(pick(beside(1, 1), top_grads[:, :1])[0])
    dtile = dtile.at[:, 0].add(pick(beside(0, -1), grad_sides[:, 1]))
    dtile = dtile.at[:, -1].add(pick(beside(0, 1), grad_sides[:, 0]))
    dub = (dtile.reshape(tokens, channels).astype(jnp.bfloat16).astype(jnp.float32) * maskf).astype(
        jnp.bfloat16
    )
    grad_b_fc1 = jnp.sum(dub.astype(jnp.float32), axis=0)
    grad_w_fc1 = mat(n2b.T, dub)
    dn2_part = mat(dub, w_fc1.T)
    zero_vector = jnp.zeros((width,), jnp.float32)
    dn2 = lax.psum(dn2_part.astype(jnp.bfloat16), "mp").astype(jnp.float32)
    dh1_norm, shared_gain, shared_bias = ln2_back(dn2)
    dh1 = dy + dh1_norm
    split_gain = zero_vector
    split_bias = zero_vector
    dattn = dh1 * maskf
    grad_b_out = jnp.sum(dattn, axis=0)
    dab = dattn.astype(jnp.bfloat16)
    grad_wo = mat(ob.T, dab)
    dob = mat(dab, wo.T).astype(jnp.bfloat16)
    dout = dob.reshape(tokens, slots, HEAD_FEATURES)
    drow = jnp.sum(dout.astype(jnp.float32) * acc, axis=-1).T

    def back_step(dq_acc, blocks):
        key_block, value_block, usable_block = blocks
        prob = jnp.exp(block_scores(key_block, usable_block) - lse[..., None])
        dv_block = jnp.einsum(
            "sqk,qsd->ksd", prob.astype(jnp.bfloat16), dout, preferred_element_type=jnp.float32
        )
        dprob = jnp.einsum("qsd,ksd->sqk", dout, value_block, preferred_element_type=jnp.float32)
        dscore = (prob * (dprob - drow[..., None])).astype(jnp.bfloat16)
        dq_acc = dq_acc + jnp.einsum(
            "sqk,ksd->qsd", dscore, key_block, preferred_element_type=jnp.float32
        )
        dk_block = (
            jnp.einsum("sqk,qsd->ksd", dscore, queries, preferred_element_type=jnp.float32) * scale
        )
        return (dq_acc, (dk_block, dv_block))

    dq_acc, (dk_blocks, dv_blocks) = lax.scan(
        back_step, empty, (key_blocks, value_blocks, usable_blocks)
    )
    zero_keys = jnp.zeros((n_dp, per_key, slots * HEAD_FEATURES), jnp.float32)
    dk_full = (
        zero_keys.at[crop_devices]
        .set(dk_blocks.reshape(per_frame, per_key, -1))
        .reshape(n_dp * per_key, -1)
    )
    dv_full = (
        zero_keys.at[crop_devices]
        .set(dv_blocks.reshape(per_frame, per_key, -1))
        .reshape(n_dp * per_key, -1)
    )
    dk_mine, dv_mine = (
        lax.psum_scatter(dk_full, "dp", scatter_dimension=0, tiled=True),
        lax.psum_scatter(dv_full, "dp", scatter_dimension=0, tiled=True),
    )
    dkb = dk_mine.astype(jnp.bfloat16)
    dvb = dv_mine.astype(jnp.bfloat16)
    dqb = (dq_acc * scale).reshape(tokens, -1).astype(jnp.bfloat16)
    grad_wq = mat(n1b.T, dqb)
    grad_bq = jnp.sum(dqb.astype(jnp.float32), axis=0)
    grad_wk = mat(xrb.T, dkb)
    grad_wv = mat(xrb.T, dvb)
    grad_bv = jnp.sum(dvb.astype(jnp.float32), axis=0)
    dxr, dn1_query = (
        lax.psum((mat(dkb, wk.T) + mat(dvb, wv.T)).astype(jnp.bfloat16), "mp").astype(jnp.float32),
        lax.psum(mat(dqb, wq.T).astype(jnp.bfloat16), "mp").astype(jnp.float32),
    )
    dreduced, grad_lnr_gain, grad_lnr_bias = lnr_back(dxr)
    drb = dreduced.astype(jnp.bfloat16)
    grad_w_reduce = mat(patches.T, drb)
    grad_b_reduce = jnp.sum(drb.astype(jnp.float32), axis=0)
    dpatch = (
        mat(drb, w_reduce.T)
        .reshape(rows // 2, cols // 2, 2, 2, width)
        .transpose(0, 2, 1, 3, 4)
        .reshape(tokens, width)
    )
    dxm, grad_ln1_gain, grad_ln1_bias = first_norm_backward(dn1_query + dpatch)
    grad_whole = (dxm + dh1) * maskf
    grad_input = lax.dynamic_slice_in_dim(grad_whole, part * share, share, 1)
    (
        grad_w_reduce,
        grad_b_reduce,
        grad_lnr_gain,
        grad_lnr_bias,
        grad_ln1_gain,
        grad_ln1_bias,
        shared_gain,
        shared_bias,
        grad_b_out,
        grad_b_fc2,
        grad_w_fc1,
        grad_b_fc1,
        grad_w_depth,
        grad_b_depth,
        grad_w_fc2,
    ) = lax.psum(
        (
            grad_w_reduce,
            grad_b_reduce,
            grad_lnr_gain,
            grad_lnr_bias,
            grad_ln1_gain,
            grad_ln1_bias,
            shared_gain,
            shared_bias,
            grad_b_out,
            grad_b_fc2,
            grad_w_fc1,
            grad_b_fc1,
            grad_w_depth,
            grad_b_depth,
            grad_w_fc2,
        ),
        "dp",
    )
    (
        grad_w_query,
        grad_b_query,
        grad_w_key,
        grad_w_value,
        grad_b_value,
        output_weight_gradient,
        split_gain,
        split_bias,
    ) = lax.psum(
        (
            spread_columns(grad_wq, select_where),
            spread_vector(grad_bq, select_where),
            spread_columns(grad_wk, select_where),
            spread_columns(grad_wv, select_where),
            spread_vector(grad_bv, select_where),
            spread_rows(grad_wo, select_where),
            split_gain,
            split_bias,
        ),
        ("dp", "mp"),
    )
    grad_ln2_gain = shared_gain + split_gain
    grad_ln2_bias = shared_bias + split_bias
    return (
        block_result,
        grad_input,
        grad_ln1_gain,
        grad_ln1_bias,
        grad_w_query,
        grad_b_query,
        grad_w_key,
        grad_w_value,
        grad_b_value,
        grad_w_reduce,
        grad_b_reduce,
        grad_lnr_gain,
        grad_lnr_bias,
        output_weight_gradient,
        grad_b_out,
        grad_ln2_gain,
        grad_ln2_bias,
        grad_w_fc1,
        grad_b_fc1,
        grad_w_depth,
        grad_b_depth,
        grad_w_fc2,
        grad_b_fc2,
    )


def solution(mesh):
    return jax.shard_map(
        on_device,
        mesh=mesh,
        in_specs=(
            P("dp", "mp"),
            P("dp", None),
            P("dp"),
            P(),
            P(),
            P(),
            P(),
            P(),
            P(),
            P(),
            P(),
            P(),
            P(),
            P(),
            P(),
            P(),
            P(),
            P(),
            P(),
            P(None, "mp"),
            P("mp"),
            P(None, "mp"),
            P("mp"),
            P("mp", None),
            P(),
        ),
        out_specs=(
            P("dp", "mp"),
            P("dp", "mp"),
            P(),
            P(),
            P(),
            P(),
            P(),
            P(),
            P(),
            P(),
            P(),
            P(),
            P(),
            P(),
            P(),
            P(),
            P(),
            P(None, "mp"),
            P("mp"),
            P(None, "mp"),
            P("mp"),
            P("mp", None),
            P(),
        ),
        check_vma=False,
    )
```

profile of v0, /device:TPU:0, one launch (start us, length us, event | category | flops | bytes accessed | tf_op | source)
XLA Modules:
  0.0 915.0 jit_solution(16229897107296276338)
XLA Ops:
  8.1 9.1 all_gather.24
  25.3 31.5 %all_gather.27 = bf16[1600,128]{1,0:T(8,128)(2,1)S(1)} all-gather(bf16[200,128]{1,0:T(8,128)(2,1)S(1)} %convolution_convert_fusion.8), channel_id=1, replica_groups=mesh['dp'=8,'mp'=4] {'dp'}, dimensions={0}, use_global_device_ids=true | all-gather | bytes 460800 | tf_op jit(solution)/shard_map/all_gather | solution.py:179
  66.9 21.2 %all-reduce.18 = bf16[1600]{0:T(1024)(128)(2,1)S(1)} all-reduce(bf16[1600]{0:T(1024)(128)(2,1)S(1)} %dynamic-update-slice.24), channel_id=1, replica_groups=mesh['dp'=8,'mp'=4] {'dp'}, use_global_device_ids=true, to_apply=%add.18 | all-reduce | flops 1600 | bytes 6400
  88.8 19.0 %while.47 = (s32[]{:T(128)}, f32[2,800]{1,0:T(2,128)S(1)}, f32[2,800]{1,0:T(2,128)S(1)}, pred[4,400]{1,0:T(4,128)(4,1)S(1)}, bf16[4,400,2,64]{1,3,2,0:T(8,128)(2...) while((s32[]{:T(128)}, f32[2,800]{1,0:T(2,128)S(1)}, ...), condition=%wide.region_9.10_spmd.clone, body=%wide.region_6.9_spmd.clone.sunk | while | flops 86408000 | bytes 5565464 | solution.py:211
  109.3 31.2 %all_gather.25 = bf16[1600,128]{1,0:T(8,128)(2,1)S(1)} all-gather(bf16[200,128]{1,0:T(8,128)(2,1)S(1)} %fusion.71), channel_id=1, replica_groups=mesh['dp'=8,'mp'=4] {'dp'}, dimensions={0}, use_global_device_ids=true | all-gather | bytes 460800 | tf_op jit(solution)/shard_map/all_gather | solution.py:180
  141.8 2.9 reshape.859
  144.7 3.5 copy.293
  148.8 8.4 while.48
  164.2 2.7 copy.303
  168.3 22.1 %all-reduce.32.cloned.1.call-done = bf16[800,320]{0,1:T(8,128)(2,1)} async-done(((bf16[800,320]{0,1:T(8,128)(2,1)}), bf16[800,320]{0,1:T(8,128)(2,1)}) %all-reduce.32.cloned.1.call-update) | async-done | bytes 512016 | tf_op jit(solution)/shard_map/psum | solution.py:228
  199.9 32.8 %all_gather.28 = bf16[16,80,320]{2,1,0:T(8,128)(2,1)S(1)} all-gather(bf16[2,80,320]{2,1,0:T(8,128)(2,1)S(1)} %copy.297), channel_id=1, replica_groups=mesh['dp'=8,'mp'=4] {'dp'}, dimensions={0}, use_global_device_ids=true | all-gather | bytes 921600 | tf_op jit(solution)/shard_map/all_gather | solution.py:236
  236.0 30.6 %all_gather.29 = bf16[16,10,320]{2,1,0:T(8,128)(2,1)S(1)} all-gather(bf16[2,10,320]{2,1,0:T(8,128)(2,1)S(1)} %pad_maximum_fusion.5), channel_id=1, replica_groups=mesh['dp'=8,'mp'=4] {'dp'}, dimensions={0}, use_global_device_ids=true | all-gather | bytes 115200 | tf_op jit(solution)/shard_map/all_gather | solution.py:237
  268.6 7.5 multiply_reduce_fusion.8
  278.2 30.8 %all_gather.31 = bf16[16,10,320]{2,1,0:T(8,128)(2,1)S(1)} all-gather(bf16[2,10,320]{2,1,0:T(8,128)(2,1)S(1)} %pad_maximum_fusion.6), channel_id=1, replica_groups=mesh['dp'=8,'mp'=4] {'dp'}, dimensions={0}, use_global_device_ids=true | all-gather | bytes 115200 | tf_op jit(solution)/shard_map/all_gather | solution.py:289
  309.2 32.5 %all_gather.30 = bf16[16,82,320]{2,1,0:T(8,128)(2,1)S(1)} all-gather(bf16[2,82,320]{2,1,0:T(8,128)(2,1)S(1)} %pad_maximum_fusion.4), channel_id=1, replica_groups=mesh['dp'=8,'mp'=4] {'dp'}, dimensions={0}, use_global_device_ids=true | all-gather | bytes 944640 | tf_op jit(solution)/shard_map/all_gather | solution.py:286
  346.2 2.8 fusion.74
  349.0 2.6 scatter-add.30
  363.4 3.0 convert_reduce_fusion.1
  366.4 2.8 copy.307
  369.2 2.6 convolution_convert_fusion
  371.9 33.9 %all-reduce.34.cloned.1.call-done = bf16[800,320]{0,1:T(8,128)(2,1)} async-done(((bf16[800,320]{0,1:T(8,128)(2,1)}), bf16[800,320]{0,1:T(8,128)(2,1)}) %all-reduce.34.cloned.1.call-update) | async-done | bytes 512016 | tf_op jit(solution)/shard_map/psum | solution.py:316
  411.2 40.5 %while.49 = (s32[]{:T(128)}, f32[800,2,64]{0,2,1:T(8,128)S(1)}, f32[4,400,2,64]{1,3,2,0:T(8,128)}, f32[4,400,2,64]{1,3,2,0:T(8,128)}, bf16[4,400,2,64]{1,3,2,0:T...) while((s32[]{:T(128)}, f32[800,2,64]{0,2,1:T(8,128)S(1)}, ...), condition=%wide.region_23.24_spmd.clone, body=%wide.region_22.23_spmd.clone.sunk | while | flops 416256000 | bytes 26335776 | solution.py:345
  412.8 2.5 multiply_convert_fusion.13
  417.9 3.4 fusion.313
  422.9 2.5 multiply_convert_fusion.13
  428.1 3.4 fusion.313
  433.1 2.5 multiply_convert_fusion.13
  438.2 3.4 fusion.313
  443.2 2.5 multiply_convert_fusion.13
  448.3 3.4 fusion.313
  451.7 3.8 copy.349
  455.5 3.1 reshape.855
  461.7 3.8 copy.350
  465.5 3.0 reshape.856
  475.9 43.3 %reduce-scatter.10.cloned.1.call-done = f32[200,128]{1,0:T(8,128)} async-done(((f32[1600,128]{1,0:T(8,128)}), f32[200,128]{1,0:T(8,128)}) %reduce-scatter.10.cloned.1.call-update) | async-done | bytes 102416
  520.2 59.4 %reduce-scatter.12.cloned.1.call-done = f32[200,128]{1,0:T(8,128)} async-done(((f32[1600,128]{1,0:T(8,128)}), f32[200,128]{1,0:T(8,128)}) %reduce-scatter.12.cloned.1.call-update) | async-done | bytes 102416
  583.1 2.9 fusion.103
  593.4 22.2 %all-reduce.40.cloned.1.call-done = (bf16[200,320]{1,0:T(8,128)(2,1)}, bf16[800,320]{0,1:T(8,128)(2,1)}) async-done(((bf16[200,320]{1,0:T(8,128)(2,1)}, bf16[800,320]{0,1:T(8,128)(2,1)}), (bf16[200,320]{1,0:T(8,128)(2,1)}, bf16[800,320]{0,1:T(8,128)(2,1)})) %all-reduce.40.cloned.1.call-update) | async-done | bytes 640016 | tf_op jit(solution)/shard_map/psum | solution.py:372
  622.4 39.7 %all-reduce.21 = (f32[320]{0:T(512)}, f32[320]{0:T(512)}) all-reduce(f32[320]{0:T(512)S(1)} %reshape.754, f32[320]{0:T(512)S(1)} %reshape.760), channel_id=1, replica_groups=mesh['dp'=8,'mp'=4] {'dp','mp'}, use_global_device_ids=true, to_apply=%region_40.41 | all-reduce | flops 640 | bytes 5120 | tf_op jit(solution)/shard_map/psum | solution.py:433
  663.6 3.2 reshape.751
  666.8 2.7 copy.440
  669.5 3.0 reshape.752
  672.5 2.8 copy.318
  677.7 38.1 %all-reduce.23 = (f32[320]{0:T(512)}, f32[320]{0:T(512)}, f32[320]{0:T(512)}, f32[320]{0:T(512)}, f32[320]{0:T(512)}, /*index=5*/f32[320]{0:T(512)}, f32[320]{0:...) all-reduce(f32[320]{0:T(512)S(1)} %get-tuple-element.602, ...), channel_id=1, replica_groups=mesh['dp'=8,'mp'=4] {'dp'}, use_global_device_ids=true, to_apply=%region_35.36 | all-reduce | flops 6400 | bytes 51200 | tf_op jit(solution)/shard_map/psum | solution.py:404
  715.8 2.8 fusion.218
  720.5 61.5 %all-reduce.36.cloned.1.call-done = (f32[320,320]{0,1:T(8,128)}, f32[320,320]{0,1:T(8,128)}, f32[320,320]{0,1:T(8,128)}, f32[320,320]{1,0:T(8,128)}) async-done(((f32[320,320]{0,1:T(8,128)}, f32[320,320]{0,1:T(8,128)}, f32[320,320]{0,1:T(8,128)}, f32[320,320]{1,0:T(8,128)}), (f32[320,320]{0,1:T(8,128)}, f32[320,320]{0,1:T(8,128)}, f32[320,320]{0,1:T(8,128)}, ...) | async-done | bytes 1638416 | tf_op jit(solution)/shard_map/psum | solution.py:433
  786.1 116.1 %all-reduce.38.cloned.1.call-done = (f32[1280,320]{0,1:T(8,128)}, f32[320,320]{1,0:T(8,128)}, f32[320,320]{1,0:T(8,128)}) async-done(((f32[1280,320]{0,1:T(8,128)}, f32[320,320]{1,0:T(8,128)}, f32[320,320]{1,0:T(8,128)}), (f32[1280,320]{0,1:T(8,128)}, f32[320,320]{1,0:T(8,128)}, f32[320,320]{1,0:T(8,128)})) %all-reduce.38.cloned.1.call-update) | async-done | bytes 2457616 | tf_op jit(solution)/shard_map/psum | solution.py:404
  902.2 2.8 copy.502
  (500 shorter events, 152.4 us)
Async XLA Ops:
  7.2 14.7 %copy-start = (bf16[1280,320]{0,1:T(8,128)(2,1)S(1)}, bf16[1280,320]{0,1:T(8,128)(2,1)}, u32[]{:S(2)}) copy-start(bf16[1280,320]{0,1:T(8,128)(2,1)} %param.58) | copy-start | bytes 2457604
  7.2 10.4 %copy-start.61 = (f32[320]{0:T(512)S(1)}, f32[320]{0:T(512)}, u32[]{:S(2)}) copy-start(f32[320]{0:T(512)} %param.51) | copy-start | bytes 3844
  7.2 10.4 %copy-start.95 = (f32[320]{0:T(512)S(1)}, f32[320]{0:T(512)}, u32[]{:S(2)}) copy-start(f32[320]{0:T(512)} %param.52) | copy-start | bytes 3844
  7.2 183.1 %all-reduce.32.cloned.1.call-start = ((), (), s32[]{:S(2)}) async-start(), calls=%async_computation.3 | async-start | bytes 1146880 | tf_op jit(solution)/shard_map/psum | solution.py:228
  17.9 46.5 %copy-start.11 = (bf16[800,320]{0,1:T(8,128)(2,1)}, bf16[800,320]{0,1:T(8,128)(2,1)S(1)}, u32[]{:S(2)}) copy-start(bf16[800,320]{0,1:T(8,128)(2,1)S(1)} %add_convert_fusion.1) | copy-start | bytes 1536004
  18.5 3.5 copy-start.96
  22.6 34.2 %copy-start.13 = (f32[200,320]{1,0:T(8,128)}, f32[200,320]{1,0:T(8,128)S(1)}, u32[]{:S(2)}) copy-start(f32[200,320]{1,0:T(8,128)S(1)} %get-tuple-element.763) | copy-start | bytes 768004
  22.8 34.0 %copy-start.57 = (s32[8,2]{0,1:T(2,128)S(1)}, s32[8,2]{0,1:T(2,128)}, u32[]{:S(2)}) copy-start(s32[8,2]{0,1:T(2,128)} %param.50) | copy-start | bytes 196
  22.9 134.3 %copy-start.54 = (s32[2]{0:T(128)}, s32[2]{0:T(128)S(1)}, u32[]{:S(2)}) copy-start(s32[2]{0:T(128)S(1)} %multiply_add_fusion.6) | copy-start | bytes 28
  24.6 84.2 %copy-start.25 = (bf16[200,320]{1,0:T(8,128)(2,1)}, bf16[200,320]{1,0:T(8,128)(2,1)S(1)}, u32[]{:S(2)}) copy-start(bf16[200,320]{1,0:T(8,128)(2,1)S(1)} %add_convert_fusion.3) | copy-start | bytes 384004
  58.3 4.3 copy-start.93
  60.2 3.9 copy-start.101
  64.0 24.8 %copy-start.37 = (bf16[320,2,64]{0,1,2:T(2,128)(2,1)}, bf16[320,2,64]{0,1,2:T(2,128)(2,1)S(1)}, u32[]{:S(2)}) copy-start(bf16[320,2,64]{0,1,2:T(2,128)(2,1)S(1)} %fusion.70) | copy-start | bytes 245764
  88.8 19.0 %copy-start.49 = (bf16[320,320]{1,0:T(8,128)(2,1)S(1)}, bf16[320,320]{1,0:T(8,128)(2,1)}, u32[]{:S(2)}) copy-start(bf16[320,320]{1,0:T(8,128)(2,1)} %param.56) | copy-start | bytes 614404
  88.8 19.6 %copy-start.102 = (f32[320]{0:T(512)S(1)}, f32[320]{0:T(512)}, u32[]{:S(2)}) copy-start(f32[320]{0:T(512)} %param.57) | copy-start | bytes 3844
  141.8 7.0 copy-start.22
  157.2 4.5 copy-start.5
  157.2 4.5 copy-start.23
  160.1 245.7 %all-reduce.34.cloned.1.call-start = ((), (), s32[]{:S(2)}) async-start(), calls=%async_computation.5 | async-start | bytes 1146880 | tf_op jit(solution)/shard_map/psum | solution.py:316
  161.6 5.3 copy-start.105
  161.6 6.0 copy-start.92
  161.7 28.7 %copy-start.103 = (f32[320]{0:T(512)S(1)}, f32[320]{0:T(512)}, u32[]{:S(2)}) copy-start(f32[320]{0:T(512)} %param.63) | copy-start | bytes 3844
  168.3 23.7 %copy-start.52 = (f32[320]{0:T(512)S(1)}, f32[320]{0:T(512)}, u32[]{:S(2)}) copy-start(f32[320]{0:T(512)} %param.64) | copy-start | bytes 3844
  168.3 23.7 %copy-start.98 = (f32[320]{0:T(512)S(1)}, f32[320]{0:T(512)}, u32[]{:S(2)}) copy-start(f32[320]{0:T(512)} %param.65) | copy-start | bytes 3844
  191.7 216.8 %copy-start.2 = (f32[800,320]{0,1:T(8,128)}, f32[800,320]{0,1:T(8,128)S(1)}, u32[]{:S(2)}) copy-start(f32[800,320]{0,1:T(8,128)S(1)} %get-tuple-element.720) | copy-start | bytes 3072004
  234.7 32.4 %copy-start.6 = (f32[10,80,320]{2,1,0:T(8,128)S(1)}, f32[10,80,320]{2,1,0:T(8,128)}, u32[]{:S(2)}) copy-start(f32[10,80,320]{2,1,0:T(8,128)} %convert_element_type.310) | copy-start | bytes 3072004
  351.6 11.8 %copy-start.56 = (f32[10,80]{1,0:T(8,128)S(1)}, f32[10,80]{1,0:T(8,128)}, u32[]{:S(2)}) copy-start(f32[10,80]{1,0:T(8,128)} %mul.565) | copy-start | bytes 9604
  369.2 36.6 %copy-start.53 = (f32[320]{0:T(512)S(1)}, f32[320]{0:T(512)}, u32[]{:S(2)}) copy-start(f32[320]{0:T(512)} %param.64) | copy-start | bytes 3844
  371.8 147.4 %reduce-scatter.10.cloned.1.call-start = ((), (), s32[]{:S(2)}) async-start(), calls=%async_computation.6 | async-start | bytes 921600
  417.9 3.4 copy-start.36
  428.1 3.4 copy-start.36
  438.2 3.4 copy-start.36
  448.3 3.4 copy-start.36
  455.5 3.2 copy-start.94
  461.6 118.0 %reduce-scatter.12.cloned.1.call-start = ((), (), s32[]{:S(2)}) async-start(), calls=%async_computation.7 | async-start | bytes 921600
  471.4 144.3 %all-reduce.40.cloned.1.call-start = ((), (), s32[]{:S(2)}) async-start(), calls=%async_computation.10 | async-start | bytes 1454080 | tf_op jit(solution)/shard_map/psum | solution.py:372
  473.3 45.8 %copy-start.42 = (bf16[320,2,64]{0,2,1:T(8,128)(2,1)S(1)}, bf16[320,2,64]{0,2,1:T(8,128)(2,1)}, u32[]{:S(2)}) copy-start(bf16[320,2,64]{0,2,1:T(8,128)(2,1)} %copy-done.41) | copy-start | bytes 245764
  474.7 104.9 %copy-start.40 = (bf16[320,2,64]{0,2,1:T(8,128)(2,1)S(1)}, bf16[320,2,64]{0,2,1:T(8,128)(2,1)}, u32[]{:S(2)}) copy-start(bf16[320,2,64]{0,2,1:T(8,128)(2,1)} %copy-done.39) | copy-start | bytes 245764
  475.9 105.8 %copy-start.31 = (bf16[320,320]{1,0:T(8,128)(2,1)S(1)}, bf16[320,320]{1,0:T(8,128)(2,1)}, u32[]{:S(2)}) copy-start(bf16[320,320]{1,0:T(8,128)(2,1)} %param.70) | copy-start | bytes 614404
  581.4 137.3 %reduce-scatter.8.cloned.1.call-start = ((), (), s32[]{:S(2)}) async-start(), calls=%async_computation.4 | async-start | bytes 716800 | tf_op jit(solution)/shard_map/reduce_scatter | solution.py:272
  586.0 196.1 %all-reduce.36.cloned.1.call-start = ((), (), s32[]{:S(2)}) async-start(), calls=%async_computation.8 | async-start | bytes 3932160 | tf_op jit(solution)/shard_map/psum | solution.py:433
  593.4 22.3 %copy-start.14 = (f32[200,320]{1,0:T(8,128)S(1)}, f32[200,320]{1,0:T(8,128)}, u32[]{:S(2)}) copy-start(f32[200,320]{1,0:T(8,128)} %copy-done.13) | copy-start | bytes 768004
  593.4 22.3 %copy-start.60 = (f32[200]{0:T(256)S(1)}, f32[200]{0:T(256)}, u32[]{:S(2)}) copy-start(f32[200]{0:T(256)} %copy-done.59) | copy-start | bytes 2404
  593.4 22.3 %copy-start.64 = (f32[320]{0:T(512)S(1)}, f32[320]{0:T(512)}, u32[]{:S(2)}) copy-start(f32[320]{0:T(512)} %param.60) | copy-start | bytes 3844
  593.4 22.4 %copy-start.75 = (f32[200]{0:T(256)S(1)}, f32[200]{0:T(256)}, u32[]{:S(2)}) copy-start(f32[200]{0:T(256)} %copy-done.74) | copy-start | bytes 2404
  593.4 24.1 %copy-start.77 = (f32[200]{0:T(256)S(1)}, f32[200]{0:T(256)}, u32[]{:S(2)}) copy-start(f32[200]{0:T(256)} %copy-done.76) | copy-start | bytes 2404
  593.4 308.8 %all-reduce.38.cloned.1.call-start = ((), (), s32[]{:S(2)}) async-start(), calls=%async_computation.9 | async-start | bytes 5242880 | tf_op jit(solution)/shard_map/psum | solution.py:404
  782.0 3.1 copy-start.44
  (77 other events, 128.8 us)
Sparse Core Ops, SparseCore 0:
  160.2 30.1 all-reduce.31
  371.9 33.8 all-reduce.33
  461.7 57.3 reduce-scatter.9
  523.3 56.2 reduce-scatter.11
  582.5 33.1 all-reduce.39
  618.0 22.3 reduce-scatter.7
  648.0 133.9 all-reduce.35
  786.5 115.6 all-reduce.37
where the time goes:
time: 924 us; the launch traced here: 915 us
  waiting for transfers between devices  359 us (39%)
  blocking collectives  298 us (32%)
  local copies, waits for them, and re-layouts  97 us (10%)
  matrix products  91.7 us (10%)
  other arithmetic  50.8 us (5%)
  between operations  18.3 us (2%)
    psum x1, waiting for transfers between devices, on_device(): lax.psum((grad_w_reduce, grad_b_reduce, grad_lnr_gain, grad_lnr_bias, gra...  116 us
    unnamed x10, waiting for transfers between devices  103 us
    psum x1, waiting for transfers between devices, on_device(): lax.psum((spread_columns(grad_wq, select_where), spread_vector(grad_bq, s...  61.5 us
    psum x1, blocking collectives, on_device(): lax.psum((spread_columns(grad_wq, select_where), spread_vector(grad_bq, s...  39.7 us
    psum x1, blocking collectives, on_device(): lax.psum((grad_w_reduce, grad_b_reduce, grad_lnr_gain, grad_lnr_bias, gra...  38.1 us
    psum x1, waiting for transfers between devices, on_device(): dn2 = lax.psum(dn2_part.astype(jnp.bfloat16), 'mp').astype(jnp.float32)  33.9 us
    all_gather x1, blocking collectives, on_device(): lax.all_gather(jnp.stack([tile_u[0], tile_u[-1]]), 'dp', axis=0, tiled=True)  32.8 us
    all_gather x1, blocking collectives, on_device(): lax.all_gather(jnp.stack([dpad[0], dpad[-1]]).astype(jnp.bfloat16), 'dp',...  32.5 us
  transfers between devices with their start and end apart: 8, of which 7 were waited for; matrix products, arithmetic and copies ran while one was open for 7% of the time, Pallas kernels for 0%

commit v1 on v0

--- a/solution.py
+++ b/solution.py
@@ -1,6 +1,10 @@
+import functools
+
 import jax
 import jax.numpy as jnp
 from jax import lax
+from jax.experimental import pallas as pl
+from jax.experimental.pallas import tpu as pltpu
 from jax.sharding import PartitionSpec as P
 
 HEADS = 5
@@ -472,9 +476,853 @@
     )
 
 
+BF = jnp.bfloat16
+F32 = jnp.float32
+LANES = 128
+SIDE_SMALL = 64
+
+
+def nn(a, b):
+    return lax.dot_general(a, b, (((1,), (0,)), ((), ())), preferred_element_type=F32)
+
+
+def nt(a, b):
+    return lax.dot_general(a, b, (((1,), (1,)), ((), ())), preferred_element_type=F32)
+
+
+def tn(a, b):
+    return lax.dot_general(a, b, (((0,), (0,)), ((), ())), preferred_element_type=F32)
+
+
+def iota(shape, axis):
+    return lax.broadcasted_iota(jnp.int32, shape, axis)
+
+
+def hot(cond):
+    return jnp.where(cond, 1.0, 0.0).astype(BF)
+
+
+def spread(value):
+    mean = jnp.sum(value, axis=-1, keepdims=True) * (1.0 / value.shape[-1])
+    centred = value - mean
+    var = jnp.sum(centred * centred, axis=-1, keepdims=True) * (1.0 / value.shape[-1])
+    rstd = lax.rsqrt(var + EPS)
+    return centred * rstd, rstd
+
+
+def norm_back(dn, gain, xhat, rstd):
+    e = dn * gain
+    scale = 1.0 / dn.shape[-1]
+    mean_e = jnp.sum(e, axis=-1, keepdims=True) * scale
+    mean_ex = jnp.sum(e * xhat, axis=-1, keepdims=True) * scale
+    return rstd * (e - mean_e - xhat * mean_ex)
+
+
+def rowsum(value):
+    return jnp.sum(value, axis=0, keepdims=True)
+
+
+class Sizes:
+    def __init__(self, n_dp, n_mp, tokens, width, hidden):
+        self.n_dp, self.n_mp = n_dp, n_mp
+        self.tokens, self.width, self.hidden = tokens, width, hidden
+        self.share = width // n_mp
+        self.rows = FRAME // TILE_ROWS
+        self.cols = tokens // self.rows
+        self.pa, self.pb = self.rows // 2, self.cols // 2
+        self.keys = self.pa * self.pb
+        self.plane = -(-self.keys // 16) * 16
+        self.all = 4 * self.plane
+        self.step = self.plane // 16 // n_mp * 16
+        self.quarter = self.plane - (n_mp - 1) * self.step
+        self.wide = -(-width // LANES) * LANES
+        self.kvrows = self.plane + self.quarter
+        self.top = 8 + self.pb
+        self.ext = self.top + self.keys + self.pb
+        self.erows = 2 * hidden + 2 * HEAD_FEATURES
+        self.echunk = self.erows // n_dp
+        self.lrows = 2 * width
+        self.lchunk = self.lrows // n_dp
+
+
+def fused_body(
+    sz,
+    mask_ref, slot_ref, pix_ref, cot_ref, ln1g_ref, ln1b_ref, wq_ref, bq_ref, wk_ref, wv_ref,
+    bv_ref, wr_ref, br_ref, lnrg_ref, lnrb_ref, wo_ref, bo_ref, ln2g_ref, ln2b_ref, w1_ref, b1_ref,
+    wd_ref, bd_ref, w2_ref, b2_ref,
+    blk_ref, gp_ref, eg_ref, wog_ref, lg_ref, veg_ref, vlg_ref,
+    x32, c32a, c32b, c32c, xg, dfm, dyh_s, dyh, dyh_g, xm_r, n1_r, xhr_r, rsr_r, xr_r, kva, qa_r, qb_r,
+    sbuf, ebuf, e5buf, lse_r, og, row_r, h1_r, n2_r, hal_s, hal, hal_g, ux, ul, ur, dgx, dzx, dzl, dzr,
+    g_r, du_r, dn2_s, dn2_r, dh1_r, dos, do_all, dabg, ff_s, ff_r, dks, dkr, dkvg, dqs, dq_all, dqt, dqt5,
+    e_s, e_r, l_s, l_r, ve_s, ve_r, vl_s, vl_r, gps,
+    ssem, rsem,
+):
+    D, HF, PB, PA, KEYS, PL, T = sz.width, HEAD_FEATURES, sz.pb, sz.pa, sz.keys, sz.plane, sz.all
+    C, FS = sz.hidden, sz.share
+    d = lax.axis_index("dp")
+    m = lax.axis_index("mp")
+    last = sz.n_mp * HF
+
+    def mpx(k):
+        if k == 1:
+            return m + 1 - 2 * lax.rem(m, 2)
+        if k == 2:
+            return lax.rem(m + 2, 4)
+        return 3 - m
+
+    def dpx(k):
+        z, x = d // 2, lax.rem(d, 2)
+        if k & 1:
+            x = 1 - x
+        kz = k >> 1
+        if kz == 1:
+            z = z + 1 - 2 * lax.rem(z, 2)
+        elif kz == 2:
+            z = lax.rem(z + 2, 4)
+        elif kz == 3:
+            z = 3 - z
+        return 2 * z + x
+
+    counter = [0]
+    pending = []
+
+    def take(n):
+        first = counter[0]
+        counter[0] += n
+        return first
+
+    def copy(src, dst, sem, dev):
+        return pltpu.make_async_remote_copy(
+            src_ref=src, dst_ref=dst, send_sem=ssem.at[sem], recv_sem=rsem.at[sem],
+            device_id=dev, device_id_type=pl.DeviceIdType.MESH,
+        )
+
+    def send(src, dst, sem, dev):
+        c = copy(src, dst, sem, dev)
+        c.start()
+        pending.append(c)
+
+    def arrived(ref, sem):
+        copy(ref, ref, sem, (d, m)).wait_recv()
+
+    def mp_start(buf):
+        base = take(3)
+        send(buf.at[m], buf.at[m], base, (d, mpx(1)))
+        send(buf.at[m], buf.at[m], base + 1, (d, mpx(2)))
+        return base
+
+    def mp_finish(buf, base):
+        arrived(buf.at[mpx(2)], base + 1)
+        send(buf.at[mpx(2)], buf.at[mpx(2)], base + 2, (d, mpx(1)))
+        arrived(buf.at[mpx(1)], base)
+        arrived(buf.at[mpx(3)], base + 2)
+
+    def dp_start(buf):
+        base = take(7)
+        for kz in (3, 2, 1):
+            send(buf.at[d], buf.at[d], base + kz, (dpx(2 * kz), m))
+        send(buf.at[d], buf.at[d], base, (dpx(1), m))
+        return base
+
+    def dp_finish(buf, base, each=None):
+        def got(k, sem):
+            arrived(buf.at[dpx(k)], sem)
+            if each is not None:
+                each(k)
+        for kz in (1, 2, 3):
+            arrived(buf.at[dpx(2 * kz)], base + kz)
+            send(buf.at[dpx(2 * kz)], buf.at[dpx(2 * kz)], base + 3 + kz, (dpx(1), m))
+            if each is not None:
+                each(2 * kz)
+        got(1, base)
+        for kz in (1, 2, 3):
+            got(2 * kz + 1, base + 3 + kz)
+
+    def mp_scatter(block, dst):
+        base = take(4)
+        for k in (2, 3, 1):
+            send(block(mpx(k)), dst(k), base + k, (d, mpx(k)))
+        return base
+
+    def dp_scatter(block, dst):
+        base = take(8)
+        for k in (6, 7, 4, 5, 2, 3, 1):
+            send(block(dpx(k)), dst(k), base + k, (dpx(k), m))
+        return base
+
+    side = jnp.where(mask_ref[sz.cols - 1] > 0, FRAME, SIDE_SMALL)
+    tile = slot_ref[d, 1]
+    tiles = [slot_ref[k, 1] for k in range(sz.n_dp)]
+    above = sum(jnp.where(tiles[k] == tile - 1, k, 0) for k in range(sz.n_dp))
+    below = sum(jnp.where(tiles[k] == tile + 1, k, 0) for k in range(sz.n_dp))
+
+    def place(p, count):
+        a = sum(jnp.where(p >= PB * k, 1, 0) for k in range(1, count))
+        return a, p - PB * a
+
+    def token_mask(i, j):
+        p = iota((PL, 1), 0)
+        a, b = place(p, PA)
+        inside = (p < KEYS) & (sz.rows * tile + 2 * a + i < side) & (2 * b + j < side)
+        return jnp.where(inside, 1.0, 0.0)
+
+    def halo_mask(i, j, a):
+        b = iota((PB, 1), 0)
+        row = sz.rows * tile + 2 * a + i
+        inside = (row >= 0) & (row < side) & (2 * b + j < side)
+        return jnp.where(inside, 1.0, 0.0)
+
+    def key_bias(p, tile_at, limit):
+        a, b = place(p, PA)
+        usable = (p < limit) & (sz.rows * tile_at + 2 * a < side) & (2 * b < side)
+        return jnp.where(usable, 0.0, NEG)
+
+    def vec(ref):
+        return ref[...].reshape(1, ref.shape[0])
+
+    def own_head(row):
+        return sum(
+            jnp.where(m == h, 1.0, 0.0) * row[:, HF * h : HF * (h + 1)] for h in range(sz.n_mp)
+        )
+
+    def plane_rows(ref, start):
+        return ref[pl.ds(pl.multiple_of(start, 16), PL), :]
+
+    peers = [(d, mpx(k)) for k in (1, 2, 3)] + [(dpx(k), m) for k in range(1, 8)]
+    bar = pltpu.get_barrier_semaphore()
+    for dev in peers:
+        pl.semaphore_signal(bar, inc=1, device_id=dev, device_id_type=pl.DeviceIdType.MESH)
+
+    x32[...] = pix_ref[...].astype(F32)
+    for i in range(2):
+        for j in range(2):
+            p = 2 * i + j
+            parts = [
+                x32[pl.ds((2 * a + i) * sz.cols + j, PB, stride=2), :] for a in range(PA)
+            ] + [jnp.zeros((PL - KEYS, FS), F32)]
+            block = jnp.concatenate(parts, axis=0)
+            block = jnp.concatenate([block, jnp.zeros((PL, LANES - FS), F32)], axis=1)
+            xg[m, PL * p : PL * (p + 1), :] = block.astype(BF)
+    pl.semaphore_wait(bar, len(peers))
+    x_at = mp_start(xg)
+
+    c32a[...] = cot_ref[:, 0:128].astype(F32)
+    c32b[...] = cot_ref[:, 128:256].astype(F32)
+    c32c[...] = cot_ref[:, 256:D].astype(F32)
+    for i in range(2):
+        for j in range(2):
+            p = 2 * i + j
+            lanes = []
+            for ref in (c32a, c32b, c32c):
+                parts = [
+                    ref[pl.ds((2 * a + i) * sz.cols + j, PB, stride=2), :] for a in range(PA)
+                ] + [jnp.zeros((PL - KEYS, ref.shape[1]), F32)]
+                lanes.append(jnp.concatenate(parts, axis=0))
+            dfm[PL * p : PL * (p + 1), :] = (
+                jnp.concatenate(lanes, axis=1) * token_mask(i, j)
+            ).astype(BF)
+    dyh_s[:, :D] = dfm[pl.ds(pl.multiple_of(PL * m + (KEYS - PB) * (m // 2), 16), 48), :]
+    dyh_s[:, D:] = jnp.zeros((48, sz.wide - D), BF)
+    dyh[d] = dyh_s[...]
+    dy_at = dp_start(dyh)
+
+    r2, c2 = iota((D, LANES), 0), iota((D, LANES), 1)
+    own_lo = hot((c2 < HF) & (r2 == HF * m + c2))
+    own_hi = hot((c2 >= HF) & (r2 == HF * m + c2 - HF))
+    last_lo = hot((c2 < HF) & (r2 == last + c2))
+    last_hi = hot((c2 >= HF) & (r2 == last + c2 - HF))
+    wq, wk, wv = wq_ref[...], wk_ref[...], wv_ref[...]
+    wq2 = nn(wq, own_lo + last_hi).astype(BF)
+    wkv = (nn(wk, own_lo) + nn(wv, own_hi)).astype(BF)
+    wkv5 = (nn(wk, last_lo) + nn(wv, last_hi)).astype(BF)
+    bq, bv = vec(bq_ref), vec(bv_ref)
+    bq2 = jnp.concatenate([own_head(bq), bq[:, last:]], axis=1)
+    nil = jnp.zeros((1, HF), F32)
+    bkv = jnp.concatenate([nil, own_head(bv)], axis=1)
+    bkv5 = jnp.concatenate([nil, bv[:, last:]], axis=1)
+
+    dgx[...] = jnp.zeros_like(dgx)
+    dzx[...] = jnp.zeros_like(dzx)
+    for p in range(4):
+        dgx[p, sz.top : sz.top + PL, :] = (
+            nt(dfm[PL * p : PL * (p + 1), :], w2_ref[...]).astype(BF).astype(F32)
+        )
+
+    rp, cp = iota((4 * LANES, D), 0), iota((4 * LANES, D), 1)
+    place_in = hot(((rp & (LANES - 1)) < FS) & (cp == FS * (rp >> 7) + (rp & (LANES - 1))))
+    mp_finish(xg, x_at)
+    for p in range(4):
+        pieces = jnp.concatenate([xg[h, PL * p : PL * (p + 1), :] for h in range(4)], axis=1)
+        xm = nn(pieces, place_in) * token_mask(p // 2, p % 2)
+        xm_r[PL * p : PL * (p + 1), :] = xm.astype(BF)
+        xhat, _ = spread(xm)
+        n1_r[PL * p : PL * (p + 1), :] = (xhat * vec(ln1g_ref) + vec(ln1b_ref)).astype(BF)
+
+    red = sum(
+        nn(n1_r[PL * p : PL * (p + 1), :], wr_ref[D * p : D * (p + 1), :]) for p in range(4)
+    ) + vec(br_ref)
+    xhr, rsr = spread(red)
+    xhr_r[...] = xhr
+    rsr_r[...] = jnp.broadcast_to(rsr, (PL, LANES))
+    xr_r[...] = (xhr * vec(lnrg_ref) + vec(lnrb_ref)).astype(BF)
+    kva[d, 0:PL, :] = (nn(xr_r[...], wkv) + bkv).astype(BF)
+    part = xr_r[pl.ds(pl.multiple_of(sz.step * m, 16), sz.quarter), :]
+    kva[d, PL:, :] = (nn(part, wkv5) + bkv5).astype(BF)
+    kv_at = dp_start(kva)
+
+    q2t = ((nn(n1_r[...], wq2) + bq2).astype(BF).astype(F32) * HF ** (-0.5)).T
+    half = jnp.zeros((HF, T), F32)
+    qa_r[...] = jnp.concatenate([q2t[0:HF], half], axis=0).astype(BF)
+    qb_r[...] = jnp.concatenate([q2t[HF:], half], axis=0).astype(BF)
+
+    dp_finish(dyh, dy_at)
+    from_above = jnp.where(m >= 2, above, below)
+    dyh_g[m] = dyh[from_above]
+    dyg_at = mp_start(dyh_g)
+    dp_finish(kva, kv_at)
+
+    limit5 = jnp.where(m == sz.n_mp - 1, KEYS - sz.step * m, sz.step)
+    pk = iota((sz.quarter, 1), 0)
+    bias5 = jnp.concatenate(
+        [
+            jnp.where(pk < limit5, key_bias(pk + sz.step * m, tiles[k], KEYS), NEG)
+            for k in range(sz.n_dp)
+        ],
+        axis=0,
+    )
+    kv5 = kva[:, PL:, :].reshape(sz.n_dp * sz.quarter, LANES)
+    s5 = nn(kv5, qb_r[...]) + bias5
+    m5 = jnp.max(s5, axis=0, keepdims=True)
+    e5 = jnp.exp(s5 - m5)
+    l5 = rowsum(e5)
+    e5b = e5.astype(BF)
+    e5buf[...] = e5b.reshape(sz.n_dp, sz.quarter, T)
+    o5t = tn(kv5, e5b)
+    lse_r[m] = jnp.broadcast_to(m5 + jnp.log(l5), (8, T))
+    lse_at = mp_scatter(lambda h: lse_r.at[m], lambda k: lse_r.at[m])
+
+    pk = iota((PL, 1), 0)
+
+    def score_step(j, top):
+        s = nn(kva[j, 0:PL, :], qa_r[...]) + key_bias(pk, slot_ref[j, 1], KEYS)
+        sbuf[j] = s
+        return jnp.maximum(top, jnp.max(s, axis=0, keepdims=True))
+
+    top = lax.fori_loop(0, sz.n_dp, score_step, jnp.full((1, T), NEG, F32))
+
+    def exp_step(j, total):
+        e = jnp.exp(sbuf[j] - top)
+        ebuf[j] = e.astype(BF)
+        return total + rowsum(e)
+
+    total = lax.fori_loop(0, sz.n_dp, exp_step, jnp.zeros((1, T), F32))
+    ot = tn(
+        kva[:, 0:PL, :].reshape(sz.n_dp * PL, LANES), ebuf[...].reshape(sz.n_dp * PL, T)
+    )
+    inv = 1.0 / total
+    for k in (1, 2, 3):
+        arrived(lse_r.at[mpx(k)], lse_at + k)
+    lses = [lse_r[h][0:1] for h in range(4)]
+    lmax = jnp.maximum(jnp.maximum(lses[0], lses[1]), jnp.maximum(lses[2], lses[3]))
+    lse5 = lmax + jnp.log(sum(jnp.exp(v - lmax) for v in lses))
+    f5 = jnp.exp(m5 - lse5)
+    row_r[0:1, :] = inv
+    row_r[1:2, :] = f5
+    o2t = jnp.concatenate([ot[HF:] * inv, o5t[HF:] * f5], axis=0)
+    og[m] = o2t.T.astype(BF)
+    og_at = mp_start(og)
+
+    mp_finish(dyh_g, dyg_at)
+    for p in range(4):
+        i, j = p // 2, p % 2
+        start = sz.top - PB if i == 1 else sz.top + KEYS
+        rows = dyh_g[p][:, :D].astype(F32)[0:PB] if i == 0 else dyh_g[p][:, :D].astype(F32)[0:PB]
+        rows = rows * halo_mask(i, j, -1 if i == 1 else PA)
+        dgx[p, start : start + PB, :] = nt(rows.astype(BF), w2_ref[...]).astype(BF).astype(F32)
+
+    wo = wo_ref[...]
+    wo_cat = jnp.concatenate(
+        [b for h in range(4) for b in (wo[HF * h : HF * (h + 1)], wo[last:])], axis=0
+    )
+    mp_finish(og, og_at)
+    for p in range(4):
+        oc = jnp.concatenate([og[h, PL * p : PL * (p + 1), :] for h in range(4)], axis=1)
+        h1 = xm_r[PL * p : PL * (p + 1), :].astype(F32) + token_mask(p // 2, p % 2) * (
+            nn(oc, wo_cat) + vec(bo_ref)
+        )
+        h1_r[PL * p : PL * (p + 1), :] = h1
+        xhat, _ = spread(h1)
+        n2_r[PL * p : PL * (p + 1), :] = (xhat * vec(ln2g_ref) + vec(ln2b_ref)).astype(BF)
+
+    mine = plane_rows(n2_r, PL * m).astype(F32)
+    hal_s[:, :D] = jnp.concatenate([mine[0:PB], mine[KEYS - PB : KEYS]], axis=0).astype(BF)
+    hal_s[:, D:] = jnp.zeros((2 * PB, sz.wide - D), BF)
+    hal[d] = hal_s[...]
+    hal_at = dp_start(hal)
+
+    def hidden(rows, mask):
+        return ((nn(rows, w1_ref[...]) + vec(b1_ref)) * mask).astype(BF).astype(F32)
+
+    for p in range(4):
+        ux[p, 0 : sz.top, :] = jnp.zeros((sz.top, C), F32)
+        ux[p, sz.top : sz.top + PL, :] = hidden(
+            n2_r[PL * p : PL * (p + 1), :], token_mask(p // 2, p % 2)
+        )
+    dp_finish(hal, hal_at)
+    up_rows = hal[above].astype(F32)[PB:]
+    down_rows = hal[below].astype(F32)[0:PB]
+    hal_g[m] = jnp.concatenate([up_rows, down_rows], axis=0).astype(BF)
+    halg_at = mp_start(hal_g)
+    mp_finish(hal_g, halg_at)
+    for p in range(4):
+        i, j = p // 2, p % 2
+        mask = jnp.concatenate([halo_mask(i, j, -1), halo_mask(i, j, PA)], axis=0)
+        u = hidden(hal_g[p][:, :D], mask)
+        ux[p, sz.top - PB : sz.top, :] = u[0:PB]
+        ux[p, sz.top + KEYS : sz.top + KEYS + PB, :] = u[PB:]
+
+    _, be = place(iota((sz.ext, 1), 0) + (PB - 8), PA + 3)
+
+    def shifted(src, left, right):
+        for i in range(2):
+            left[i] = jnp.where(be == 0, 0.0, pltpu.roll(src[2 * i + 1], 1, 0))
+            right[i] = jnp.where(be == PB - 1, 0.0, pltpu.roll(src[2 * i], sz.ext - 1, 0))
+
+    def source(refs, i, j, di, dj, start):
+        base, left, right = refs
+        i2, up = (i + di) % 2, (i + di) // 2
+        j2, across = (j + dj) % 2, (j + dj) // 2
+        at = pl.ds(pl.multiple_of(start + PB * up, 8), PB)
+        if across < 0:
+            return left[i2, at, :]
+        if across > 0:
+            return right[i2, at, :]
+        return base[2 * i2 + j2, at, :]
+
+    TAPS = [(di, dj) for di in (-1, 0, 1) for dj in (-1, 0, 1)]
+    shifted(ux, ul, ur)
+    g_r[...] = jnp.zeros_like(g_r)
+    du_r[...] = jnp.zeros_like(du_r)
+
+    def activation(i, j, start):
+        p = 2 * i + j
+        z = vec(bd_ref) + sum(
+            wd_ref[t : t + 1, :] * source((ux, ul, ur), i, j, di, dj, start)
+            for t, (di, dj) in enumerate(TAPS)
+        )
+        phi = 0.5 * (1.0 + lax.erf(z * 0.7071067811865476))
+        dens = jnp.exp(-0.5 * z * z) * 0.3989422804014327
+        dz = dgx[p, pl.ds(pl.multiple_of(start, 8), PB), :] * (phi + z * dens)
+        dzx[p, pl.ds(pl.multiple_of(start, 8), PB), :] = dz
+        return z * phi, dz
+
+    def fold(value):
+        return jnp.sum(value.reshape(PB // 8, 8, C), axis=0)
+
+    sums = [jnp.zeros((8, C), F32) for _ in range(10)]
+    for i in range(2):
+        for j in range(2):
+            p = 2 * i + j
+            activation(i, j, sz.top - PB if i == 1 else sz.top + KEYS)
+
+            def forward_step(a, acc, i=i, j=j, p=p):
+                start = sz.top + PB * a
+                act, dz = activation(i, j, start)
+                g_r[p, pl.ds(pl.multiple_of(PB * a, 8), PB), :] = act
+                new = [
+                    acc[t] + fold(dz * source((ux, ul, ur), i, j, di, dj, start))
+                    for t, (di, dj) in enumerate(TAPS)
+                ]
+                return tuple(new) + (acc[9] + fold(dz),)
+
+            sums = lax.fori_loop(0, PA, forward_step, tuple(sums))
+    for t in range(10):
+        ve_s[t : t + 1, :C] = rowsum(sums[t])
+    shifted(dzx, dzl, dzr)
+    for i in range(2):
+        for j in range(2):
+            p = 2 * i + j
+
+            def backward_step(a, carry, i=i, j=j, p=p):
+                start = sz.top + PB * a
+                du_r[p, pl.ds(pl.multiple_of(PB * a, 8), PB), :] = sum(
+                    wd_ref[t : t + 1, :] * source((dzx, dzl, dzr), i, j, -di, -dj, start)
+                    for t, (di, dj) in enumerate(TAPS)
+                )
+                return carry
+
+            lax.fori_loop(0, PA, backward_step, 0)
+    dus = []
+    for p in range(4):
+        du = du_r[p].astype(BF).astype(F32) * token_mask(p // 2, p % 2)
+        dus.append(du.astype(BF))
+        dn2_s[p, :, :D] = nt(dus[p], w1_ref[...]).astype(BF)
+    ve_s[10:11, :C] = sum(rowsum(v.astype(F32)) for v in dus)
+    dn2_at = mp_scatter(lambda h: dn2_s.at[h], lambda k: dn2_r.at[k - 1])
+
+    dub = jnp.concatenate(dus, axis=0)
+    gb = g_r[...].reshape(T, C).astype(BF)
+    e_s[0:D, :C] = tn(n2_r[...], dub).astype(BF)
+    e_s[D : D + C, :D] = tn(gb, dfm[...]).astype(BF)
+
+    for k in (1, 2, 3):
+        arrived(dn2_r.at[k - 1], dn2_at + k)
+    dn2 = dn2_s[m][:, :D].astype(F32) + sum(dn2_r[k][:, :D].astype(F32) for k in range(3))
+    xhat2, rstd2 = spread(plane_rows(h1_r, PL * m))
+    dfp = plane_rows(dfm, PL * m).astype(F32)
+    dh1 = dfp + norm_back(dn2, vec(ln2g_ref), xhat2, rstd2)
+    dh1_r[...] = dh1
+    dab = dh1.astype(BF)
+    docat = nt(dab, wo_cat).astype(BF)
+    for h in range(4):
+        dos[h] = docat[:, LANES * h : LANES * (h + 1)]
+    do_at = mp_scatter(lambda h: dos.at[h], lambda k: do_all.at[m])
+    do_all[m] = dos[m]
+    dabg[m, :, :D] = dab
+    dab_at = mp_start(dabg)
+    ve_s[11:12, :D] = rowsum(dfp)
+    ve_s[12:13, :D] = rowsum(dh1)
+    ve_s[13:14, :D] = rowsum(dn2 * xhat2)
+    ve_s[14:15, :D] = rowsum(dn2)
+    ve_s[15:16, :] = jnp.zeros((1, sz.wide), F32)
+
+    rt, ct = iota((D, 4 * LANES), 0), iota((D, 4 * LANES), 1)
+    place_out = hot(((ct & (LANES - 1)) < FS) & (rt == FS * (ct >> 7) + (ct & (LANES - 1))))
+    ff = nn(gb, nn(w2_ref[...], place_out).astype(BF)).astype(BF)
+    for h in range(4):
+        ff_s[h] = ff[:, LANES * h : LANES * (h + 1)]
+
+    for k in (1, 2, 3):
+        arrived(do_all.at[mpx(k)], do_at + k)
+    ff_at = mp_scatter(lambda h: ff_s.at[h], lambda k: ff_r.at[k - 1])
+    do2 = do_all[...].reshape(T, LANES).astype(F32)
+    lane = iota((T, LANES), 1)
+    o_own = og[m].astype(F32)
+    o_mix = jnp.where(lane < HF, o_own, sum(og[h].astype(F32) for h in range(4)))
+    prod = (do2 * o_mix).T
+    dot_t = do2.T
+    inv, f5 = row_r[0:1, :], row_r[1:2, :]
+    da_t = jnp.concatenate([half, dot_t[0:HF] * inv], axis=0).astype(BF)
+    db_t = jnp.concatenate([half, dot_t[HF:] * f5], axis=0).astype(BF)
+    drow = rowsum(prod[0:HF]) * inv
+    drow5 = rowsum(prod[HF:]) * f5
+    dqt[...] = jnp.zeros_like(dqt)
+    dqt5[...] = jnp.zeros_like(dqt5)
+
+    def key_block(j):
+        kv = kva[j, 0:PL, :]
+        e = ebuf[j]
+        ds = (e.astype(F32) * (nn(kv, da_t) - drow)).astype(BF)
+        dks[j, 0:PL, :] = (nt(ds, qa_r[...]) + nt(e, da_t)).astype(BF)
+        dqt[...] += tn(kv, ds)
+        kv = kva[j, PL:, :]
+        e = e5buf[j]
+        ds = (e.astype(F32) * (nn(kv, db_t) - drow5)).astype(BF)
+        dks[j, PL:, :] = (nt(ds, qb_r[...]) + nt(e, db_t)).astype(BF)
+        dqt5[...] += tn(kv, ds)
+
+    dk_at = take(8)
+
+    def send_step(k, carry):
+        j = lax.rem(d + k, sz.n_dp)
+        key_block(j)
+        copy(dks.at[j], dkr.at[k - 1], dk_at + k, (j, m)).start()
+        return carry
+
+    lax.fori_loop(1, sz.n_dp, send_step, 0)
+    key_block(d)
+
+    dq2 = (jnp.concatenate([dqt[0:HF], dqt5[0:HF]], axis=0) * HF ** (-0.5)).T.astype(BF)
+    for h in range(4):
+        dqs[h] = dq2[PL * h : PL * (h + 1)]
+    dq_at = mp_scatter(lambda h: dqs.at[h], lambda k: dq_all.at[m])
+    dq_all[m] = dqs[m]
+    l_s[0:D, 0:LANES] = tn(n1_r[...], dq2).astype(BF)
+    vl_s[...] = jnp.zeros_like(vl_s)
+    vl_s[5:6, 0:LANES] = rowsum(dq2.astype(F32))
+    mp_finish(dabg, dab_at)
+    e_s[D + C :, :D] = tn(og[m], dabg[...].reshape(T, sz.wide)[:, :D]).astype(BF)
+    e_at = dp_scatter(
+        lambda j: e_s.at[pl.ds(pl.multiple_of(sz.echunk * j, 16), sz.echunk)],
+        lambda k: e_r.at[k - 1],
+    )
+    ve_at = dp_scatter(lambda j: ve_s, lambda k: ve_r.at[d])
+    ve_r[d] = ve_s[...]
+
+    for k in (1, 2, 3):
+        arrived(ff_r.at[k - 1], ff_at + k)
+    sel = hot((c2 < FS) & (r2 == FS * m + c2))
+    b2 = vec(b2_ref)
+    b2q = sum(jnp.where(m == h, 1.0, 0.0) * b2[:, FS * h : FS * (h + 1)] for h in range(4))
+    b2q = jnp.concatenate([b2q, jnp.zeros((1, LANES - FS), F32)], axis=1)
+    for p in range(4):
+        at = slice(PL * p, PL * (p + 1))
+        h1 = h1_r[at, :]
+        hi = h1.astype(BF)
+        h1q = nn(hi, sel) + nn((h1 - hi.astype(F32)).astype(BF), sel)
+        ffq = ff_s[m, at, :].astype(F32) + sum(ff_r[k, at, :].astype(F32) for k in range(3))
+        blk_ref[at, :] = h1q + token_mask(p // 2, p % 2) * (ffq + b2q)
+
+    for k in range(1, sz.n_dp):
+        arrived(dkr.at[k - 1], dk_at + k)
+    dkv = dks[d].astype(F32) + sum(dkr[k].astype(F32) for k in range(sz.n_dp - 1))
+    dkvb = dkv.astype(BF)
+    dkvg[m] = dkvb
+    dkv_at = mp_start(dkvg)
+    l_s[0:D, LANES : 2 * LANES] = tn(xr_r[...], dkvb[0:PL]).astype(BF)
+    part = xr_r[pl.ds(pl.multiple_of(sz.step * m, 16), sz.quarter), :]
+    l_s[0:D, 2 * LANES :] = tn(part, dkvb[PL:]).astype(BF)
+    bvg = jnp.concatenate(
+        [rowsum(dkvb[0:PL].astype(F32))[:, HF:], rowsum(dkvb[PL:].astype(F32))[:, HF:]], axis=1
+    )
+    vl_s[6:7, 0:LANES] = bvg
+    rk, ck = iota((D, 5 * LANES), 0), iota((D, 5 * LANES), 1)
+    lane5 = ck & (LANES - 1)
+    head5 = ck >> 7
+    w_all = (
+        nn(wk, hot((lane5 < HF) & (rk == HF * head5 + lane5)))
+        + nn(wv, hot((lane5 >= HF) & (rk == HF * head5 + lane5 - HF)))
+    ).astype(BF)
+    lane4 = ct & (LANES - 1)
+    head4 = ct >> 7
+    wq_cat = nn(
+        wq, hot(rt == jnp.where(lane4 < HF, HF * head4 + lane4, last + lane4 - HF))
+    ).astype(BF)
+    mp_finish(dkvg, dkv_at)
+    tail = jnp.concatenate(
+        [dkvg[h, PL : PL + sz.step, :] for h in range(3)] + [dkvg[3, PL:, :]], axis=0
+    )
+    dkv_all = jnp.concatenate([dkvg[h, 0:PL, :] for h in range(4)] + [tail], axis=1)
+    dxr = nt(dkv_all, w_all)
+    xhr = xhr_r[...]
+    vl_s[2:3, :D] = rowsum(dxr * xhr)
+    vl_s[3:4, :D] = rowsum(dxr)
+    drb = norm_back(dxr, vec(lnrg_ref), xhr, rsr_r[:, 0:1]).astype(BF)
+    vl_s[4:5, :D] = rowsum(drb.astype(F32))
+    l_s[D:, :D] = tn(plane_rows(n1_r, PL * m), drb).astype(BF)
+    l_s[D:, D:] = jnp.zeros((D, sz.wide - D), BF)
+    l_at = dp_scatter(
+        lambda j: l_s.at[pl.ds(pl.multiple_of(sz.lchunk * j, 16), sz.lchunk)],
+        lambda k: l_r.at[k - 1],
+    )
+
+    for k in (1, 2, 3):
+        arrived(dq_all.at[mpx(k)], dq_at + k)
+    dq_cat = jnp.concatenate([dq_all[h] for h in range(4)], axis=1)
+    wr_m = wr_ref[pl.ds(pl.multiple_of(D * m, 16), D), :]
+    dn1 = nt(dq_cat, wq_cat) + nt(drb, wr_m)
+    xhat1, rstd1 = spread(plane_rows(xm_r, PL * m).astype(F32))
+    vl_s[0:1, :D] = rowsum(dn1 * xhat1)
+    vl_s[1:2, :D] = rowsum(dn1)
+    vl_at = dp_scatter(lambda j: vl_s, lambda k: vl_r.at[d])
+    vl_r[d] = vl_s[...]
+    masks = [token_mask(p // 2, p % 2) for p in range(4)]
+    mask_m = sum(jnp.where(m == p, 1.0, 0.0) * masks[p] for p in range(4))
+    dxm = norm_back(dn1, vec(ln1g_ref), xhat1, rstd1)
+    gp = (mask_m * (dh1_r[...] + dxm)).astype(BF)
+    gpf = nn(gp, place_out).astype(BF)
+    for h in range(4):
+        gps[h] = gpf[:, LANES * h : LANES * (h + 1)]
+    gp_at = mp_scatter(lambda h: gps.at[h], lambda k: gp_ref.at[m])
+    gp_ref[m] = gps[m]
+
+    for k in range(1, sz.n_dp):
+        arrived(e_r.at[k - 1], e_at + k)
+    mine = e_s[pl.ds(pl.multiple_of(sz.echunk * d, 16), sz.echunk), :].astype(F32)
+    eg_ref[d] = (mine + sum(e_r[k].astype(F32) for k in range(sz.n_dp - 1))).astype(BF)
+    eg_at = dp_start(eg_ref)
+    for k in range(1, sz.n_dp):
+        arrived(ve_r.at[dpx(k)], ve_at + k)
+    veg_ref[m] = sum(ve_r[k] for k in range(sz.n_dp))
+    veg_at = mp_start(veg_ref)
+
+    for k in range(1, sz.n_dp):
+        arrived(l_r.at[k - 1], l_at + k)
+    mine = l_s[pl.ds(pl.multiple_of(sz.lchunk * d, 16), sz.lchunk), :].astype(F32)
+    lg_ref[m, d] = (mine + sum(l_r[k].astype(F32) for k in range(sz.n_dp - 1))).astype(BF)
+    own = lg_ref.at[m]
+    lg_at = dp_start(own)
+    over = take(3 * sz.n_dp)
+
+    def across(k):
+        j = dpx(k)
+        send(lg_ref.at[m, j], lg_ref.at[m, j], over + 3 * k, (d, mpx(1)))
+        send(lg_ref.at[m, j], lg_ref.at[m, j], over + 3 * k + 1, (d, mpx(2)))
+
+    across(0)
+    for k in range(1, sz.n_dp):
+        arrived(vl_r.at[dpx(k)], vl_at + k)
+    vlg_ref[m] = sum(vl_r[k] for k in range(sz.n_dp))
+    vlg_at = mp_start(vlg_ref)
+    dp_finish(own, lg_at, across)
+    dp_finish(eg_ref, eg_at)
+    first = sz.erows - 2 * HF
+    for k in range(2 * HF // 16):
+        row = first + 16 * k
+        wog_ref[m, 16 * k : 16 * (k + 1), :] = eg_ref[
+            row // sz.echunk, row % sz.echunk : row % sz.echunk + 16, :
+        ]
+    wog_at = mp_start(wog_ref)
+    mp_finish(veg_ref, veg_at)
+    mp_finish(vlg_ref, vlg_at)
+    order = [0, 2, 4, 6, 1, 3, 5, 7]
+    for k in order:
+        j = dpx(k)
+        arrived(lg_ref.at[mpx(2), j], over + 3 * k + 1)
+        send(lg_ref.at[mpx(2), j], lg_ref.at[mpx(2), j], over + 3 * k + 2, (d, mpx(1)))
+    mp_finish(wog_ref, wog_at)
+    for k in order:
+        arrived(lg_ref.at[mpx(1), dpx(k)], over + 3 * k)
+        arrived(lg_ref.at[mpx(3), dpx(k)], over + 3 * k + 2)
+    for k in (1, 2, 3):
+        arrived(gp_ref.at[mpx(k)], gp_at + k)
+    for c in pending:
+        c.wait_send()
+    for k in range(1, sz.n_dp):
+        copy(dks.at[0], dkr.at[0], dk_at + k, (d, m)).wait_send()
+
+
+def unpack_body(
+    sz, blk_ref, gp_ref, eg_ref, wog_ref, lg_ref, veg_ref, vlg_ref,
+    out_ref, gpix_ref, ln1g_ref, ln1b_ref, gwq_ref, gbq_ref, gwk_ref, gwv_ref, gbv_ref, gwr_ref, gbr_ref,
+    lnrg_ref, lnrb_ref, gwo_ref, gbo_ref, ln2g_ref, ln2b_ref, gw1_ref, gb1_ref, gwd_ref, gbd_ref,
+    gw2_ref, gb2_ref, out32,
+):
+    D, HF, PB, PA, PL = sz.width, HEAD_FEATURES, sz.pb, sz.pa, sz.plane
+    C, FS = sz.hidden, sz.share
+    m = lax.axis_index("mp")
+    for i in range(2):
+        for j in range(2):
+            p = 2 * i + j
+            for a in range(PA):
+                at = pl.ds((2 * a + i) * sz.cols + j, PB, stride=2)
+                out32[at, :] = blk_ref[PL * p + PB * a : PL * p + PB * (a + 1), 0:FS]
+                gpix_ref[at, :] = gp_ref[p].astype(F32)[PB * a : PB * (a + 1), 0:FS]
+    out_ref[...] = out32[...].astype(BF)
+
+    lg = [lg_ref[h].reshape(sz.lrows, sz.wide) for h in range(4)]
+
+    def heads(first, tail):
+        parts = [lg[h][0:D, first : first + HF].astype(F32) for h in range(4)]
+        parts.append(sum(lg[h][0:D, tail : tail + HF].astype(F32) for h in range(4)))
+        return jnp.concatenate(parts, axis=1)
+
+    gwq_ref[...] = heads(0, HF)
+    gwk_ref[...] = heads(LANES, 2 * LANES)
+    gwv_ref[...] = heads(LANES + HF, 2 * LANES + HF)
+    for h in range(4):
+        gwr_ref[D * h : D * (h + 1), :] = lg[h][D:, :D].astype(F32)
+    for h in range(4):
+        gwo_ref[HF * h : HF * (h + 1), :] = wog_ref[h][0:HF, :D].astype(F32)
+    gwo_ref[HF * 4 :, :] = sum(wog_ref[h][HF:, :D].astype(F32) for h in range(4))
+    eg = eg_ref[...].reshape(sz.erows, sz.wide)
+    gw1_ref[...] = eg[0:D, :C].astype(F32)
+    gw2_ref[...] = eg[D : D + C, :D].astype(F32)
+
+    def row(value):
+        return value.reshape(value.shape[1])
+
+    ve = veg_ref[m]
+    gwd_ref[...] = ve[0:9, :C]
+    gbd_ref[...] = row(ve[9:10, :C])
+    gb1_ref[...] = row(ve[10:11, :C])
+    vs = sum(veg_ref[h] for h in range(4))
+    gb2_ref[...] = row(vs[11:12, :D])
+    gbo_ref[...] = row(vs[12:13, :D])
+    ln2g_ref[...] = row(vs[13:14, :D])
+    ln2b_ref[...] = row(vs[14:15, :D])
+    vl = sum(vlg_ref[h] for h in range(4))
+    ln1g_ref[...] = row(vl[0:1, :D])
+    ln1b_ref[...] = row(vl[1:2, :D])
+    lnrg_ref[...] = row(vlg_ref[0][2:3, :D])
+    lnrb_ref[...] = row(vlg_ref[0][3:4, :D])
+    gbr_ref[...] = row(vlg_ref[0][4:5, :D])
+
+    def head_row(r):
+        parts = [vlg_ref[h][r : r + 1, 0:HF] for h in range(4)] + [vl[r : r + 1, HF : 2 * HF]]
+        return row(jnp.concatenate(parts, axis=1))
+
+    gbq_ref[...] = head_row(5)
+    gbv_ref[...] = head_row(6)
+
+
+def on_device_fused(*args):
+    pixels_in, cotangent, pixel_mask, tile_slot = args[:4]
+    w_fc1 = args[19]
+    sz = Sizes(
+        lax.axis_size("dp"), lax.axis_size("mp"), pixels_in.shape[0], cotangent.shape[1], w_fc1.shape[1]
+    )
+    D, C, PL, T, W, LN = sz.width, sz.hidden, sz.plane, sz.all, sz.wide, LANES
+    vm = pl.BlockSpec(memory_space=pltpu.VMEM)
+    sm = pl.BlockSpec(memory_space=pltpu.SMEM)
+    S = jax.ShapeDtypeStruct
+    mids = [
+        S((T, LN), F32), S((4, PL, LN), BF), S((sz.n_dp, sz.echunk, W), BF), S((4, 2 * HEAD_FEATURES, W), BF),
+        S((4, sz.n_dp, sz.lchunk, W), BF), S((4, 16, W), F32), S((4, 8, W), F32),
+    ]
+    v = pltpu.VMEM
+    scratch = dict(
+        x32=v((sz.tokens, sz.share), F32), c32a=v((sz.tokens, LN), F32), c32b=v((sz.tokens, LN), F32),
+        c32c=v((sz.tokens, D - 2 * LN), F32), xg=v((4, T, LN), BF), dfm=v((T, D), BF), dyh_s=v((48, W), BF),
+        dyh=v((sz.n_dp, 48, W), BF), dyh_g=v((4, 48, W), BF), xm_r=v((T, D), BF), n1_r=v((T, D), BF),
+        xhr_r=v((PL, D), F32), rsr_r=v((PL, LN), F32), xr_r=v((PL, D), BF), kva=v((sz.n_dp, sz.kvrows, LN), BF),
+        qa_r=v((LN, T), BF), qb_r=v((LN, T), BF), sbuf=v((sz.n_dp, PL, T), F32), ebuf=v((sz.n_dp, PL, T), BF),
+        e5buf=v((sz.n_dp, sz.quarter, T), BF), lse_r=v((4, 8, T), F32), og=v((4, T, LN), BF), row_r=v((8, T), F32),
+        h1_r=v((T, D), F32), n2_r=v((T, D), BF), hal_s=v((2 * sz.pb, W), BF), hal=v((sz.n_dp, 2 * sz.pb, W), BF),
+        hal_g=v((4, 2 * sz.pb, W), BF), ux=v((4, sz.ext, C), F32), ul=v((2, sz.ext, C), F32),
+        ur=v((2, sz.ext, C), F32), dgx=v((4, sz.ext, C), F32), dzx=v((4, sz.ext, C), F32),
+        dzl=v((2, sz.ext, C), F32), dzr=v((2, sz.ext, C), F32), g_r=v((4, PL, C), F32), du_r=v((4, PL, C), F32),
+        dn2_s=v((4, PL, W), BF), dn2_r=v((3, PL, W), BF), dh1_r=v((PL, D), F32), dos=v((4, PL, LN), BF),
+        do_all=v((4, PL, LN), BF), dabg=v((4, PL, W), BF), ff_s=v((4, T, LN), BF), ff_r=v((3, T, LN), BF),
+        dks=v((sz.n_dp, sz.kvrows, LN), BF), dkr=v((sz.n_dp - 1, sz.kvrows, LN), BF), dkvg=v((4, sz.kvrows, LN), BF),
+        dqs=v((4, PL, LN), BF), dq_all=v((4, PL, LN), BF), dqt=v((LN, T), F32), dqt5=v((LN, T), F32),
+        e_s=v((sz.erows, W), BF), e_r=v((sz.n_dp - 1, sz.echunk, W), BF), l_s=v((sz.lrows, W), BF),
+        l_r=v((sz.n_dp - 1, sz.lchunk, W), BF), ve_s=v((16, W), F32), ve_r=v((sz.n_dp, 16, W), F32),
+        vl_s=v((8, W), F32), vl_r=v((sz.n_dp, 8, W), F32), gps=v((4, PL, LN), BF),
+        ssem=pltpu.SemaphoreType.DMA((176,)), rsem=pltpu.SemaphoreType.DMA((176,)),
+    )
+    mid = pl.pallas_call(
+        functools.partial(fused_body, sz),
+        out_shape=mids,
+        in_specs=[sm, sm] + [vm] * 23,
+        out_specs=[vm] * len(mids),
+        scratch_shapes=list(scratch.values()),
+        compiler_params=pltpu.CompilerParams(
+            collective_id=0, has_side_effects=True, vmem_limit_bytes=60 * 2**20
+        ),
+        name="fused_block",
+    )(pixel_mask, tile_slot, pixels_in, cotangent, *args[4:])
+    outs = [
+        S((sz.tokens, sz.share), BF), S((sz.tokens, sz.share), F32), S((D,), F32), S((D,), F32), S((D, D), F32),
+        S((D,), F32), S((D, D), F32), S((D, D), F32), S((D,), F32), S((4 * D, D), F32), S((D,), F32), S((D,), F32),
+        S((D,), F32), S((D, D), F32), S((D,), F32), S((D,), F32), S((D,), F32), S((D, C), F32), S((C,), F32),
+        S((9, C), F32), S((C,), F32), S((C, D), F32), S((D,), F32),
+    ]
+    return tuple(
+        pl.pallas_call(
+            functools.partial(unpack_body, sz),
+            out_shape=outs,
+            in_specs=[vm] * len(mids),
+            out_specs=[vm] * len(outs),
+            scratch_shapes=[pltpu.VMEM((sz.tokens, sz.share), F32)],
+            compiler_params=pltpu.CompilerParams(vmem_limit_bytes=40 * 2**20),
+            name="unpack",
+        )(*mid)
+    )
+
+
+def choose(*args):
+    tokens, width = args[1].shape
+    whole_rows = tokens == FRAME * (FRAME // TILE_ROWS)
+    shape = (lax.axis_size("dp"), lax.axis_size("mp"))
+    if whole_rows and shape == (TILE_ROWS, 4) and TILE_ROWS == 8 and HEADS == 5 and width == 320 == args[19].shape[1]:
+        return on_device_fused(*args)
+    return on_device(*args)
+
+
 def solution(mesh):
     return jax.shard_map(
-        on_device,
+        choose,
         mesh=mesh,
         in_specs=(
             P("dp", "mp"),

time: 924 us -> 178 us (0.19)
  waiting for transfers between devices: 359 us -> 0 us
  blocking collectives: 298 us -> 0 us
  Pallas kernels: 0 us -> 160 us
  matrix products: 91.7 us -> 0 us
  local copies, waits for them, and re-layouts: 97 us -> 17.2 us
  other arithmetic: 50.8 us -> 0 us
  between operations: 18.3 us -> 0.69 us
    psum x5 -> x0, waiting for transfers between devices: 256 us -> none  [the longest x1 116 us: on_device(): lax.psum((grad_w_reduce, grad_b_reduce, grad_lnr_gain, grad_lnr_bias, gra...]
    all_gather x7 -> x0, blocking collectives: 199 us -> none  [the longest x1 32.8 us: on_device(): lax.all_gather(jnp.stack([tile_u[0], tile_u[-1]]), 'dp', axis=0, tiled=True)]
    pallas_call x0 -> x2, Pallas kernels: none -> 160 us  [the longest x1 157 us: on_device_fused(): pl.pallas_call(functools.partial(fused_body, sz), out_shape=mids, in_spec...]
    unnamed x10 -> x0, waiting for transfers between devices: 103 us -> none
    dot_general x77 -> x0, matrix products: 91.7 us -> none  [the longest x21 22.4 us: mat(): return jnp.dot(left, right, preferred_element_type=jnp.float32)]
    psum x2 -> x0, blocking collectives: 77.8 us -> none  [the longest x1 39.7 us: on_device(): lax.psum((spread_columns(grad_wq, select_where), spread_vector(grad_bq, s...]
    reshape x20 -> x0, local copies, waits for them, and re-layouts: 35.5 us -> none  [the longest x4 11.7 us: on_device(): dpatch = mat(drb, w_reduce.T).reshape(rows // 2, cols // 2, 2, 2, width)....]
    reduce_sum x23 -> x0, other arithmetic: 34.3 us -> none  [the longest x4 9.89 us: top_step(): jnp.sum(jnp.exp(scores - new_top[..., None]), axis=-1)]
  transfers between devices with their start and end apart: 8 -> 0, of which waited for: 7 -> 0; matrix products, arithmetic and copies ran while one was open for 7% -> 0% of each run, Pallas kernels for 0% -> 0%
where the time goes in v1:
time: 178 us; the launch traced here: 177 us
  Pallas kernels  160 us (90%)
  local copies, waits for them, and re-layouts  17.2 us (10%)
    pallas_call x1, Pallas kernels, on_device_fused(): pl.pallas_call(functools.partial(fused_body, sz), out_shape=mids, in_spec...  157 us
    unnamed x20, local copies, waits for them, and re-layouts  13.8 us

profile of v1, /device:TPU:0, one launch (start us, length us, event | category | flops | bytes accessed | tf_op | source)
XLA Modules:
  0.0 177.4 jit_solution(30517141552656401)
XLA Ops:
  0.7 0.0 copy-start.7
  0.7 1.4 copy.48.slot_ref
  2.1 1.7 copy.49.pix_ref
  3.8 2.1 %copy.50.cot_ref = bf16[800,320]{1,0:T(8,128)(2,1)} copy(bf16[800,320]{0,1:T(8,128)(2,1)} %param.26) | data formatting | bytes 1024000 | tf_op args[1]
  5.9 0.0 copy-done.7
  5.9 1.3 copy.51.wr_ref
  7.2 157.5 %fused_block.1 = (f32[832,128]{1,0:T(8,128)}, bf16[4,208,128]{2,1,0:T(8,128)(2,1)}, bf16[8,96,384]{2,1,0:T(8,128)(2,1)}, bf16[4,128,384]{2,1,0:T(8,128)(2,1)}, b...) custom-call(s32[800]{0:T(1024)} %mask_ref.1, s32[8,2]{1,0:T(8,128)} %copy.48.slot_ref, ...), custom_call_target="tpu_custom_call" | custom-call | tf_op jit(solution)/shard_map/fused_block/pallas_call | solution.py:1284
  164.7 0.0 copy-start
  164.7 1.5 copy-done
  166.2 0.0 copy-start.1
  166.2 1.1 copy-done.1
  167.3 0.0 copy-start.2
  167.3 1.0 copy-done.2
  168.3 0.0 copy-start.3
  168.3 1.0 copy-done.3
  169.3 0.0 copy-start.4
  169.3 0.9 copy-done.4
  170.2 0.0 copy-start.5
  170.2 0.9 copy-done.5
  171.1 0.0 copy-start.6
  171.1 0.8 copy-done.6
  171.9 2.1 %unpack.1 = (bf16[800,80]{1,0:T(8,128)(2,1)S(1)}, f32[800,80]{1,0:T(8,128)S(1)}, f32[320]{0:T(512)}, f32[320]{0:T(512)}, f32[320,320]{1,0:T(8,128)}, /*index=5*/...) custom-call(f32[832,128]{1,0:T(8,128)S(1)} %copy-done.2, ...), custom_call_target="tpu_custom_call" | custom-call | tf_op jit(solution)/shard_map/unpack/pallas_call | solution.py:1302
  174.1 0.8 copy.52
  174.9 0.9 copy.53
  175.8 1.7 copy.54
Async XLA Ops:
  0.7 5.3 %copy-start.7 = (bf16[1280,320]{0,1:T(8,128)(2,1)S(1)}, bf16[1280,320]{0,1:T(8,128)(2,1)}, u32[]{:S(2)}) copy-start(bf16[1280,320]{0,1:T(8,128)(2,1)} %param.36) | copy-start | bytes 2457604
  164.7 1.5 copy-start
  166.2 1.1 copy-start.1
  167.3 1.0 copy-start.2
  168.3 1.0 copy-start.3
  169.3 0.9 copy-start.4
  170.2 0.9 copy-start.5
  171.1 0.8 copy-start.6

commit v2 on v0

--- a/solution.py
+++ b/solution.py
@@ -1,6 +1,10 @@
+import functools
+
 import jax
 import jax.numpy as jnp
 from jax import lax
+from jax.experimental import pallas as pl
+from jax.experimental.pallas import tpu as pltpu
 from jax.sharding import PartitionSpec as P
 
 HEADS = 5
@@ -472,9 +476,1053 @@
     )
 
 
+BF = jnp.bfloat16
+F32 = jnp.float32
+LANES = 128
+SIDE_SMALL = 64
+VMEM_MB = 56
+
+
+def nn(a, b):
+    return lax.dot_general(a, b, (((1,), (0,)), ((), ())), preferred_element_type=F32)
+
+
+def nt(a, b):
+    return lax.dot_general(a, b, (((1,), (1,)), ((), ())), preferred_element_type=F32)
+
+
+def tn(a, b):
+    return lax.dot_general(a, b, (((0,), (0,)), ((), ())), preferred_element_type=F32)
+
+
+def iota(shape, axis):
+    return lax.broadcasted_iota(jnp.int32, shape, axis)
+
+
+def hot(cond):
+    return jnp.where(cond, 1.0, 0.0).astype(BF)
+
+
+def spread(value):
+    mean = jnp.sum(value, axis=-1, keepdims=True) * (1.0 / value.shape[-1])
+    centred = value - mean
+    var = jnp.sum(centred * centred, axis=-1, keepdims=True) * (1.0 / value.shape[-1])
+    rstd = lax.rsqrt(var + EPS)
+    return centred * rstd, rstd
+
+
+def norm_back(dn, gain, xhat, rstd):
+    e = dn * gain
+    scale = 1.0 / dn.shape[-1]
+    mean_e = jnp.sum(e, axis=-1, keepdims=True) * scale
+    mean_ex = jnp.sum(e * xhat, axis=-1, keepdims=True) * scale
+    return rstd * (e - mean_e - xhat * mean_ex)
+
+
+def rowsum(value):
+    return jnp.sum(value, axis=0, keepdims=True)
+
+
+class Sizes:
+    def __init__(self, n_dp, n_mp, tokens, width, hidden):
+        self.n_dp, self.n_mp = n_dp, n_mp
+        self.tokens, self.width, self.hidden = tokens, width, hidden
+        self.share = width // n_mp
+        self.rows = FRAME // TILE_ROWS
+        self.cols = tokens // self.rows
+        self.pa, self.pb = self.rows // 2, self.cols // 2
+        self.keys = self.pa * self.pb
+        self.plane = -(-self.keys // 16) * 16
+        self.all = 4 * self.plane
+        self.step = self.plane // 16 // n_mp * 16
+        self.quarter = self.plane - (n_mp - 1) * self.step
+        self.wide = -(-width // LANES) * LANES
+        self.kvrows = self.plane + self.quarter
+        self.top = 8 + self.pb
+        self.ext = self.top + self.keys + self.pb
+        self.edge = 4 * 2 * self.pb
+        self.inner = 4 * (self.keys - 2 * self.pb)
+        self.edge_q = -(-self.edge // LANES) * LANES
+        self.inner_q = -(-self.inner // LANES) * LANES
+        self.queries = self.edge_q + self.inner_q
+        self.echunk = (width + hidden) // n_dp
+        self.lrows = width + HEAD_FEATURES
+        self.lchunk = self.lrows // n_dp
+
+
+class Load:
+    def __init__(self, src, dst, sem):
+        self.dst, self.shape, self.waiting = dst, dst.shape, True
+        self.copy = pltpu.make_async_copy(src, dst, sem)
+        self.copy.start()
+
+    def ready(self):
+        if self.waiting:
+            self.waiting = False
+            self.copy.wait()
+        return self.dst
+
+    def __getitem__(self, at):
+        return self.ready()[at]
+
+
+def fused_body(
+    sz, names,
+    mask_ref, slot_ref, *refs,
+):
+    ins, refs = refs[:23], refs[23:]
+    outs, refs = refs[:7], refs[7:]
+    blk_ref, gp_ref, eg_ref, lg1_ref, lg2_ref, veg_ref, vlg_ref = outs
+    s = dict(zip(names, refs))
+    D, HF, PB, PA, KEYS, PL, T = sz.width, HEAD_FEATURES, sz.pb, sz.pa, sz.keys, sz.plane, sz.all
+    C, FS, W = sz.hidden, sz.share, sz.wide
+    d = lax.axis_index("dp")
+    m = lax.axis_index("mp")
+    last = sz.n_mp * HF
+    ssem, rsem = s["ssem"], s["rsem"]
+
+    def mpx(k):
+        if k == 0:
+            return m
+        if k == 1:
+            return m + 1 - 2 * lax.rem(m, 2)
+        if k == 2:
+            return lax.rem(m + 2, 4)
+        return 3 - m
+
+    def dpx(k):
+        z, x = d // 2, lax.rem(d, 2)
+        if k & 1:
+            x = 1 - x
+        kz = k >> 1
+        if kz == 1:
+            z = z + 1 - 2 * lax.rem(z, 2)
+        elif kz == 2:
+            z = lax.rem(z + 2, 4)
+        elif kz == 3:
+            z = 3 - z
+        return 2 * z + x
+
+    counter = [0]
+    pending = []
+
+    def take(n):
+        first = counter[0]
+        counter[0] += n
+        return first
+
+    def copy(src, dst, sem, dev):
+        return pltpu.make_async_remote_copy(
+            src_ref=src, dst_ref=dst, send_sem=ssem.at[sem], recv_sem=rsem.at[sem],
+            device_id=dev, device_id_type=pl.DeviceIdType.MESH,
+        )
+
+    def send(src, dst, sem, dev):
+        c = copy(src, dst, sem, dev)
+        c.start()
+        pending.append(c)
+
+    def arrived(ref, sem):
+        copy(ref, ref, sem, (d, m)).wait_recv()
+
+    opened = []
+
+    def handle(finish):
+        state = [False]
+
+        def once(*a):
+            if not state[0]:
+                state[0] = True
+                return finish(*a)
+
+        opened.append(once)
+        return once
+
+    def mp_start(buf):
+        base = take(3)
+        send(buf.at[m], buf.at[m], base, (d, mpx(1)))
+        send(buf.at[m], buf.at[m], base + 1, (d, mpx(2)))
+
+        def middle():
+            arrived(buf.at[mpx(2)], base + 1)
+            send(buf.at[mpx(2)], buf.at[mpx(2)], base + 2, (d, mpx(1)))
+
+        mid = handle(middle)
+
+        def finish():
+            mid()
+            arrived(buf.at[mpx(1)], base)
+            arrived(buf.at[mpx(3)], base + 2)
+
+        return handle(finish), mid
+
+    def dp_start(buf):
+        base = take(7)
+        for kz in (3, 2, 1):
+            send(buf.at[d], buf.at[d], base + kz, (dpx(2 * kz), m))
+        send(buf.at[d], buf.at[d], base, (dpx(1), m))
+
+        def finish(each=lambda k: None):
+            for kz in (1, 2, 3):
+                arrived(buf.at[dpx(2 * kz)], base + kz)
+                send(buf.at[dpx(2 * kz)], buf.at[dpx(2 * kz)], base + 3 + kz, (dpx(1), m))
+                each(2 * kz)
+            arrived(buf.at[dpx(1)], base)
+            each(1)
+            for kz in (1, 2, 3):
+                arrived(buf.at[dpx(2 * kz + 1)], base + 3 + kz)
+                each(2 * kz + 1)
+
+        return handle(finish)
+
+    def mp_scatter(block, dst, landed):
+        base = take(4)
+        for k in (2, 3, 1):
+            send(block(mpx(k)), dst(k), base + k, (d, mpx(k)))
+
+        def finish():
+            for k in (1, 2, 3):
+                arrived(landed(k), base + k)
+
+        return handle(finish)
+
+    def dp_scatter(block, dst, landed):
+        base = take(8)
+        for k in (6, 7, 4, 5, 2, 3, 1):
+            send(block(dpx(k)), dst(k), base + k, (dpx(k), m))
+
+        def finish():
+            for k in range(1, sz.n_dp):
+                arrived(landed(k), base + k)
+
+        return handle(finish)
+
+    def mp_sum(block, out, near, far):
+        base = take(3)
+        out[0] = block(mpx(1)).astype(BF)
+        send(out.at[0], near.at[0], base, (d, mpx(1)))
+        out[1] = block(mpx(3)).astype(BF)
+        send(out.at[1], near.at[1], base + 1, (d, mpx(1)))
+
+        def middle():
+            value = block(mpx(2))
+            arrived(near.at[1], base + 1)
+            out[2] = (value + near[1].astype(F32)).astype(BF)
+            send(out.at[2], far, base + 2, (d, mpx(2)))
+
+        mid = handle(middle)
+
+        def finish():
+            mid()
+            value = block(m)
+            arrived(near.at[0], base)
+            value = value + near[0].astype(F32)
+            arrived(far, base + 2)
+            return value + far[...].astype(F32)
+
+        return mid, handle(finish)
+
+    def dp_sum(chunk, near, out, far):
+        base = take(8)
+        for kz in (2, 3, 1, 0):
+            send(chunk(dpx(2 * kz + 1)), near.at[kz], base + kz, (dpx(1), m))
+
+        def middle():
+            for kz in (2, 3, 1):
+                value = chunk(dpx(2 * kz))[...].astype(F32)
+                arrived(near.at[kz], base + kz)
+                out[kz] = (value + near[kz].astype(F32)).astype(BF)
+                send(out.at[kz], far.at[kz], base + 4 + kz, (dpx(2 * kz), m))
+
+        mid = handle(middle)
+
+        def finish():
+            mid()
+            value = chunk(d)[...].astype(F32)
+            arrived(near.at[0], base)
+            value = value + near[0].astype(F32)
+            for kz in (1, 2, 3):
+                arrived(far.at[kz], base + 4 + kz)
+                value = value + far[kz].astype(F32)
+            return value
+
+        return mid, handle(finish)
+
+    def dp_total(src, near, parts):
+        base = take(4)
+        z = d // 2
+        send(src, near, base, (dpx(1), m))
+
+        def middle():
+            arrived(near, base)
+            parts[z] = src[...] + near[...]
+            for kz in (2, 3, 1):
+                send(parts.at[z], parts.at[z], base + kz, (dpx(2 * kz), m))
+
+        mid = handle(middle)
+
+        def finish():
+            mid()
+            for kz in (1, 2, 3):
+                arrived(parts.at[dpx(2 * kz) // 2], base + kz)
+            return (parts[0] + parts[1]) + (parts[2] + parts[3])
+
+        return mid, handle(finish)
+
+    peers = [(d, mpx(k)) for k in (1, 2, 3)] + [(dpx(k), m) for k in range(1, 8)]
+    bar = pltpu.get_barrier_semaphore()
+    for dev in peers:
+        pl.semaphore_signal(bar, inc=1, device_id=dev, device_id_type=pl.DeviceIdType.MESH)
+
+    order = (0, 1, 2, 3, 8, 7, 9, 10, 11, 12, 4, 5, 6, 21, 22, 13, 14, 15, 16, 17, 18, 19, 20)
+    loads = [None] * 23
+    for i in order:
+        dst = s["xt"].at[m] if i == 0 else s["in%d" % i]
+        loads[i] = Load(ins[i], dst, s["isem"].at[i])
+    (
+        pix_ref, cot_ref, ln1g_ref, ln1b_ref, wq_ref, bq_ref, wk_ref, wv_ref, bv_ref, wr_ref, br_ref,
+        lnrg_ref, lnrb_ref, wo_ref, bo_ref, ln2g_ref, ln2b_ref, w1_ref, b1_ref, wd_ref, bd_ref, w2_ref, b2_ref,
+    ) = loads
+
+    side = jnp.where(mask_ref[sz.cols - 1] > 0, FRAME, SIDE_SMALL)
+    tile = slot_ref[1, d]
+    tiles = [slot_ref[1, k] for k in range(sz.n_dp)]
+    above = sum(jnp.where(tiles[k] == tile - 1, k, 0) for k in range(sz.n_dp))
+    below = sum(jnp.where(tiles[k] == tile + 1, k, 0) for k in range(sz.n_dp))
+
+    def place(p, count):
+        a = sum(jnp.where(p >= PB * k, 1, 0) for k in range(1, count))
+        return a, p - PB * a
+
+    def token_mask(i, j):
+        p = iota((PL, 1), 0)
+        a, b = place(p, PA)
+        inside = (p < KEYS) & (sz.rows * tile + 2 * a + i < side) & (2 * b + j < side)
+        return jnp.where(inside, 1.0, 0.0)
+
+    def row_mask(i, j, a):
+        b = iota((PB, 1), 0)
+        row = sz.rows * tile + 2 * a + i
+        inside = (row >= 0) & (row < side) & (2 * b + j < side)
+        return jnp.where(inside, 1.0, 0.0)
+
+    def key_bias(p, tile_at):
+        a, b = place(p, PA)
+        usable = (p < KEYS) & (sz.rows * tile_at + 2 * a < side) & (2 * b < side)
+        return jnp.where(usable, 0.0, NEG)
+
+    def vec(ref):
+        return ref[...].reshape(1, ref.shape[0])
+
+    def own_part(row, size):
+        return sum(
+            jnp.where(m == h, 1.0, 0.0) * row[:, size * h : size * (h + 1)] for h in range(sz.n_mp)
+        )
+
+    def plane_rows(ref, start):
+        return ref[pl.ds(pl.multiple_of(start, 16), PL), :]
+
+    def plane(p):
+        return slice(PL * p, PL * (p + 1))
+
+    lanes3 = (s["t0"], s["t1"], s["t2"])
+
+    def to_planes(rows_of):
+        for n, ref in enumerate(lanes3):
+            ref[...] = rows_of(LANES * n, min(D, LANES * (n + 1))).astype(F32).T
+        for i in range(2):
+            for j in range(2):
+                parts = []
+                for ref in lanes3:
+                    rows = [
+                        ref[pl.ds((2 * a + i) * sz.cols + j, PB, stride=2), :] for a in range(PA)
+                    ] + [jnp.zeros((PL - KEYS, ref.shape[1]), F32)]
+                    parts.append(jnp.concatenate(rows, axis=0))
+                yield i, j, jnp.concatenate(parts, axis=1)
+
+    def to_queries(planes):
+        n = planes[0].shape[1]
+        edge = [v for p in planes for v in (p[0:PB], p[KEYS - PB : KEYS])]
+        inner = [p[PB : KEYS - PB] for p in planes]
+        return jnp.concatenate(
+            edge + [jnp.zeros((sz.edge_q - sz.edge, n), F32)]
+            + inner + [jnp.zeros((sz.inner_q - sz.inner, n), F32)],
+            axis=0,
+        )
+
+    def from_queries(edge, inner, p):
+        n = KEYS - 2 * PB
+        return jnp.concatenate(
+            [
+                edge[2 * PB * p : 2 * PB * p + PB], inner[n * p : n * (p + 1)],
+                edge[2 * PB * p + PB : 2 * PB * (p + 1)], jnp.zeros((PL - KEYS, edge.shape[1]), F32),
+            ],
+            axis=0,
+        )
+
+    xt, dfm = s["xt"], s["dfm"]
+    pl.semaphore_wait(bar, len(peers))
+    pix_ref.ready()
+    x_at, x_mid = mp_start(xt)
+
+    for i, j, value in to_planes(lambda lo, hi: cot_ref[lo:hi, :]):
+        dfm[plane(2 * i + j), :] = (value * token_mask(i, j)).astype(BF)
+    dyh, dyh_g = s["dyh"], s["dyh_g"]
+    dyh[d, :, :D] = dfm[pl.ds(pl.multiple_of(PL * m + (KEYS - PB) * (m // 2), 16), 48), :]
+    dyh[d, :, D:] = jnp.zeros((48, W - D), BF)
+    dy_at = dp_start(dyh)
+    x_mid()
+
+    r2, c2 = iota((D, LANES), 0), iota((D, LANES), 1)
+    own_lo = hot((c2 < HF) & (r2 == HF * m + c2))
+    own_hi = hot((c2 >= HF) & (r2 == HF * m + c2 - HF))
+    last_lo = hot((c2 < HF) & (r2 == last + c2))
+    last_hi = hot((c2 >= HF) & (r2 == last + c2 - HF))
+    wq, wk, wv = wq_ref[...], wk_ref[...], wv_ref[...]
+    wq2 = nn(wq, own_lo + last_hi).astype(BF)
+    wkv = (nn(wk, own_lo) + nn(wv, own_hi)).astype(BF)
+    wkv5 = (nn(wk, last_lo) + nn(wv, last_hi)).astype(BF)
+    bq, bv = vec(bq_ref), vec(bv_ref)
+    bq2 = jnp.concatenate([own_part(bq, HF), bq[:, last:]], axis=1)
+    nil = jnp.zeros((1, HF), F32)
+    bkv = jnp.concatenate([nil, own_part(bv, HF)], axis=1)
+    bkv5 = jnp.concatenate([nil, bv[:, last:]], axis=1)
+    wr_t = s["wr_t"]
+    wr_t[...] = wr_ref[...].T
+
+    xm_r, n1_r = s["xm_r"], s["n1_r"]
+    x_at()
+    x_all = xt[...].reshape(D, sz.tokens)
+    for i, j, value in to_planes(lambda lo, hi: x_all[lo:hi, :]):
+        xm = value * token_mask(i, j)
+        xm_r[plane(2 * i + j), :] = xm.astype(BF)
+        xhat, _ = spread(xm)
+        n1_r[plane(2 * i + j), :] = (xhat * vec(ln1g_ref) + vec(ln1b_ref)).astype(BF)
+
+    kva, xr_r = s["kva"], s["xr_r"]
+    red = sum(nn(n1_r[plane(p), :], wr_t[D * p : D * (p + 1), :]) for p in range(4)) + vec(br_ref)
+    xhr, rsr = spread(red)
+    s["xhr_r"][...] = xhr
+    s["rsr_r"][...] = jnp.broadcast_to(rsr, (PL, LANES))
+    xr_r[...] = (xhr * vec(lnrg_ref) + vec(lnrb_ref)).astype(BF)
+    kva[d, 0:PL, :] = (nn(xr_r[...], wkv) + bkv).astype(BF)
+    quarter_rows = pl.ds(pl.multiple_of(sz.step * m, 16), sz.quarter)
+    kva[d, PL:, :] = (nn(xr_r[quarter_rows, :], wkv5) + bkv5).astype(BF)
+    kv_at = dp_start(kva)
+
+    qa_r, qb_r = s["qa_r"], s["qb_r"]
+    Q = sz.queries
+    q2 = (nn(n1_r[...], wq2) + bq2).astype(BF).astype(F32) * HF ** (-0.5)
+    q2t = to_queries([q2[plane(p)] for p in range(4)]).T
+    half = jnp.zeros((HF, Q), F32)
+    qa_r[...] = jnp.concatenate([q2t[0:HF], half], axis=0).astype(BF)
+    qb_r[...] = jnp.concatenate([q2t[HF:], half], axis=0).astype(BF)
+
+    dy_at()
+    dyh_g[m] = dyh[jnp.where(m >= 2, above, below)]
+    dyg_at, dyg_mid = mp_start(dyh_g)
+
+    dgx, dzx = s["dgx"], s["dzx"]
+    w2 = w2_ref[...]
+    dgx[...] = jnp.zeros_like(dgx)
+    dzx[...] = jnp.zeros_like(dzx)
+    for p in range(4):
+        dgx[p, sz.top : sz.top + PL, :] = nt(dfm[plane(p), :], w2).astype(BF).astype(F32)
+    wo = wo_ref[...]
+    wo_cat = jnp.concatenate(
+        [b for h in range(4) for b in (wo[HF * h : HF * (h + 1)], wo[last:])], axis=0
+    )
+    limit5 = jnp.where(m == sz.n_mp - 1, KEYS - sz.step * m, sz.step)
+    pk = iota((sz.quarter, 1), 0)
+    bias5 = jnp.concatenate(
+        [
+            jnp.where(pk < limit5, key_bias(pk + sz.step * m, tiles[k]), NEG)
+            for k in range(sz.n_dp)
+        ],
+        axis=0,
+    )
+    dyg_mid()
+    kv_at()
+
+    e5buf, ebuf, sbuf, row_r, ot_r = s["e5buf"], s["ebuf"], s["sbuf"], s["row_r"], s["ot_r"]
+    kv5 = kva[:, PL:, :].reshape(sz.n_dp * sz.quarter, LANES)
+    chunks = ((0, sz.edge_q, s["lse_a"], s["og_a"]), (sz.edge_q, sz.queries, s["lse_b"], s["og_b"]))
+    fives = []
+    for lo, hi, lse_r, _ in chunks:
+        s5 = nn(kv5, qb_r[:, lo:hi]) + bias5
+        m5 = jnp.max(s5, axis=0, keepdims=True)
+        e5 = jnp.exp(s5 - m5).astype(BF)
+        l5 = rowsum(e5.astype(F32))
+        e5buf[:, :, lo:hi] = e5.reshape(sz.n_dp, sz.quarter, hi - lo)
+        lse_r[m] = jnp.broadcast_to(m5 + jnp.log(l5), (8, hi - lo))
+        at = mp_scatter(
+            lambda h, r=lse_r: r.at[m], lambda k, r=lse_r: r.at[m], lambda k, r=lse_r: r.at[mpx(k)]
+        )
+        fives.append((m5, tn(kv5, e5), at))
+
+    pk = iota((PL, 1), 0)
+    ogs = []
+    for (lo, hi, lse_r, og), (m5, o5t, lse_at) in zip(chunks, fives):
+
+        def score_step(j, top, lo=lo, hi=hi):
+            v = nn(kva[j, 0:PL, :], qa_r[:, lo:hi]) + key_bias(pk, slot_ref[1, j])
+            sbuf[j, :, lo:hi] = v
+            return jnp.maximum(top, jnp.max(v, axis=0, keepdims=True))
+
+        top = lax.fori_loop(0, sz.n_dp, score_step, jnp.full((1, hi - lo), NEG, F32))
+
+        def exp_step(j, total, lo=lo, hi=hi, top=top):
+            e = jnp.exp(sbuf[j, :, lo:hi] - top).astype(BF)
+            ebuf[j, :, lo:hi] = e
+            return total + rowsum(e.astype(F32))
+
+        total = lax.fori_loop(0, sz.n_dp, exp_step, jnp.zeros((1, hi - lo), F32))
+        ot = tn(
+            kva[:, 0:PL, :].reshape(sz.n_dp * PL, LANES),
+            ebuf[:, :, lo:hi].reshape(sz.n_dp * PL, hi - lo),
+        )
+        inv = 1.0 / total
+        lse_at()
+        lses = [lse_r[h][0:1] for h in range(4)]
+        lmax = jnp.maximum(jnp.maximum(lses[0], lses[1]), jnp.maximum(lses[2], lses[3]))
+        lse5 = lmax + jnp.log(sum(jnp.exp(v - lmax) for v in lses))
+        f5 = jnp.exp(m5 - lse5)
+        row_r[0:1, lo:hi] = inv
+        row_r[1:2, lo:hi] = f5
+        o2t = jnp.concatenate([ot[HF:] * inv, o5t[HF:] * f5], axis=0)
+        ot_r[:, lo:hi] = o2t
+        og[m] = o2t.T[0 : og.shape[1]].astype(BF)
+        ogs.append(mp_start(og))
+
+    og_a, og_b = s["og_a"], s["og_b"]
+    hal, hal_g, h1_r, n2_r = s["hal"], s["hal_g"], s["h1_r"], s["n2_r"]
+
+    def second_norm(h1):
+        xhat, _ = spread(h1)
+        return (xhat * vec(ln2g_ref) + vec(ln2b_ref)).astype(BF)
+
+    ogs[0][0]()
+    border = pl.ds(pl.multiple_of(2 * PB * m, 16), 2 * PB)
+    oc = jnp.concatenate([og_a[h, border, :] for h in range(4)], axis=1)
+    xmine = plane_rows(xm_r, PL * m).astype(F32)
+    xmine = jnp.concatenate([xmine[0:PB], xmine[KEYS - PB : KEYS]], axis=0)
+    im, jm = m // 2, lax.rem(m, 2)
+    emask = jnp.concatenate([row_mask(im, jm, 0), row_mask(im, jm, PA - 1)], axis=0)
+    hal[d, :, :D] = second_norm(xmine + emask * (nn(oc, wo_cat) + vec(bo_ref)))
+    hal[d, :, D:] = jnp.zeros((2 * PB, W - D), BF)
+    hal_at = dp_start(hal)
+
+    dyg_at()
+    for p in range(4):
+        i, j = p // 2, p % 2
+        start = sz.top - PB if i == 1 else sz.top + KEYS
+        rows = dyh_g[p][:, :D].astype(F32)[0:PB] * row_mask(i, j, -1 if i == 1 else PA)
+        dgx[p, start : start + PB, :] = nt(rows.astype(BF), w2).astype(BF).astype(F32)
+    for k in range(sz.n_dp):
+        e5buf[k] = (e5buf[k].astype(F32) * row_r[1:2, :]).astype(BF)
+
+    ogs[1][0]()
+    mixed = []
+    for og in (og_a, og_b):
+        oc = jnp.concatenate([og[h] for h in range(4)], axis=1)
+        mixed.append(nn(oc, wo_cat) + vec(bo_ref))
+    w1, b1 = w1_ref[...], vec(b1_ref)
+
+    def hidden(rows, mask):
+        return ((nn(rows, w1) + b1) * mask).astype(BF).astype(F32)
+
+    ux, ul, ur, dzl, dzr = s["ux"], s["ul"], s["ur"], s["dzl"], s["dzr"]
+    for p in range(4):
+        mask = token_mask(p // 2, p % 2)
+        h1 = xm_r[plane(p), :].astype(F32) + mask * from_queries(mixed[0], mixed[1], p)
+        h1_r[plane(p), :] = h1
+        n2_r[plane(p), :] = second_norm(h1)
+        ux[p, 0 : sz.top, :] = jnp.zeros((sz.top, C), F32)
+        ux[p, sz.top : sz.top + PL, :] = hidden(n2_r[plane(p), :], mask)
+    ogp = s["ogp"]
+    for p in range(4):
+        ogp[plane(p), :] = from_queries(og_a[m].astype(F32), og_b[m].astype(F32), p).astype(BF)
+    w2p = s["w2p"]
+    rt, ct = iota((D, 4 * LANES), 0), iota((D, 4 * LANES), 1)
+    lane4, head4 = ct & (LANES - 1), ct >> 7
+    place_out = hot((lane4 < FS) & (rt == FS * head4 + lane4))
+    w2_wide = nn(w2, place_out).astype(BF)
+    for h in range(4):
+        w2p[h] = w2_wide[:, LANES * h : LANES * (h + 1)]
+    hal_at()
+    up_rows = hal[above].astype(F32)[PB:]
+    down_rows = hal[below].astype(F32)[0:PB]
+    hal_g[m] = jnp.concatenate([up_rows, down_rows], axis=0).astype(BF)
+    halg_at, _ = mp_start(hal_g)
+    g_r, du_r = s["g_r"], s["du_r"]
+    g_r[...] = jnp.zeros_like(g_r)
+    du_r[...] = jnp.zeros_like(du_r)
+    halg_at()
+    for p in range(4):
+        i, j = p // 2, p % 2
+        mask = jnp.concatenate([row_mask(i, j, -1), row_mask(i, j, PA)], axis=0)
+        u = hidden(hal_g[p][:, :D], mask)
+        ux[p, sz.top - PB : sz.top, :] = u[0:PB]
+        ux[p, sz.top + KEYS : sz.top + KEYS + PB, :] = u[PB:]
+
+    _, be = place(iota((sz.ext, 1), 0) + (PB - 8), PA + 3)
+    wd_ref, bd_row = wd_ref.ready(), vec(bd_ref)
+
+    def shifted(src, left, right):
+        for i in range(2):
+            left[i] = jnp.where(be == 0, 0.0, pltpu.roll(src[2 * i + 1], 1, 0))
+            right[i] = jnp.where(be == PB - 1, 0.0, pltpu.roll(src[2 * i], sz.ext - 1, 0))
+
+    def source(refs, i, j, di, dj, start):
+        base, left, right = refs
+        i2, up = (i + di) % 2, (i + di) // 2
+        j2, across = (j + dj) % 2, (j + dj) // 2
+        at = pl.ds(pl.multiple_of(start + PB * up, 8), PB)
+        if across < 0:
+            return left[i2, at, :]
+        if across > 0:
+            return right[i2, at, :]
+        return base[2 * i2 + j2, at, :]
+
+    TAPS = [(di, dj) for di in (-1, 0, 1) for dj in (-1, 0, 1)]
+    shifted(ux, ul, ur)
+
+    def activation(i, j, start):
+        p = 2 * i + j
+        z = bd_row + sum(
+            wd_ref[t : t + 1, :] * source((ux, ul, ur), i, j, di, dj, start)
+            for t, (di, dj) in enumerate(TAPS)
+        )
+        phi = 0.5 * (1.0 + lax.erf(z * 0.7071067811865476))
+        dens = jnp.exp(-0.5 * z * z) * 0.3989422804014327
+        dz = dgx[p, pl.ds(pl.multiple_of(start, 8), PB), :] * (phi + z * dens)
+        dzx[p, pl.ds(pl.multiple_of(start, 8), PB), :] = dz
+        return z * phi, dz
+
+    def fold(value):
+        return jnp.sum(value.reshape(PB // 8, 8, C), axis=0)
+
+    ve_s, vl_s = s["ve_s"], s["vl_s"]
+    sums = [jnp.zeros((8, C), F32) for _ in range(10)]
+    for i in range(2):
+        for j in range(2):
+            p = 2 * i + j
+            activation(i, j, sz.top - PB if i == 1 else sz.top + KEYS)
+
+            def forward_step(a, acc, i=i, j=j, p=p):
+                start = sz.top + PB * a
+                act, dz = activation(i, j, start)
+                g_r[p, pl.ds(pl.multiple_of(PB * a, 8), PB), :] = act
+                new = [
+                    acc[t] + fold(dz * source((ux, ul, ur), i, j, di, dj, start))
+                    for t, (di, dj) in enumerate(TAPS)
+                ]
+                return tuple(new) + (acc[9] + fold(dz),)
+
+            sums = lax.fori_loop(0, PA, forward_step, tuple(sums))
+    for t in range(10):
+        ve_s[t : t + 1, :C] = rowsum(sums[t])
+    shifted(dzx, dzl, dzr)
+    dub = s["dub"]
+    for i in range(2):
+        for j in range(2):
+            p = 2 * i + j
+
+            def backward_step(a, carry, i=i, j=j, p=p):
+                start = sz.top + PB * a
+                du_r[p, pl.ds(pl.multiple_of(PB * a, 8), PB), :] = sum(
+                    wd_ref[t : t + 1, :] * source((dzx, dzl, dzr), i, j, -di, -dj, start)
+                    for t, (di, dj) in enumerate(TAPS)
+                )
+                return carry
+
+            lax.fori_loop(0, PA, backward_step, 0)
+            dub[p] = (du_r[p].astype(BF).astype(F32) * token_mask(i, j)).astype(BF)
+    dn2_mid, dn2_at = mp_sum(lambda h: nt(dub[h], w1), s["dn2_s"], s["dn2_n"], s["dn2_f"])
+    dn2_mid()
+
+    e_s = s["e_s"]
+    gb = g_r[...].reshape(T, C).astype(BF)
+    du_all = dub[...].reshape(T, C)
+    e_s[0:D, :C] = tn(n2_r[...], du_all).astype(BF)
+    e_s[D:, :D] = tn(gb, dfm[...]).astype(BF)
+    e_at = dp_scatter(
+        lambda j: e_s.at[pl.ds(pl.multiple_of(sz.echunk * j, 16), sz.echunk)],
+        lambda k: s["e_r"].at[k - 1],
+        lambda k: s["e_r"].at[k - 1],
+    )
+    ve_s[10:11, :C] = rowsum(du_all.astype(F32))
+
+    xhat2, rstd2 = spread(plane_rows(h1_r, PL * m))
+    dfp = plane_rows(dfm, PL * m).astype(F32)
+    ve_s[11:12, :D] = rowsum(dfp)
+    dn2 = dn2_at()
+    dh1 = dfp + norm_back(dn2, vec(ln2g_ref), xhat2, rstd2)
+    s["dh1_r"][...] = dh1
+    dab = dh1.astype(BF)
+    docat = nt(dab, wo_cat).astype(BF)
+    dos, do_all, dabg = s["dos"], s["do_all"], s["dabg"]
+    for h in range(4):
+        dos[h] = docat[:, LANES * h : LANES * (h + 1)]
+    do_at = mp_scatter(lambda h: dos.at[h], lambda k: do_all.at[m], lambda k: do_all.at[mpx(k)])
+    do_all[m] = dos[m]
+    dabg[m, :, :D] = dab
+    dab_at, dab_mid = mp_start(dabg)
+    ve_s[12:13, :D] = rowsum(dh1)
+    ve_s[13:14, :D] = rowsum(dn2 * xhat2)
+    ve_s[14:15, :D] = rowsum(dn2)
+    ve_s[15:16, :] = jnp.zeros((1, W), F32)
+    ve_mid, ve_at = dp_total(ve_s, s["ve_n"], s["ve_p"])
+
+    ff_mid, ff_at = mp_sum(lambda h: nn(gb, w2p[h]), s["ff_s"], s["ff_n"], s["ff_f"])
+
+    do_at()
+    dr_r = s["dr_r"]
+    dot_t = to_queries([do_all[p].astype(F32) for p in range(4)]).T
+    dr_r[m] = jnp.broadcast_to(rowsum(dot_t[HF:] * ot_r[HF:, :]), (8, Q))
+    dr_at = mp_scatter(lambda h: dr_r.at[m], lambda k: dr_r.at[m], lambda k: dr_r.at[mpx(k)])
+    da_own = (dot_t[0:HF] * row_r[0:1, :]).astype(BF)
+    drow = rowsum(da_own.astype(F32) * ot_r[0:HF, :])
+    da_t = jnp.concatenate([half.astype(BF), da_own], axis=0)
+    db_t = jnp.concatenate([half, dot_t[HF:]], axis=0).astype(BF)
+    dqt, dqt5 = s["dqt"], s["dqt5"]
+    dqt[...] = jnp.zeros_like(dqt)
+    dqt5[...] = jnp.zeros_like(dqt5)
+    ff_mid()
+    dr_at()
+    drow5 = sum(dr_r[h][0:1] for h in range(4))
+
+    def key_block(j):
+        kv = kva[j, 0:PL, :]
+        e = ebuf[j]
+        ds = (e.astype(F32) * (nn(kv, da_t) - drow)).astype(BF)
+        own = nt(ds, qa_r[...]) + nt(e, da_t)
+        dqt[...] += tn(kv, ds)
+        kv = kva[j, PL:, :]
+        e = e5buf[j]
+        ds = (e.astype(F32) * (nn(kv, db_t) - drow5)).astype(BF)
+        dqt5[...] += tn(kv, ds)
+        return jnp.concatenate([own, nt(ds, qb_r[...]) + nt(e, db_t)], axis=0)
+
+    dk_x, dk_n, dk_o, dk_f = s["dk_x"], s["dk_n"], s["dk_o"], s["dk_f"]
+    dk_at = take(8)
+    for kz in (2, 3, 1, 0):
+        dk_x[kz] = key_block(dpx(2 * kz + 1)).astype(BF)
+        send(dk_x.at[kz], dk_n.at[kz], dk_at + kz, (dpx(1), m))
+    for kz in (2, 3, 1):
+        value = key_block(dpx(2 * kz))
+        arrived(dk_n.at[kz], dk_at + kz)
+        dk_o[kz] = (value + dk_n[kz].astype(F32)).astype(BF)
+        send(dk_o.at[kz], dk_f.at[kz], dk_at + 4 + kz, (dpx(2 * kz), m))
+    dkv = key_block(d)
+
+    def dk_finish():
+        arrived(dk_n.at[0], dk_at)
+        total = dkv + dk_n[0].astype(F32)
+        for kz in (1, 2, 3):
+            arrived(dk_f.at[kz], dk_at + 4 + kz)
+            total = total + dk_f[kz].astype(F32)
+        return total
+
+    dk_fin = handle(dk_finish)
+
+    dq2 = (jnp.concatenate([dqt[0:HF], dqt5[0:HF]], axis=0) * HF ** (-0.5)).T
+    dqs, dq_all = s["dqs"], s["dq_all"]
+    for h in range(4):
+        dqs[h] = from_queries(dq2[: sz.edge_q], dq2[sz.edge_q :], h).astype(BF)
+    dq_at = mp_scatter(lambda h: dqs.at[h], lambda k: dq_all.at[m], lambda k: dq_all.at[mpx(k)])
+    dq_all[m] = dqs[m]
+    ve_mid()
+    l1_s, l2_s = s["l1_s"], s["l2_s"]
+    dqp = dqs[...].reshape(T, LANES)
+    l1_s[0:D, 0:LANES] = tn(n1_r[...], dqp).astype(BF)
+    vl_s[...] = jnp.zeros_like(vl_s)
+    vl_s[5:6, 0:LANES] = rowsum(dqp.astype(F32))
+    dab_at()
+    gwo = tn(ogp[...], dabg[...].reshape(T, W)[:, :D]).astype(BF)
+    l1_s[D:, :D] = gwo[0:HF]
+    l2_s[D:, :D] = gwo[HF:]
+
+    ff = ff_at()
+    sel = hot((c2 < FS) & (r2 == FS * m + c2))
+    b2q = jnp.concatenate(
+        [own_part(vec(b2_ref), FS), jnp.zeros((1, LANES - FS), F32)], axis=1
+    )
+    for p in range(4):
+        h1 = h1_r[plane(p), :]
+        hi = h1.astype(BF)
+        h1q = nn(hi, sel) + nn((h1 - hi.astype(F32)).astype(BF), sel)
+        blk_ref[plane(p), :] = h1q + token_mask(p // 2, p % 2) * (ff[plane(p)] + b2q)
+
+    e_at()
+    mine = e_s[pl.ds(pl.multiple_of(sz.echunk * d, 16), sz.echunk), :].astype(F32)
+    eg_ref[d] = (mine + sum(s["e_r"][k].astype(F32) for k in range(sz.n_dp - 1))).astype(BF)
+
+    dkvb = dk_fin().astype(BF)
+    dkvg = s["dkvg"]
+    dkvg[m] = dkvb
+    dkv_at, dkv_mid = mp_start(dkvg)
+    l1_s[0:D, LANES : 2 * LANES] = tn(xr_r[...], dkvb[0:PL]).astype(BF)
+    l1_s[0:D, 2 * LANES :] = tn(xr_r[quarter_rows, :], dkvb[PL:]).astype(BF)
+
+    def lchunk(ref):
+        return lambda j: ref.at[pl.ds(pl.multiple_of(sz.lchunk * j, 16), sz.lchunk)]
+
+    l1_mid, l1_at = dp_sum(lchunk(l1_s), s["l1_n"], s["l1_o"], s["l1_f"])
+    vl_s[6:7, 0:LANES] = jnp.concatenate(
+        [rowsum(dkvb[0:PL].astype(F32))[:, HF:], rowsum(dkvb[PL:].astype(F32))[:, HF:]], axis=1
+    )
+    rk, ck = iota((D, 5 * LANES), 0), iota((D, 5 * LANES), 1)
+    lane5, head5 = ck & (LANES - 1), ck >> 7
+    w_all = (
+        nn(wk, hot((lane5 < HF) & (rk == HF * head5 + lane5)))
+        + nn(wv, hot((lane5 >= HF) & (rk == HF * head5 + lane5 - HF)))
+    ).astype(BF)
+    wq_cat = nn(
+        wq, hot(rt == jnp.where(lane4 < HF, HF * head4 + lane4, last + lane4 - HF))
+    ).astype(BF)
+    dq_at()
+    dq_cat = jnp.concatenate([dq_all[h] for h in range(4)], axis=1)
+    dn1 = nt(dq_cat, wq_cat)
+    xhat1, rstd1 = spread(plane_rows(xm_r, PL * m).astype(F32))
+    dkv_at()
+    rest = jnp.concatenate(
+        [dkvg[h, PL : PL + sz.step, :] for h in range(3)] + [dkvg[3, PL:, :]], axis=0
+    )
+    dkv_all = jnp.concatenate([dkvg[h, 0:PL, :] for h in range(4)] + [rest], axis=1)
+    dxr = nt(dkv_all, w_all)
+    xhr = s["xhr_r"][...]
+    drb = norm_back(dxr, vec(lnrg_ref), xhr, s["rsr_r"][:, 0:1]).astype(BF)
+    l2_s[0:D, :D] = tn(drb, plane_rows(n1_r, PL * m)).astype(BF)
+    l1_mid()
+    l2_mid, l2_at = dp_sum(lchunk(l2_s), s["l2_n"], s["l2_o"], s["l2_f"])
+    vl_s[2:3, :D] = rowsum(dxr * xhr)
+    vl_s[3:4, :D] = rowsum(dxr)
+    vl_s[4:5, :D] = rowsum(drb.astype(F32))
+
+    wr_m = wr_t[pl.ds(pl.multiple_of(D * m, 16), D), :]
+    dn1 = dn1 + nt(drb, wr_m)
+    vl_s[0:1, :D] = rowsum(dn1 * xhat1)
+    vl_s[1:2, :D] = rowsum(dn1)
+    vl_mid, vl_at = dp_total(vl_s, s["vl_n"], s["vl_p"])
+    dxm = norm_back(dn1, vec(ln1g_ref), xhat1, rstd1)
+    gp = (token_mask(im, jm) * (s["dh1_r"][...] + dxm)).astype(BF)
+    gpf = nn(gp, place_out).astype(BF)
+    gps = s["gps"]
+    for h in range(4):
+        gps[h] = gpf[:, LANES * h : LANES * (h + 1)]
+    gp_at = mp_scatter(lambda h: gps.at[h], lambda k: gp_ref.at[m], lambda k: gp_ref.at[mpx(k)])
+    gp_ref[m] = gps[m]
+
+    def gather(buf):
+        own = buf.at[m]
+        near = dp_start(own)
+        base = take(3 * sz.n_dp)
+
+        def across(k):
+            j = dpx(k)
+            send(buf.at[m, j], buf.at[m, j], base + 3 * k, (d, mpx(1)))
+            send(buf.at[m, j], buf.at[m, j], base + 3 * k + 1, (d, mpx(2)))
+
+        across(0)
+        seq = (0, 2, 4, 6, 1, 3, 5, 7)
+
+        def middle():
+            for k in seq:
+                j = dpx(k)
+                arrived(buf.at[mpx(2), j], base + 3 * k + 1)
+                send(buf.at[mpx(2), j], buf.at[mpx(2), j], base + 3 * k + 2, (d, mpx(1)))
+
+        mid = handle(middle)
+
+        def finish():
+            near(across)
+            mid()
+            for k in seq:
+                arrived(buf.at[mpx(1), dpx(k)], base + 3 * k)
+                arrived(buf.at[mpx(3), dpx(k)], base + 3 * k + 2)
+
+        return lambda: near(across), handle(finish)
+
+    lg1_ref[m, d] = l1_at().astype(BF)
+    lg1_near, lg1_at = gather(lg1_ref)
+    l2_mid()
+    vl_mid()
+    eg_at = dp_start(eg_ref)
+    veg_ref[m] = ve_at()
+    veg_at, _ = mp_start(veg_ref)
+    lg1_near()
+    lg2_ref[m, d] = l2_at().astype(BF)
+    lg2_near, lg2_at = gather(lg2_ref)
+    vlg_ref[m] = vl_at()
+    vlg_at, _ = mp_start(vlg_ref)
+    lg2_near()
+    eg_at()
+    gp_at()
+    veg_at()
+    lg1_at()
+    vlg_at()
+    lg2_at()
+    for c in pending:
+        c.wait_send()
+
+
+def unpack_body(
+    sz, blk_ref, gp_ref, eg_ref, lg1_ref, lg2_ref, veg_ref, vlg_ref,
+    out_ref, gpix_ref, ln1g_ref, ln1b_ref, gwq_ref, gbq_ref, gwk_ref, gwv_ref, gbv_ref, gwr_ref, gbr_ref,
+    lnrg_ref, lnrb_ref, gwo_ref, gbo_ref, ln2g_ref, ln2b_ref, gw1_ref, gb1_ref, gwd_ref, gbd_ref,
+    gw2_ref, gb2_ref, out32, gp32,
+):
+    D, HF, PB, PA, PL = sz.width, HEAD_FEATURES, sz.pb, sz.pa, sz.plane
+    C, FS = sz.hidden, sz.share
+    m = lax.axis_index("mp")
+    for i in range(2):
+        for j in range(2):
+            p = 2 * i + j
+            for a in range(PA):
+                at = pl.ds((2 * a + i) * sz.cols + j, PB, stride=2)
+                out32[at, :] = blk_ref[PL * p + PB * a : PL * p + PB * (a + 1), 0:FS]
+                gp32[at, :] = gp_ref[p].astype(F32)[PB * a : PB * (a + 1), 0:FS]
+    out_ref[...] = out32[...].T.astype(BF)
+    gpix_ref[...] = gp32[...].T
+
+    lg1 = [lg1_ref[h].reshape(sz.lrows, sz.wide) for h in range(4)]
+    lg2 = [lg2_ref[h].reshape(sz.lrows, sz.wide) for h in range(4)]
+
+    def heads(first, tail):
+        parts = [lg1[h][0:D, first : first + HF].astype(F32) for h in range(4)]
+        parts.append(sum(lg1[h][0:D, tail : tail + HF].astype(F32) for h in range(4)))
+        return jnp.concatenate(parts, axis=1)
+
+    gwq_ref[...] = heads(0, HF)
+    gwk_ref[...] = heads(LANES, 2 * LANES)
+    gwv_ref[...] = heads(LANES + HF, 2 * LANES + HF)
+    gwr_ref[...] = jnp.concatenate([lg2[h][0:D, :D].astype(F32) for h in range(4)], axis=1)
+    for h in range(4):
+        gwo_ref[HF * h : HF * (h + 1), :] = lg1[h][D:, :D].astype(F32)
+    gwo_ref[HF * 4 :, :] = sum(lg2[h][D:, :D].astype(F32) for h in range(4))
+    eg = eg_ref[...].reshape(D + C, sz.wide)
+    gw1_ref[...] = eg[0:D, :C].astype(F32)
+    gw2_ref[...] = eg[D:, :D].astype(F32)
+
+    def row(value):
+        return value.reshape(value.shape[1])
+
+    ve = veg_ref[m]
+    gwd_ref[...] = ve[0:9, :C]
+    gbd_ref[...] = row(ve[9:10, :C])
+    gb1_ref[...] = row(ve[10:11, :C])
+    vs = sum(veg_ref[h] for h in range(4))
+    gb2_ref[...] = row(vs[11:12, :D])
+    gbo_ref[...] = row(vs[12:13, :D])
+    ln2g_ref[...] = row(vs[13:14, :D])
+    ln2b_ref[...] = row(vs[14:15, :D])
+    vl = sum(vlg_ref[h] for h in range(4))
+    ln1g_ref[...] = row(vl[0:1, :D])
+    ln1b_ref[...] = row(vl[1:2, :D])
+    lnrg_ref[...] = row(vlg_ref[0][2:3, :D])
+    lnrb_ref[...] = row(vlg_ref[0][3:4, :D])
+    gbr_ref[...] = row(vlg_ref[0][4:5, :D])
+
+    def head_row(r):
+        parts = [vlg_ref[h][r : r + 1, 0:HF] for h in range(4)] + [vl[r : r + 1, HF : 2 * HF]]
+        return row(jnp.concatenate(parts, axis=1))
+
+    gbq_ref[...] = head_row(5)
+    gbv_ref[...] = head_row(6)
+
+
+def on_device_fused(*args):
+    pixels_in, cotangent, pixel_mask, tile_slot = args[:4]
+    w_fc1 = args[19]
+    sz = Sizes(
+        lax.axis_size("dp"), lax.axis_size("mp"), pixels_in.shape[0], cotangent.shape[1], w_fc1.shape[1]
+    )
+    D, C, PL, T, W, LN, HF = sz.width, sz.hidden, sz.plane, sz.all, sz.wide, LANES, HEAD_FEATURES
+    Q, N, PB = sz.queries, sz.n_dp, sz.pb
+    sm = pl.BlockSpec(memory_space=pltpu.SMEM)
+    vm = pl.BlockSpec(memory_space=pltpu.VMEM)
+    hbm = pl.BlockSpec(memory_space=pl.ANY)
+    S = jax.ShapeDtypeStruct
+    ins = [pixels_in.T, cotangent.T, *args[4:11], args[11].T, *args[12:]]
+    mids = [
+        S((T, LN), F32), S((4, PL, LN), BF), S((N, sz.echunk, W), BF), S((4, N, sz.lchunk, W), BF),
+        S((4, N, sz.lchunk, W), BF), S((4, 16, W), F32), S((4, 8, W), F32),
+    ]
+    shapes = {
+        BF: dict(
+            xt=(4, sz.share, sz.tokens), dfm=(T, D), dyh=(N, 48, W), dyh_g=(4, 48, W), xm_r=(T, D), n1_r=(T, D),
+            xr_r=(PL, D), kva=(N, sz.kvrows, LN), qa_r=(LN, Q), qb_r=(LN, Q), ebuf=(N, PL, Q),
+            e5buf=(N, sz.quarter, Q), og_a=(4, sz.edge, LN), og_b=(4, sz.inner, LN), n2_r=(T, D),
+            hal=(N, 2 * PB, W), hal_g=(4, 2 * PB, W), dub=(4, PL, C), dn2_s=(3, PL, D), dn2_n=(2, PL, D),
+            dn2_f=(PL, D), dos=(4, PL, LN), do_all=(4, PL, LN), dabg=(4, PL, W), ff_s=(3, T, LN), ff_n=(2, T, LN),
+            ff_f=(T, LN), dk_x=(4, sz.kvrows, LN), dk_n=(4, sz.kvrows, LN), dk_o=(4, sz.kvrows, LN),
+            dk_f=(4, sz.kvrows, LN), dkvg=(4, sz.kvrows, LN), dqs=(4, PL, LN), dq_all=(4, PL, LN),
+            e_s=(D + C, W), e_r=(N - 1, sz.echunk, W), l1_s=(sz.lrows, W), l1_n=(4, sz.lchunk, W),
+            l1_o=(4, sz.lchunk, W), l1_f=(4, sz.lchunk, W), l2_s=(sz.lrows, W), l2_n=(4, sz.lchunk, W),
+            l2_o=(4, sz.lchunk, W), l2_f=(4, sz.lchunk, W), gps=(4, PL, LN), wr_t=(4 * D, D), ogp=(T, LN),
+            w2p=(4, C, LN),
+        ),
+        F32: dict(
+            t0=(sz.tokens, LN), t1=(sz.tokens, LN), t2=(sz.tokens, D - 2 * LN), xhr_r=(PL, D), rsr_r=(PL, LN),
+            sbuf=(N, PL, Q), lse_a=(4, 8, sz.edge_q), lse_b=(4, 8, sz.inner_q), row_r=(8, Q), ot_r=(LN, Q),
+            h1_r=(T, D), ux=(4, sz.ext, C), ul=(2, sz.ext, C), ur=(2, sz.ext, C), dgx=(4, sz.ext, C),
+            dzx=(4, sz.ext, C), dzl=(2, sz.ext, C), dzr=(2, sz.ext, C), g_r=(4, PL, C), du_r=(4, PL, C),
+            dh1_r=(PL, D), dr_r=(4, 8, Q), dqt=(LN, Q), dqt5=(LN, Q), ve_s=(16, W), ve_n=(16, W),
+            ve_p=(4, 16, W), vl_s=(8, W), vl_n=(8, W), vl_p=(4, 8, W),
+        ),
+    }
+    scratch = {k: pltpu.VMEM(v, t) for t, group in shapes.items() for k, v in group.items()}
+    for i in range(1, len(ins)):
+        scratch["in%d" % i] = pltpu.VMEM(ins[i].shape, ins[i].dtype)
+    scratch["ssem"] = pltpu.SemaphoreType.DMA((200,))
+    scratch["rsem"] = pltpu.SemaphoreType.DMA((200,))
+    scratch["isem"] = pltpu.SemaphoreType.DMA((len(ins),))
+    mid = pl.pallas_call(
+        functools.partial(fused_body, sz, tuple(scratch)),
+        out_shape=mids,
+        in_specs=[sm, sm] + [hbm] * len(ins),
+        out_specs=[vm] * len(mids),
+        scratch_shapes=list(scratch.values()),
+        compiler_params=pltpu.CompilerParams(
+            collective_id=0, has_side_effects=True, vmem_limit_bytes=VMEM_MB * 2**20
+        ),
+        name="fused_block",
+    )(pixel_mask, tile_slot.T, *ins)
+    outs = [
+        S((sz.share, sz.tokens), BF), S((sz.share, sz.tokens), F32), S((D,), F32), S((D,), F32), S((D, D), F32),
+        S((D,), F32), S((D, D), F32), S((D, D), F32), S((D,), F32), S((D, 4 * D), F32), S((D,), F32), S((D,), F32),
+        S((D,), F32), S((D, D), F32), S((D,), F32), S((D,), F32), S((D,), F32), S((D, C), F32), S((C,), F32),
+        S((9, C), F32), S((C,), F32), S((C, D), F32), S((D,), F32),
+    ]
+    res = list(
+        pl.pallas_call(
+            functools.partial(unpack_body, sz),
+            out_shape=outs,
+            in_specs=[vm] * len(mids),
+            out_specs=[vm] * len(outs),
+            scratch_shapes=[pltpu.VMEM((sz.tokens, sz.share), F32)] * 2,
+            compiler_params=pltpu.CompilerParams(vmem_limit_bytes=24 * 2**20),
+            name="unpack",
+        )(*mid)
+    )
+    for k in (0, 1, 9):
+        res[k] = res[k].T
+    return tuple(res)
+
+
+def choose(*args):
+    tokens, width = args[1].shape
+    whole_rows = tokens == FRAME * (FRAME // TILE_ROWS)
+    shape = (lax.axis_size("dp"), lax.axis_size("mp"))
+    if whole_rows and shape == (TILE_ROWS, 4) and TILE_ROWS == 8 and HEADS == 5 and width == 320 == args[19].shape[1]:
+        return on_device_fused(*args)
+    return on_device(*args)
+
+
 def solution(mesh):
     return jax.shard_map(
-        on_device,
+        choose,
         mesh=mesh,
         in_specs=(
             P("dp", "mp"),

time: 924 us -> 146 us (0.16)
  waiting for transfers between devices: 359 us -> 0 us
  blocking collectives: 298 us -> 0 us
  Pallas kernels: 0 us -> 137 us
  matrix products: 91.7 us -> 0 us
  local copies, waits for them, and re-layouts: 97 us -> 7.19 us
  other arithmetic: 50.8 us -> 0 us
  between operations: 18.3 us -> 0.83 us
    psum x5 -> x0, waiting for transfers between devices: 256 us -> none  [the longest x1 116 us: on_device(): lax.psum((grad_w_reduce, grad_b_reduce, grad_lnr_gain, grad_lnr_bias, gra...]
    all_gather x7 -> x0, blocking collectives: 199 us -> none  [the longest x1 32.8 us: on_device(): lax.all_gather(jnp.stack([tile_u[0], tile_u[-1]]), 'dp', axis=0, tiled=True)]
    pallas_call x0 -> x2, Pallas kernels: none -> 137 us  [the longest x1 134 us: on_device_fused(): pl.pallas_call(functools.partial(fused_body, sz, tuple(scratch)), out_sha...]
    unnamed x10 -> x0, waiting for transfers between devices: 103 us -> none
    dot_general x77 -> x0, matrix products: 91.7 us -> none  [the longest x21 22.4 us: mat(): return jnp.dot(left, right, preferred_element_type=jnp.float32)]
    psum x2 -> x0, blocking collectives: 77.8 us -> none  [the longest x1 39.7 us: on_device(): lax.psum((spread_columns(grad_wq, select_where), spread_vector(grad_bq, s...]
    reshape x20 -> x0, local copies, waits for them, and re-layouts: 35.5 us -> none  [the longest x4 11.7 us: on_device(): dpatch = mat(drb, w_reduce.T).reshape(rows // 2, cols // 2, 2, 2, width)....]
    reduce_sum x23 -> x0, other arithmetic: 34.3 us -> none  [the longest x4 9.89 us: top_step(): jnp.sum(jnp.exp(scores - new_top[..., None]), axis=-1)]
  transfers between devices with their start and end apart: 8 -> 0, of which waited for: 7 -> 0; matrix products, arithmetic and copies ran while one was open for 7% -> 0% of each run, Pallas kernels for 0% -> 0%
where the time goes in v2:
time: 146 us; the launch traced here: 145 us
  Pallas kernels  137 us (94%)
  local copies, waits for them, and re-layouts  7.19 us (5%)
    pallas_call x1, Pallas kernels, on_device_fused(): pl.pallas_call(functools.partial(fused_body, sz, tuple(scratch)), out_sha...  134 us
    unnamed x14, local copies, waits for them, and re-layouts  7.19 us

profile of v2, /device:TPU:0, one launch (start us, length us, event | category | flops | bytes accessed | tf_op | source)
XLA Modules:
  0.0 145.4 jit_solution(10876535035764350458)
XLA Ops:
  0.7 134.4 %fused_block.1 = (f32[832,128]{1,0:T(8,128)}, bf16[4,208,128]{2,1,0:T(8,128)(2,1)}, bf16[8,80,384]{2,1,0:T(8,128)(2,1)}, bf16[4,8,48,384]{3,2,1,0:T(8,128)(2,1)}...) custom-call(s32[800]{0:T(1024)} %mask_ref.1, s32[2,8]{1,0:T(2,128)} %bitcast.10, ...), custom_call_target="tpu_custom_call" | custom-call | tf_op jit(solution)/shard_map/fused_block/pallas_call | solution.py:1481
  135.1 0.0 copy-start
  135.1 1.3 copy-done
  136.4 0.0 copy-start.1
  136.4 1.3 copy-done.1
  137.7 0.0 copy-start.2
  137.7 1.0 copy-done.2
  138.7 0.0 copy-start.3
  138.7 1.0 copy-done.3
  139.7 0.0 copy-start.4
  139.7 0.9 copy-done.4
  140.6 0.0 copy-start.5
  140.6 0.9 copy-done.5
  141.5 0.0 copy-start.6
  141.5 0.8 copy-done.6
  142.3 2.9 %unpack.1 = (bf16[80,800]{1,0:T(8,128)(2,1)}, f32[80,800]{1,0:T(8,128)}, f32[320]{0:T(512)}, f32[320]{0:T(512)}, f32[320,320]{1,0:T(8,128)}, /*index=5*/f32[320]...) custom-call(f32[832,128]{1,0:T(8,128)S(1)} %copy-done.3, ...), custom_call_target="tpu_custom_call" | custom-call | tf_op jit(solution)/shard_map/unpack/pallas_call | solution.py:1499
Async XLA Ops:
  135.1 1.3 copy-start
  136.4 1.3 copy-start.1
  137.7 1.0 copy-start.2
  138.7 1.0 copy-start.3
  139.7 0.9 copy-start.4
  140.6 0.9 copy-start.5
  141.5 0.8 copy-start.6

commit v3 on v2

--- a/solution.py
+++ b/solution.py
@@ -546,8 +546,11 @@
         self.inner_q = -(-self.inner // LANES) * LANES
         self.queries = self.edge_q + self.inner_q
         self.echunk = (width + hidden) // n_dp
-        self.lrows = width + HEAD_FEATURES
-        self.lchunk = self.lrows // n_dp
+        self.half = width - 2 * LANES
+        self.wrows = 2 * width + width // 2
+        self.l2rows = -(-(self.wrows + self.share) // (16 * n_dp)) * 16 * n_dp
+        self.orows = HEAD_FEATURES + HEAD_FEATURES // n_mp
+        self.l1rows = -(-(2 * width + 2 * self.orows + self.orows // 2) // (16 * n_dp)) * 16 * n_dp
 
 
 class Load:
@@ -572,8 +575,15 @@
 ):
     ins, refs = refs[:23], refs[23:]
     outs, refs = refs[:7], refs[7:]
-    blk_ref, gp_ref, eg_ref, lg1_ref, lg2_ref, veg_ref, vlg_ref = outs
     s = dict(zip(names, refs))
+    blk_ref, gp_ref, eg_ref, lg1_ref, lg2_ref, veg_ref, vlg_ref = (s["out%d" % i] for i in range(7))
+    stores = []
+
+    def store(i):
+        c = pltpu.make_async_copy(s["out%d" % i], outs[i], s["osem"].at[i])
+        c.start()
+        stores.append(c)
+
     D, HF, PB, PA, KEYS, PL, T = sz.width, HEAD_FEATURES, sz.pb, sz.pa, sz.keys, sz.plane, sz.all
     C, FS, W = sz.hidden, sz.share, sz.wide
     d = lax.axis_index("dp")
@@ -656,24 +666,33 @@
 
         return handle(finish), mid
 
-    def dp_start(buf):
+    def dp_start(buf, each=lambda k: None):
         base = take(7)
         for kz in (3, 2, 1):
             send(buf.at[d], buf.at[d], base + kz, (dpx(2 * kz), m))
         send(buf.at[d], buf.at[d], base, (dpx(1), m))
 
-        def finish(each=lambda k: None):
+        def along(kz):
+            arrived(buf.at[dpx(2 * kz)], base + kz)
+            send(buf.at[dpx(2 * kz)], buf.at[dpx(2 * kz)], base + 3 + kz, (dpx(1), m))
+            each(2 * kz)
+
+        def across(kz):
+            arrived(buf.at[dpx(2 * kz + 1)], base + 3 + kz if kz else base)
+            each(2 * kz + 1)
+
+        steps = [handle(lambda kz=kz: along(kz)) for kz in (1, 2, 3)] + [handle(lambda: across(0))]
+
+        def mid():
+            for step in steps:
+                step()
+
+        def finish():
+            mid()
             for kz in (1, 2, 3):
-                arrived(buf.at[dpx(2 * kz)], base + kz)
-                send(buf.at[dpx(2 * kz)], buf.at[dpx(2 * kz)], base + 3 + kz, (dpx(1), m))
-                each(2 * kz)
-            arrived(buf.at[dpx(1)], base)
-            each(1)
-            for kz in (1, 2, 3):
-                arrived(buf.at[dpx(2 * kz + 1)], base + 3 + kz)
-                each(2 * kz + 1)
-
-        return handle(finish)
+                across(kz)
+
+        return handle(finish), mid, steps
 
     def mp_scatter(block, dst, landed):
         base = take(4)
@@ -870,7 +889,7 @@
     dyh, dyh_g = s["dyh"], s["dyh_g"]
     dyh[d, :, :D] = dfm[pl.ds(pl.multiple_of(PL * m + (KEYS - PB) * (m // 2), 16), 48), :]
     dyh[d, :, D:] = jnp.zeros((48, W - D), BF)
-    dy_at = dp_start(dyh)
+    dy_at, _, _ = dp_start(dyh)
     x_mid()
 
     r2, c2 = iota((D, LANES), 0), iota((D, LANES), 1)
@@ -887,6 +906,25 @@
     nil = jnp.zeros((1, HF), F32)
     bkv = jnp.concatenate([nil, own_part(bv, HF)], axis=1)
     bkv5 = jnp.concatenate([nil, bv[:, last:]], axis=1)
+    rt, ct = iota((D, 4 * LANES), 0), iota((D, 4 * LANES), 1)
+    lane4, head4 = ct & (LANES - 1), ct >> 7
+    place_out = hot((lane4 < FS) & (rt == FS * head4 + lane4))
+    rk, ck = iota((D, 5 * LANES), 0), iota((D, 5 * LANES), 1)
+    lane5, head5 = ck & (LANES - 1), ck >> 7
+    w_all, wq_cat, w2_t, wo_cat = s["w_all"], s["wq_cat"], s["w2_t"], s["wo_cat"]
+    w_all[...] = (
+        nn(wk, hot((lane5 < HF) & (rk == HF * head5 + lane5)))
+        + nn(wv, hot((lane5 >= HF) & (rk == HF * head5 + lane5 - HF)))
+    ).astype(BF)
+    wq_cat[...] = nn(
+        wq, hot(rt == jnp.where(lane4 < HF, HF * head4 + lane4, last + lane4 - HF))
+    ).astype(BF)
+    w2 = w2_ref[...]
+    w2_t[...] = w2.T
+    wo = wo_ref[...]
+    wo_cat[...] = jnp.concatenate(
+        [b for h in range(4) for b in (wo[HF * h : HF * (h + 1)], wo[last:])], axis=0
+    )
     wr_t = s["wr_t"]
     wr_t[...] = wr_ref[...].T
 
@@ -908,7 +946,7 @@
     kva[d, 0:PL, :] = (nn(xr_r[...], wkv) + bkv).astype(BF)
     quarter_rows = pl.ds(pl.multiple_of(sz.step * m, 16), sz.quarter)
     kva[d, PL:, :] = (nn(xr_r[quarter_rows, :], wkv5) + bkv5).astype(BF)
-    kv_at = dp_start(kva)
+    kv_at, _, _ = dp_start(kva)
 
     qa_r, qb_r = s["qa_r"], s["qb_r"]
     Q = sz.queries
@@ -923,15 +961,8 @@
     dyg_at, dyg_mid = mp_start(dyh_g)
 
     dgx, dzx = s["dgx"], s["dzx"]
-    w2 = w2_ref[...]
-    dgx[...] = jnp.zeros_like(dgx)
-    dzx[...] = jnp.zeros_like(dzx)
     for p in range(4):
         dgx[p, sz.top : sz.top + PL, :] = nt(dfm[plane(p), :], w2).astype(BF).astype(F32)
-    wo = wo_ref[...]
-    wo_cat = jnp.concatenate(
-        [b for h in range(4) for b in (wo[HF * h : HF * (h + 1)], wo[last:])], axis=0
-    )
     limit5 = jnp.where(m == sz.n_mp - 1, KEYS - sz.step * m, sz.step)
     pk = iota((sz.quarter, 1), 0)
     bias5 = jnp.concatenate(
@@ -970,6 +1001,8 @@
             return jnp.maximum(top, jnp.max(v, axis=0, keepdims=True))
 
         top = lax.fori_loop(0, sz.n_dp, score_step, jnp.full((1, hi - lo), NEG, F32))
+        if ogs:
+            ogs[0][1]()
 
         def exp_step(j, total, lo=lo, hi=hi, top=top):
             e = jnp.exp(sbuf[j, :, lo:hi] - top).astype(BF)
@@ -1008,9 +1041,10 @@
     xmine = jnp.concatenate([xmine[0:PB], xmine[KEYS - PB : KEYS]], axis=0)
     im, jm = m // 2, lax.rem(m, 2)
     emask = jnp.concatenate([row_mask(im, jm, 0), row_mask(im, jm, PA - 1)], axis=0)
-    hal[d, :, :D] = second_norm(xmine + emask * (nn(oc, wo_cat) + vec(bo_ref)))
+    hal[d, :, :D] = second_norm(xmine + emask * (nn(oc, wo_cat[...]) + vec(bo_ref)))
     hal[d, :, D:] = jnp.zeros((2 * PB, W - D), BF)
-    hal_at = dp_start(hal)
+    hal_at, hal_mid, hal_steps = dp_start(hal)
+    ogs[1][1]()
 
     dyg_at()
     for p in range(4):
@@ -1018,60 +1052,40 @@
         start = sz.top - PB if i == 1 else sz.top + KEYS
         rows = dyh_g[p][:, :D].astype(F32)[0:PB] * row_mask(i, j, -1 if i == 1 else PA)
         dgx[p, start : start + PB, :] = nt(rows.astype(BF), w2).astype(BF).astype(F32)
-    for k in range(sz.n_dp):
-        e5buf[k] = (e5buf[k].astype(F32) * row_r[1:2, :]).astype(BF)
-
     ogs[1][0]()
     mixed = []
     for og in (og_a, og_b):
         oc = jnp.concatenate([og[h] for h in range(4)], axis=1)
-        mixed.append(nn(oc, wo_cat) + vec(bo_ref))
+        mixed.append(nn(oc, wo_cat[...]) + vec(bo_ref))
     w1, b1 = w1_ref[...], vec(b1_ref)
 
     def hidden(rows, mask):
         return ((nn(rows, w1) + b1) * mask).astype(BF).astype(F32)
 
     ux, ul, ur, dzl, dzr = s["ux"], s["ul"], s["ur"], s["dzl"], s["dzr"]
+    b40 = iota((PB, 1), 0)
+
+    def shift(src, left, right, i, start):
+        at = slice(start, start + PB)
+        left[i, at, :] = jnp.where(b40 == 0, 0.0, pltpu.roll(src[2 * i + 1, at, :], 1, 0))
+        right[i, at, :] = jnp.where(b40 == PB - 1, 0.0, pltpu.roll(src[2 * i, at, :], PB - 1, 0))
+
     for p in range(4):
         mask = token_mask(p // 2, p % 2)
         h1 = xm_r[plane(p), :].astype(F32) + mask * from_queries(mixed[0], mixed[1], p)
         h1_r[plane(p), :] = h1
         n2_r[plane(p), :] = second_norm(h1)
-        ux[p, 0 : sz.top, :] = jnp.zeros((sz.top, C), F32)
         ux[p, sz.top : sz.top + PL, :] = hidden(n2_r[plane(p), :], mask)
-    ogp = s["ogp"]
+    for i in range(2):
+        for a in range(PA):
+            shift(ux, ul, ur, i, sz.top + PB * a)
+    hal_steps[0]()
+
+    wd_ref, bd_row = wd_ref.ready(), vec(bd_ref)
+    g_r, du_r = s["g_r"], s["du_r"]
     for p in range(4):
-        ogp[plane(p), :] = from_queries(og_a[m].astype(F32), og_b[m].astype(F32), p).astype(BF)
-    w2p = s["w2p"]
-    rt, ct = iota((D, 4 * LANES), 0), iota((D, 4 * LANES), 1)
-    lane4, head4 = ct & (LANES - 1), ct >> 7
-    place_out = hot((lane4 < FS) & (rt == FS * head4 + lane4))
-    w2_wide = nn(w2, place_out).astype(BF)
-    for h in range(4):
-        w2p[h] = w2_wide[:, LANES * h : LANES * (h + 1)]
-    hal_at()
-    up_rows = hal[above].astype(F32)[PB:]
-    down_rows = hal[below].astype(F32)[0:PB]
-    hal_g[m] = jnp.concatenate([up_rows, down_rows], axis=0).astype(BF)
-    halg_at, _ = mp_start(hal_g)
-    g_r, du_r = s["g_r"], s["du_r"]
-    g_r[...] = jnp.zeros_like(g_r)
-    du_r[...] = jnp.zeros_like(du_r)
-    halg_at()
-    for p in range(4):
-        i, j = p // 2, p % 2
-        mask = jnp.concatenate([row_mask(i, j, -1), row_mask(i, j, PA)], axis=0)
-        u = hidden(hal_g[p][:, :D], mask)
-        ux[p, sz.top - PB : sz.top, :] = u[0:PB]
-        ux[p, sz.top + KEYS : sz.top + KEYS + PB, :] = u[PB:]
-
-    _, be = place(iota((sz.ext, 1), 0) + (PB - 8), PA + 3)
-    wd_ref, bd_row = wd_ref.ready(), vec(bd_ref)
-
-    def shifted(src, left, right):
-        for i in range(2):
-            left[i] = jnp.where(be == 0, 0.0, pltpu.roll(src[2 * i + 1], 1, 0))
-            right[i] = jnp.where(be == PB - 1, 0.0, pltpu.roll(src[2 * i], sz.ext - 1, 0))
+        g_r[p, KEYS:PL, :] = jnp.zeros((PL - KEYS, C), F32)
+        du_r[p, KEYS:PL, :] = jnp.zeros((PL - KEYS, C), F32)
 
     def source(refs, i, j, di, dj, start):
         base, left, right = refs
@@ -1085,7 +1099,6 @@
         return base[2 * i2 + j2, at, :]
 
     TAPS = [(di, dj) for di in (-1, 0, 1) for dj in (-1, 0, 1)]
-    shifted(ux, ul, ur)
 
     def activation(i, j, start):
         p = 2 * i + j
@@ -1102,27 +1115,59 @@
     def fold(value):
         return jnp.sum(value.reshape(PB // 8, 8, C), axis=0)
 
-    ve_s, vl_s = s["ve_s"], s["vl_s"]
-    sums = [jnp.zeros((8, C), F32) for _ in range(10)]
+    def forward_step(i, j):
+        p = 2 * i + j
+
+        def step(a, acc):
+            start = sz.top + PB * a
+            act, dz = activation(i, j, start)
+            g_r[p, pl.ds(pl.multiple_of(PB * a, 8), PB), :] = act
+            new = [
+                acc[t] + fold(dz * source((ux, ul, ur), i, j, di, dj, start))
+                for t, (di, dj) in enumerate(TAPS)
+            ]
+            return tuple(new) + (acc[9] + fold(dz),)
+
+        return step
+
+    sums = tuple(jnp.zeros((8, C), F32) for _ in range(10))
     for i in range(2):
         for j in range(2):
-            p = 2 * i + j
+            sums = lax.fori_loop(1 - i, PA - i, forward_step(i, j), sums)
+        hal_steps[1 + i]()
+    hal_at()
+    up_rows = hal[above].astype(F32)[PB:]
+    down_rows = hal[below].astype(F32)[0:PB]
+    hal_g[m] = jnp.concatenate([up_rows, down_rows], axis=0).astype(BF)
+    halg_at, _ = mp_start(hal_g)
+    for k in range(sz.n_dp):
+        e5buf[k] = (e5buf[k].astype(F32) * row_r[1:2, :]).astype(BF)
+    ogp = s["ogp"]
+    lane = iota((T, LANES), 1)
+    fifth = [sum(og[h].astype(F32) for h in range(4)) for og in (og_a, og_b)]
+    owns = [og[m].astype(F32) for og in (og_a, og_b)]
+    for p in range(4):
+        ogp[plane(p), :] = jnp.where(
+            lane[plane(p)] < HF, from_queries(*owns, p), from_queries(*fifth, p)
+        ).astype(BF)
+    halg_at()
+    for p in range(4):
+        i, j = p // 2, p % 2
+        mask = jnp.concatenate([row_mask(i, j, -1), row_mask(i, j, PA)], axis=0)
+        u = hidden(hal_g[p][:, :D], mask)
+        ux[p, sz.top - PB : sz.top, :] = u[0:PB]
+        ux[p, sz.top + KEYS : sz.top + KEYS + PB, :] = u[PB:]
+    for i in range(2):
+        shift(ux, ul, ur, i, sz.top - PB)
+        shift(ux, ul, ur, i, sz.top + KEYS)
+    for i in range(2):
+        for j in range(2):
             activation(i, j, sz.top - PB if i == 1 else sz.top + KEYS)
-
-            def forward_step(a, acc, i=i, j=j, p=p):
-                start = sz.top + PB * a
-                act, dz = activation(i, j, start)
-                g_r[p, pl.ds(pl.multiple_of(PB * a, 8), PB), :] = act
-                new = [
-                    acc[t] + fold(dz * source((ux, ul, ur), i, j, di, dj, start))
-                    for t, (di, dj) in enumerate(TAPS)
-                ]
-                return tuple(new) + (acc[9] + fold(dz),)
-
-            sums = lax.fori_loop(0, PA, forward_step, tuple(sums))
-    for t in range(10):
-        ve_s[t : t + 1, :C] = rowsum(sums[t])
-    shifted(dzx, dzl, dzr)
+            sums = forward_step(i, j)((PA - 1) * i, sums)
+    e_s, ve_s, vl_s = s["e_s"], s["ve_s"], s["vl_s"]
+    for i in range(2):
+        for a in range(PA + 1):
+            shift(dzx, dzl, dzr, i, sz.top + PB * (a - i))
     dub = s["dub"]
     for i in range(2):
         for j in range(2):
@@ -1141,16 +1186,17 @@
     dn2_mid, dn2_at = mp_sum(lambda h: nt(dub[h], w1), s["dn2_s"], s["dn2_n"], s["dn2_f"])
     dn2_mid()
 
-    e_s = s["e_s"]
     gb = g_r[...].reshape(T, C).astype(BF)
     du_all = dub[...].reshape(T, C)
     e_s[0:D, :C] = tn(n2_r[...], du_all).astype(BF)
     e_s[D:, :D] = tn(gb, dfm[...]).astype(BF)
-    e_at = dp_scatter(
-        lambda j: e_s.at[pl.ds(pl.multiple_of(sz.echunk * j, 16), sz.echunk)],
-        lambda k: s["e_r"].at[k - 1],
-        lambda k: s["e_r"].at[k - 1],
-    )
+
+    def rows_of(ref, n):
+        return lambda j: ref.at[pl.ds(pl.multiple_of(n * j, 16), n)]
+
+    e_mid, e_at = dp_sum(rows_of(e_s, sz.echunk), s["e_n"], s["e_o"], s["e_f"])
+    for t in range(10):
+        ve_s[t : t + 1, :C] = rowsum(sums[t])
     ve_s[10:11, :C] = rowsum(du_all.astype(F32))
 
     xhat2, rstd2 = spread(plane_rows(h1_r, PL * m))
@@ -1158,29 +1204,33 @@
     ve_s[11:12, :D] = rowsum(dfp)
     dn2 = dn2_at()
     dh1 = dfp + norm_back(dn2, vec(ln2g_ref), xhat2, rstd2)
-    s["dh1_r"][...] = dh1
     dab = dh1.astype(BF)
-    docat = nt(dab, wo_cat).astype(BF)
+    docat = nt(dab, wo_cat[...]).astype(BF)
     dos, do_all, dabg = s["dos"], s["do_all"], s["dabg"]
     for h in range(4):
         dos[h] = docat[:, LANES * h : LANES * (h + 1)]
     do_at = mp_scatter(lambda h: dos.at[h], lambda k: do_all.at[m], lambda k: do_all.at[mpx(k)])
     do_all[m] = dos[m]
+    s["dh1_r"][...] = dh1
     dabg[m, :, :D] = dab
-    dab_at, dab_mid = mp_start(dabg)
     ve_s[12:13, :D] = rowsum(dh1)
     ve_s[13:14, :D] = rowsum(dn2 * xhat2)
     ve_s[14:15, :D] = rowsum(dn2)
     ve_s[15:16, :] = jnp.zeros((1, W), F32)
     ve_mid, ve_at = dp_total(ve_s, s["ve_n"], s["ve_p"])
-
-    ff_mid, ff_at = mp_sum(lambda h: nn(gb, w2p[h]), s["ff_s"], s["ff_n"], s["ff_f"])
+    e_mid()
+
+    def ff_block(h):
+        return nt(w2_t[pl.ds(pl.multiple_of(FS * h, 16), FS), :], gb)
+
+    ff_mid, ff_at = mp_sum(ff_block, s["ff_s"], s["ff_n"], s["ff_f"])
 
     do_at()
     dr_r = s["dr_r"]
     dot_t = to_queries([do_all[p].astype(F32) for p in range(4)]).T
     dr_r[m] = jnp.broadcast_to(rowsum(dot_t[HF:] * ot_r[HF:, :]), (8, Q))
     dr_at = mp_scatter(lambda h: dr_r.at[m], lambda k: dr_r.at[m], lambda k: dr_r.at[mpx(k)])
+    dab_at, dab_mid = mp_start(dabg)
     da_own = (dot_t[0:HF] * row_r[0:1, :]).astype(BF)
     drow = rowsum(da_own.astype(F32) * ot_r[0:HF, :])
     da_t = jnp.concatenate([half.astype(BF), da_own], axis=0)
@@ -1188,33 +1238,49 @@
     dqt, dqt5 = s["dqt"], s["dqt5"]
     dqt[...] = jnp.zeros_like(dqt)
     dqt5[...] = jnp.zeros_like(dqt5)
-    ff_mid()
-    dr_at()
-    drow5 = sum(dr_r[h][0:1] for h in range(4))
-
-    def key_block(j):
-        kv = kva[j, 0:PL, :]
-        e = ebuf[j]
+    five_row = []
+
+    def own_keys(j):
+        kv, e = kva[j, 0:PL, :], ebuf[j]
         ds = (e.astype(F32) * (nn(kv, da_t) - drow)).astype(BF)
-        own = nt(ds, qa_r[...]) + nt(e, da_t)
         dqt[...] += tn(kv, ds)
-        kv = kva[j, PL:, :]
-        e = e5buf[j]
-        ds = (e.astype(F32) * (nn(kv, db_t) - drow5)).astype(BF)
+        return nt(ds, qa_r[...]) + nt(e, da_t)
+
+    def last_keys(j):
+        kv, e = kva[j, PL:, :], e5buf[j]
+        ds = (e.astype(F32) * (nn(kv, db_t) - five_row[0])).astype(BF)
         dqt5[...] += tn(kv, ds)
-        return jnp.concatenate([own, nt(ds, qb_r[...]) + nt(e, db_t)], axis=0)
+        return nt(ds, qb_r[...]) + nt(e, db_t)
 
     dk_x, dk_n, dk_o, dk_f = s["dk_x"], s["dk_n"], s["dk_o"], s["dk_f"]
     dk_at = take(8)
-    for kz in (2, 3, 1, 0):
-        dk_x[kz] = key_block(dpx(2 * kz + 1)).astype(BF)
+
+    def dk_across(kz, own):
+        dk_x[kz] = jnp.concatenate([own, last_keys(dpx(2 * kz + 1))], axis=0).astype(BF)
         send(dk_x.at[kz], dk_n.at[kz], dk_at + kz, (dpx(1), m))
-    for kz in (2, 3, 1):
-        value = key_block(dpx(2 * kz))
+
+    def dk_along(kz):
+        j = dpx(2 * kz)
+        value = jnp.concatenate([own_keys(j), last_keys(j)], axis=0)
         arrived(dk_n.at[kz], dk_at + kz)
         dk_o[kz] = (value + dk_n[kz].astype(F32)).astype(BF)
         send(dk_o.at[kz], dk_f.at[kz], dk_at + 4 + kz, (dpx(2 * kz), m))
-    dkv = key_block(d)
+
+    own2 = own_keys(dpx(5))
+    own3 = own_keys(dpx(7))
+    dr_at()
+    five_row.append(sum(dr_r[h][0:1] for h in range(4)))
+    dk_across(2, own2)
+    dk_across(3, own3)
+    ve_mid()
+    dk_across(1, own_keys(dpx(3)))
+    dab_mid()
+    dk_across(0, own_keys(dpx(1)))
+    dk_along(2)
+    dk_along(3)
+    ff_mid()
+    dk_along(1)
+    dkv = jnp.concatenate([own_keys(d), last_keys(d)], axis=0)
 
     def dk_finish():
         arrived(dk_n.at[0], dk_at)
@@ -1232,70 +1298,57 @@
         dqs[h] = from_queries(dq2[: sz.edge_q], dq2[sz.edge_q :], h).astype(BF)
     dq_at = mp_scatter(lambda h: dqs.at[h], lambda k: dq_all.at[m], lambda k: dq_all.at[mpx(k)])
     dq_all[m] = dqs[m]
-    ve_mid()
+    eg_ref[d] = e_at().astype(BF)
+    eg_at, eg_mid, _ = dp_start(eg_ref)
     l1_s, l2_s = s["l1_s"], s["l2_s"]
     dqp = dqs[...].reshape(T, LANES)
-    l1_s[0:D, 0:LANES] = tn(n1_r[...], dqp).astype(BF)
+    l1_s[0:D, :] = tn(n1_r[...], dqp).astype(BF)
     vl_s[...] = jnp.zeros_like(vl_s)
     vl_s[5:6, 0:LANES] = rowsum(dqp.astype(F32))
+
+    def packed(value):
+        n = value.shape[0] // 2
+        parts = [value[:, 0:LANES], value[:, LANES : 2 * LANES]]
+        parts.append(jnp.concatenate([value[0:n, 2 * LANES :], value[n:, 2 * LANES :]], axis=1))
+        return jnp.concatenate(parts, axis=0)
+
+    def fill(ref, first, value):
+        rest = jnp.zeros((ref.shape[0] - first - value.shape[0], LANES), F32)
+        ref[first:, :] = jnp.concatenate([value, rest], axis=0).astype(BF)
+
+    def own_rows(value, n):
+        return sum(jnp.where(m == h, 1.0, 0.0) * value[n * h : n * (h + 1)] for h in range(4))
+
     dab_at()
-    gwo = tn(ogp[...], dabg[...].reshape(T, W)[:, :D]).astype(BF)
-    l1_s[D:, :D] = gwo[0:HF]
-    l2_s[D:, :D] = gwo[HF:]
-
-    ff = ff_at()
-    sel = hot((c2 < FS) & (r2 == FS * m + c2))
-    b2q = jnp.concatenate(
-        [own_part(vec(b2_ref), FS), jnp.zeros((1, LANES - FS), F32)], axis=1
-    )
-    for p in range(4):
-        h1 = h1_r[plane(p), :]
-        hi = h1.astype(BF)
-        h1q = nn(hi, sel) + nn((h1 - hi.astype(F32)).astype(BF), sel)
-        blk_ref[plane(p), :] = h1q + token_mask(p // 2, p % 2) * (ff[plane(p)] + b2q)
-
-    e_at()
-    mine = e_s[pl.ds(pl.multiple_of(sz.echunk * d, 16), sz.echunk), :].astype(F32)
-    eg_ref[d] = (mine + sum(s["e_r"][k].astype(F32) for k in range(sz.n_dp - 1))).astype(BF)
+    gwo = tn(ogp[...], dabg[...].reshape(T, W)[:, :D])
+    fill(l1_s, 2 * D, packed(jnp.concatenate([gwo[0:HF], own_rows(gwo[HF:], HF // 4)], axis=0)))
 
     dkvb = dk_fin().astype(BF)
     dkvg = s["dkvg"]
     dkvg[m] = dkvb
     dkv_at, dkv_mid = mp_start(dkvg)
-    l1_s[0:D, LANES : 2 * LANES] = tn(xr_r[...], dkvb[0:PL]).astype(BF)
-    l1_s[0:D, 2 * LANES :] = tn(xr_r[quarter_rows, :], dkvb[PL:]).astype(BF)
-
-    def lchunk(ref):
-        return lambda j: ref.at[pl.ds(pl.multiple_of(sz.lchunk * j, 16), sz.lchunk)]
-
-    l1_mid, l1_at = dp_sum(lchunk(l1_s), s["l1_n"], s["l1_o"], s["l1_f"])
+    l1_s[D : 2 * D, :] = tn(xr_r[...], dkvb[0:PL]).astype(BF)
+    l1_mid, l1_at = dp_sum(rows_of(l1_s, sz.l1rows // sz.n_dp), s["l1_n"], s["l1_o"], s["l1_f"])
     vl_s[6:7, 0:LANES] = jnp.concatenate(
         [rowsum(dkvb[0:PL].astype(F32))[:, HF:], rowsum(dkvb[PL:].astype(F32))[:, HF:]], axis=1
     )
-    rk, ck = iota((D, 5 * LANES), 0), iota((D, 5 * LANES), 1)
-    lane5, head5 = ck & (LANES - 1), ck >> 7
-    w_all = (
-        nn(wk, hot((lane5 < HF) & (rk == HF * head5 + lane5)))
-        + nn(wv, hot((lane5 >= HF) & (rk == HF * head5 + lane5 - HF)))
-    ).astype(BF)
-    wq_cat = nn(
-        wq, hot(rt == jnp.where(lane4 < HF, HF * head4 + lane4, last + lane4 - HF))
-    ).astype(BF)
     dq_at()
     dq_cat = jnp.concatenate([dq_all[h] for h in range(4)], axis=1)
-    dn1 = nt(dq_cat, wq_cat)
+    dn1 = nt(dq_cat, wq_cat[...])
     xhat1, rstd1 = spread(plane_rows(xm_r, PL * m).astype(F32))
+    dkv_mid()
     dkv_at()
     rest = jnp.concatenate(
         [dkvg[h, PL : PL + sz.step, :] for h in range(3)] + [dkvg[3, PL:, :]], axis=0
     )
     dkv_all = jnp.concatenate([dkvg[h, 0:PL, :] for h in range(4)] + [rest], axis=1)
-    dxr = nt(dkv_all, w_all)
+    dxr = nt(dkv_all, w_all[...])
     xhr = s["xhr_r"][...]
     drb = norm_back(dxr, vec(lnrg_ref), xhr, s["rsr_r"][:, 0:1]).astype(BF)
-    l2_s[0:D, :D] = tn(drb, plane_rows(n1_r, PL * m)).astype(BF)
+    l2_s[0 : sz.wrows, :] = packed(tn(drb, plane_rows(n1_r, PL * m))).astype(BF)
+    fill(l2_s, sz.wrows, own_rows(tn(xr_r[...], rest), FS))
+    l2_mid, l2_at = dp_sum(rows_of(l2_s, sz.l2rows // sz.n_dp), s["l2_n"], s["l2_o"], s["l2_f"])
     l1_mid()
-    l2_mid, l2_at = dp_sum(lchunk(l2_s), s["l2_n"], s["l2_o"], s["l2_f"])
     vl_s[2:3, :D] = rowsum(dxr * xhr)
     vl_s[3:4, :D] = rowsum(dxr)
     vl_s[4:5, :D] = rowsum(drb.astype(F32))
@@ -1313,97 +1366,104 @@
         gps[h] = gpf[:, LANES * h : LANES * (h + 1)]
     gp_at = mp_scatter(lambda h: gps.at[h], lambda k: gp_ref.at[m], lambda k: gp_ref.at[mpx(k)])
     gp_ref[m] = gps[m]
+    eg_mid()
+
+    ff = ff_at().T
+    ff = jnp.concatenate([ff, jnp.zeros((T, LANES - FS), F32)], axis=1)
+    sel = hot((c2 < FS) & (r2 == FS * m + c2))
+    b2q = jnp.concatenate(
+        [own_part(vec(b2_ref), FS), jnp.zeros((1, LANES - FS), F32)], axis=1
+    )
+    for p in range(4):
+        h1 = h1_r[plane(p), :]
+        hi = h1.astype(BF)
+        h1q = nn(hi, sel) + nn((h1 - hi.astype(F32)).astype(BF), sel)
+        blk_ref[plane(p), :] = h1q + token_mask(p // 2, p % 2) * (ff[plane(p)] + b2q)
+    store(0)
+    veg_ref[m] = ve_at()
+    veg_at, _ = mp_start(veg_ref)
 
     def gather(buf):
-        own = buf.at[m]
-        near = dp_start(own)
         base = take(3 * sz.n_dp)
 
-        def across(k):
+        def onward(k):
             j = dpx(k)
             send(buf.at[m, j], buf.at[m, j], base + 3 * k, (d, mpx(1)))
             send(buf.at[m, j], buf.at[m, j], base + 3 * k + 1, (d, mpx(2)))
 
-        across(0)
+        near, mid, steps = dp_start(buf.at[m], onward)
+        onward(0)
         seq = (0, 2, 4, 6, 1, 3, 5, 7)
 
-        def middle():
-            for k in seq:
-                j = dpx(k)
-                arrived(buf.at[mpx(2), j], base + 3 * k + 1)
-                send(buf.at[mpx(2), j], buf.at[mpx(2), j], base + 3 * k + 2, (d, mpx(1)))
-
-        mid = handle(middle)
+        def relay(k):
+            j = dpx(k)
+            arrived(buf.at[mpx(2), j], base + 3 * k + 1)
+            send(buf.at[mpx(2), j], buf.at[mpx(2), j], base + 3 * k + 2, (d, mpx(1)))
+
+        relays = [handle(lambda k=k: relay(k)) for k in seq]
 
         def finish():
-            near(across)
-            mid()
+            near()
+            for r in relays:
+                r()
             for k in seq:
                 arrived(buf.at[mpx(1), dpx(k)], base + 3 * k)
                 arrived(buf.at[mpx(3), dpx(k)], base + 3 * k + 2)
 
-        return lambda: near(across), handle(finish)
+        return near, mid, relays, handle(finish)
 
     lg1_ref[m, d] = l1_at().astype(BF)
-    lg1_near, lg1_at = gather(lg1_ref)
+    near1, mid1, relays1, lg1_at = gather(lg1_ref)
     l2_mid()
     vl_mid()
-    eg_at = dp_start(eg_ref)
-    veg_ref[m] = ve_at()
-    veg_at, _ = mp_start(veg_ref)
-    lg1_near()
+    mid1()
     lg2_ref[m, d] = l2_at().astype(BF)
-    lg2_near, lg2_at = gather(lg2_ref)
+    near2, mid2, relays2, lg2_at = gather(lg2_ref)
+    near1()
     vlg_ref[m] = vl_at()
     vlg_at, _ = mp_start(vlg_ref)
-    lg2_near()
+    for r in relays1[:4]:
+        r()
+    mid2()
+    for r in relays1[4:]:
+        r()
+    near2()
+    for r in relays2:
+        r()
     eg_at()
+    store(2)
     gp_at()
+    store(1)
     veg_at()
+    store(5)
     lg1_at()
+    store(3)
     vlg_at()
+    store(6)
     lg2_at()
+    store(4)
     for c in pending:
         c.wait_send()
-
-
-def unpack_body(
-    sz, blk_ref, gp_ref, eg_ref, lg1_ref, lg2_ref, veg_ref, vlg_ref,
-    out_ref, gpix_ref, ln1g_ref, ln1b_ref, gwq_ref, gbq_ref, gwk_ref, gwv_ref, gbv_ref, gwr_ref, gbr_ref,
-    lnrg_ref, lnrb_ref, gwo_ref, gbo_ref, ln2g_ref, ln2b_ref, gw1_ref, gb1_ref, gwd_ref, gbd_ref,
-    gw2_ref, gb2_ref, out32, gp32,
-):
+    for c in stores:
+        c.wait()
+
+
+def unpack_body(sz, *refs):
+    srcs, refs = refs[:7], refs[7:]
+    (
+        out_ref, gpix_ref, ln1g_ref, ln1b_ref, gwq_ref, gbq_ref, gwk_ref, gwv_ref, gbv_ref, gwr_ref, gbr_ref,
+        lnrg_ref, lnrb_ref, gwo_ref, gbo_ref, ln2g_ref, ln2b_ref, gw1_ref, gb1_ref, gwd_ref, gbd_ref,
+        gw2_ref, gb2_ref,
+    ), refs = refs[:23], refs[23:]
+    out32, gp32, sem = refs[7:]
+    order = (5, 6, 0, 1, 2, 3, 4)
+    loads = [None] * 7
+    for i in order:
+        loads[i] = Load(srcs[i], refs[i], sem.at[i])
+    blk_ref, gp_ref, eg_ref, lg1_ref, lg2_ref, veg_ref, vlg_ref = loads
     D, HF, PB, PA, PL = sz.width, HEAD_FEATURES, sz.pb, sz.pa, sz.plane
     C, FS = sz.hidden, sz.share
     m = lax.axis_index("mp")
-    for i in range(2):
-        for j in range(2):
-            p = 2 * i + j
-            for a in range(PA):
-                at = pl.ds((2 * a + i) * sz.cols + j, PB, stride=2)
-                out32[at, :] = blk_ref[PL * p + PB * a : PL * p + PB * (a + 1), 0:FS]
-                gp32[at, :] = gp_ref[p].astype(F32)[PB * a : PB * (a + 1), 0:FS]
-    out_ref[...] = out32[...].T.astype(BF)
-    gpix_ref[...] = gp32[...].T
-
-    lg1 = [lg1_ref[h].reshape(sz.lrows, sz.wide) for h in range(4)]
-    lg2 = [lg2_ref[h].reshape(sz.lrows, sz.wide) for h in range(4)]
-
-    def heads(first, tail):
-        parts = [lg1[h][0:D, first : first + HF].astype(F32) for h in range(4)]
-        parts.append(sum(lg1[h][0:D, tail : tail + HF].astype(F32) for h in range(4)))
-        return jnp.concatenate(parts, axis=1)
-
-    gwq_ref[...] = heads(0, HF)
-    gwk_ref[...] = heads(LANES, 2 * LANES)
-    gwv_ref[...] = heads(LANES + HF, 2 * LANES + HF)
-    gwr_ref[...] = jnp.concatenate([lg2[h][0:D, :D].astype(F32) for h in range(4)], axis=1)
-    for h in range(4):
-        gwo_ref[HF * h : HF * (h + 1), :] = lg1[h][D:, :D].astype(F32)
-    gwo_ref[HF * 4 :, :] = sum(lg2[h][D:, :D].astype(F32) for h in range(4))
-    eg = eg_ref[...].reshape(D + C, sz.wide)
-    gw1_ref[...] = eg[0:D, :C].astype(F32)
-    gw2_ref[...] = eg[D:, :D].astype(F32)
 
     def row(value):
         return value.reshape(value.shape[1])
@@ -1430,6 +1490,38 @@
 
     gbq_ref[...] = head_row(5)
     gbv_ref[...] = head_row(6)
+    for i in range(2):
+        for j in range(2):
+            p = 2 * i + j
+            for a in range(PA):
+                at = pl.ds((2 * a + i) * sz.cols + j, PB, stride=2)
+                out32[at, :] = blk_ref[PL * p + PB * a : PL * p + PB * (a + 1), 0:FS]
+                gp32[at, :] = gp_ref[p].astype(F32)[PB * a : PB * (a + 1), 0:FS]
+    out_ref[...] = out32[...].T.astype(BF)
+    gpix_ref[...] = gp32[...].T
+    eg = eg_ref[...].reshape(D + C, sz.wide)
+    gw1_ref[...] = eg[0:D, :C].astype(F32)
+    gw2_ref[...] = eg[D:, :D].astype(F32)
+
+    def unpacked(value):
+        n = value.shape[0] * 2 // 5
+        tail = value[2 * n :]
+        tail = jnp.concatenate([tail[:, 0:HF], tail[:, HF:]], axis=0)
+        return jnp.concatenate([value[0:n], value[n : 2 * n], tail], axis=1)
+
+    lg1 = [lg1_ref[h].reshape(sz.l1rows, LANES).astype(F32) for h in range(4)]
+    lg2 = [lg2_ref[h].reshape(sz.l2rows, LANES).astype(F32) for h in range(4)]
+    tail = jnp.concatenate([lg2[h][sz.wrows : sz.wrows + FS] for h in range(4)], axis=0)
+    fifth = sum(lg1[h][0:D, HF:] for h in range(4))
+    gwq_ref[...] = jnp.concatenate([lg1[h][0:D, 0:HF] for h in range(4)] + [fifth], axis=1)
+    gwk_ref[...] = jnp.concatenate([lg1[h][D : 2 * D, 0:HF] for h in range(4)] + [tail[:, 0:HF]], axis=1)
+    gwv_ref[...] = jnp.concatenate([lg1[h][D : 2 * D, HF:] for h in range(4)] + [tail[:, HF:]], axis=1)
+    gwr_ref[...] = jnp.concatenate([unpacked(lg2[h][0 : sz.wrows]) for h in range(4)], axis=1)
+    n = HF // 4
+    for h in range(4):
+        wo = unpacked(lg1[h][2 * D : 2 * D + 5 * sz.orows // 2])
+        gwo_ref[HF * h : HF * (h + 1), :] = wo[0:HF]
+        gwo_ref[4 * HF + n * h : 4 * HF + n * (h + 1), :] = wo[HF:]
 
 
 def on_device_fused(*args):
@@ -1442,26 +1534,27 @@
     Q, N, PB = sz.queries, sz.n_dp, sz.pb
     sm = pl.BlockSpec(memory_space=pltpu.SMEM)
     vm = pl.BlockSpec(memory_space=pltpu.VMEM)
-    hbm = pl.BlockSpec(memory_space=pl.ANY)
+    hbm = pl.BlockSpec(memory_space=pltpu.HBM)
     S = jax.ShapeDtypeStruct
     ins = [pixels_in.T, cotangent.T, *args[4:11], args[11].T, *args[12:]]
     mids = [
-        S((T, LN), F32), S((4, PL, LN), BF), S((N, sz.echunk, W), BF), S((4, N, sz.lchunk, W), BF),
-        S((4, N, sz.lchunk, W), BF), S((4, 16, W), F32), S((4, 8, W), F32),
+        S((T, LN), F32), S((4, PL, LN), BF), S((N, sz.echunk, W), BF), S((4, N, sz.l1rows // N, LN), BF),
+        S((4, N, sz.l2rows // N, LN), BF), S((4, 16, W), F32), S((4, 8, W), F32),
     ]
+    chunks = dict(e=(sz.echunk, W), l1=(sz.l1rows // N, LN), l2=(sz.l2rows // N, LN))
     shapes = {
         BF: dict(
             xt=(4, sz.share, sz.tokens), dfm=(T, D), dyh=(N, 48, W), dyh_g=(4, 48, W), xm_r=(T, D), n1_r=(T, D),
             xr_r=(PL, D), kva=(N, sz.kvrows, LN), qa_r=(LN, Q), qb_r=(LN, Q), ebuf=(N, PL, Q),
             e5buf=(N, sz.quarter, Q), og_a=(4, sz.edge, LN), og_b=(4, sz.inner, LN), n2_r=(T, D),
             hal=(N, 2 * PB, W), hal_g=(4, 2 * PB, W), dub=(4, PL, C), dn2_s=(3, PL, D), dn2_n=(2, PL, D),
-            dn2_f=(PL, D), dos=(4, PL, LN), do_all=(4, PL, LN), dabg=(4, PL, W), ff_s=(3, T, LN), ff_n=(2, T, LN),
-            ff_f=(T, LN), dk_x=(4, sz.kvrows, LN), dk_n=(4, sz.kvrows, LN), dk_o=(4, sz.kvrows, LN),
+            dn2_f=(PL, D), dos=(4, PL, LN), do_all=(4, PL, LN), dabg=(4, PL, W), ff_s=(3, sz.share, T), ff_n=(2, sz.share, T),
+            ff_f=(sz.share, T), dk_x=(4, sz.kvrows, LN), dk_n=(4, sz.kvrows, LN), dk_o=(4, sz.kvrows, LN),
             dk_f=(4, sz.kvrows, LN), dkvg=(4, sz.kvrows, LN), dqs=(4, PL, LN), dq_all=(4, PL, LN),
-            e_s=(D + C, W), e_r=(N - 1, sz.echunk, W), l1_s=(sz.lrows, W), l1_n=(4, sz.lchunk, W),
-            l1_o=(4, sz.lchunk, W), l1_f=(4, sz.lchunk, W), l2_s=(sz.lrows, W), l2_n=(4, sz.lchunk, W),
-            l2_o=(4, sz.lchunk, W), l2_f=(4, sz.lchunk, W), gps=(4, PL, LN), wr_t=(4 * D, D), ogp=(T, LN),
-            w2p=(4, C, LN),
+            e_s=(D + C, W), gps=(4, PL, LN), wr_t=(4 * D, D), ogp=(T, LN),
+            w2_t=(D, C), w_all=(D, 5 * LN), wq_cat=(D, 4 * LN), wo_cat=(4 * LN, D), l1_s=(sz.l1rows, LN),
+            l2_s=(sz.l2rows, LN),
+            **{n + "_" + k: (4, *v) for k in "nof" for n, v in chunks.items()},
         ),
         F32: dict(
             t0=(sz.tokens, LN), t1=(sz.tokens, LN), t2=(sz.tokens, D - 2 * LN), xhr_r=(PL, D), rsr_r=(PL, LN),
@@ -1477,12 +1570,15 @@
         scratch["in%d" % i] = pltpu.VMEM(ins[i].shape, ins[i].dtype)
     scratch["ssem"] = pltpu.SemaphoreType.DMA((200,))
     scratch["rsem"] = pltpu.SemaphoreType.DMA((200,))
+    for i, v in enumerate(mids):
+        scratch["out%d" % i] = pltpu.VMEM(v.shape, v.dtype)
+    scratch["osem"] = pltpu.SemaphoreType.DMA((len(mids),))
     scratch["isem"] = pltpu.SemaphoreType.DMA((len(ins),))
     mid = pl.pallas_call(
         functools.partial(fused_body, sz, tuple(scratch)),
         out_shape=mids,
         in_specs=[sm, sm] + [hbm] * len(ins),
-        out_specs=[vm] * len(mids),
+        out_specs=[hbm] * len(mids),
         scratch_shapes=list(scratch.values()),
         compiler_params=pltpu.CompilerParams(
             collective_id=0, has_side_effects=True, vmem_limit_bytes=VMEM_MB * 2**20
@@ -1499,10 +1595,12 @@
         pl.pallas_call(
             functools.partial(unpack_body, sz),
             out_shape=outs,
-            in_specs=[vm] * len(mids),
+            in_specs=[hbm] * len(mids),
             out_specs=[vm] * len(outs),
-            scratch_shapes=[pltpu.VMEM((sz.tokens, sz.share), F32)] * 2,
-            compiler_params=pltpu.CompilerParams(vmem_limit_bytes=24 * 2**20),
+            scratch_shapes=[pltpu.VMEM(v.shape, v.dtype) for v in mids]
+            + [pltpu.VMEM((sz.tokens, sz.share), F32)] * 2
+            + [pltpu.SemaphoreType.DMA((len(mids),))],
+            compiler_params=pltpu.CompilerParams(vmem_limit_bytes=60 * 2**20),
             name="unpack",
         )(*mid)
     )

time: 146 us -> 125 us (0.86)
  Pallas kernels: 137 us -> 124 us
  local copies, waits for them, and re-layouts: 7.19 us -> 0 us
    pallas_call x1, Pallas kernels: 134 us -> 120 us  [on_device_fused(): pl.pallas_call(functools.partial(fused_body, sz, tuple(scratch)), out_sha...]
    unnamed x14 -> x0, local copies, waits for them, and re-layouts: 7.19 us -> none
where the time goes in v3:
time: 125 us
  Pallas kernels  124 us (99%)
    pallas_call x1, Pallas kernels, on_device_fused(): pl.pallas_call(functools.partial(fused_body, sz, tuple(scratch)), out_sha...  120 us
    pallas_call x1, Pallas kernels, on_device_fused(): pl.pallas_call(functools.partial(unpack_body, sz), out_shape=outs, in_spe...  4.33 us

profile of v3, /device:TPU:0, one launch (start us, length us, event | category | flops | bytes accessed | tf_op | source)
XLA Modules:
  0.0 125.2 jit_solution(6400169828645554361)
XLA Ops:
  0.7 120.0 %fused_block.1 = (f32[832,128]{1,0:T(8,128)}, bf16[4,208,128]{2,1,0:T(8,128)(2,1)}, bf16[8,80,384]{2,1,0:T(8,128)(2,1)}, bf16[4,8,112,128]{3,2,1,0:T(8,128)(2,1)...) custom-call(s32[800]{0:T(1024)} %mask_ref.1, s32[2,8]{1,0:T(2,128)} %bitcast.10, ...), custom_call_target="tpu_custom_call" | custom-call | tf_op jit(solution)/shard_map/fused_block/pallas_call | solution.py:1577
  120.7 4.3 %unpack.1 = (bf16[80,800]{1,0:T(8,128)(2,1)}, f32[80,800]{1,0:T(8,128)}, f32[320]{0:T(512)}, f32[320]{0:T(512)}, f32[320,320]{1,0:T(8,128)}, /*index=5*/f32[320]...) custom-call(f32[832,128]{1,0:T(8,128)} %get-tuple-element.53.refs_0_, ...), custom_call_target="tpu_custom_call" | custom-call | tf_op jit(solution)/shard_map/unpack/pallas_call | solution.py:1595

commit v4 on v3

--- a/solution.py
+++ b/solution.py
@@ -541,10 +541,8 @@
         self.top = 8 + self.pb
         self.ext = self.top + self.keys + self.pb
         self.edge = 4 * 2 * self.pb
-        self.inner = 4 * (self.keys - 2 * self.pb)
         self.edge_q = -(-self.edge // LANES) * LANES
-        self.inner_q = -(-self.inner // LANES) * LANES
-        self.queries = self.edge_q + self.inner_q
+        self.queries = -(-4 * self.keys // LANES) * LANES
         self.echunk = (width + hidden) // n_dp
         self.half = width - 2 * LANES
         self.wrows = 2 * width + width // 2
@@ -681,18 +679,38 @@
             arrived(buf.at[dpx(2 * kz + 1)], base + 3 + kz if kz else base)
             each(2 * kz + 1)
 
-        steps = [handle(lambda kz=kz: along(kz)) for kz in (1, 2, 3)] + [handle(lambda: across(0))]
+        steps = [handle(lambda kz=kz: along(kz)) for kz in (1, 2, 3)]
+        steps += [handle(lambda kz=kz: across(kz)) for kz in range(4)]
 
         def mid():
+            for step in steps[:4]:
+                step()
+
+        def finish():
             for step in steps:
                 step()
 
+        return handle(finish), mid, steps
+
+    def dp_pick(buf, chosen, out, came):
+        base = take(4)
+        z = d // 2
+        for kz in (3, 2, 1):
+            send(buf.at[z], buf.at[z], base + kz, (dpx(2 * kz), m))
+
+        def middle():
+            for kz in (1, 2, 3):
+                arrived(buf.at[dpx(2 * kz) // 2], base + kz)
+            out[...] = chosen(*beside(dpx(1)))
+            send(out, came, base, (dpx(1), m))
+
+        mid = handle(middle)
+
         def finish():
             mid()
-            for kz in (1, 2, 3):
-                across(kz)
-
-        return handle(finish), mid, steps
+            arrived(came, base)
+
+        return handle(finish), mid
 
     def mp_scatter(block, dst, landed):
         base = take(4)
@@ -806,8 +824,17 @@
     side = jnp.where(mask_ref[sz.cols - 1] > 0, FRAME, SIDE_SMALL)
     tile = slot_ref[1, d]
     tiles = [slot_ref[1, k] for k in range(sz.n_dp)]
-    above = sum(jnp.where(tiles[k] == tile - 1, k, 0) for k in range(sz.n_dp))
-    below = sum(jnp.where(tiles[k] == tile + 1, k, 0) for k in range(sz.n_dp))
+
+    def beside(at):
+        t = slot_ref[1, at]
+        up = sum(jnp.where(tiles[k] == t - 1, k, 0) for k in range(sz.n_dp))
+        down = sum(jnp.where(tiles[k] == t + 1, k, 0) for k in range(sz.n_dp))
+        return up, down
+
+    above, below = beside(d)
+
+    def same_x(j):
+        return lax.rem(j, 2) == lax.rem(d, 2)
 
     def place(p, count):
         a = sum(jnp.where(p >= PB * k, 1, 0) for k in range(1, count))
@@ -859,37 +886,34 @@
                     parts.append(jnp.concatenate(rows, axis=0))
                 yield i, j, jnp.concatenate(parts, axis=1)
 
+    def from_queries(rows, p):
+        n = rows.shape[1]
+        return jnp.concatenate([rows[KEYS * p : KEYS * (p + 1)], jnp.zeros((PL - KEYS, n), F32)], axis=0)
+
     def to_queries(planes):
         n = planes[0].shape[1]
-        edge = [v for p in planes for v in (p[0:PB], p[KEYS - PB : KEYS])]
-        inner = [p[PB : KEYS - PB] for p in planes]
-        return jnp.concatenate(
-            edge + [jnp.zeros((sz.edge_q - sz.edge, n), F32)]
-            + inner + [jnp.zeros((sz.inner_q - sz.inner, n), F32)],
-            axis=0,
-        )
-
-    def from_queries(edge, inner, p):
-        n = KEYS - 2 * PB
-        return jnp.concatenate(
-            [
-                edge[2 * PB * p : 2 * PB * p + PB], inner[n * p : n * (p + 1)],
-                edge[2 * PB * p + PB : 2 * PB * (p + 1)], jnp.zeros((PL - KEYS, edge.shape[1]), F32),
-            ],
-            axis=0,
-        )
+        rows = [v[0:KEYS] for v in planes]
+        return jnp.concatenate(rows + [jnp.zeros((sz.queries - 4 * KEYS, n), F32)], axis=0)
 
     xt, dfm = s["xt"], s["dfm"]
     pl.semaphore_wait(bar, len(peers))
     pix_ref.ready()
     x_at, x_mid = mp_start(xt)
 
+    edge, edge_g, EP = s["edge"], s["edge_g"], 4 * PB
+    lane_pad = jnp.zeros((FS, sz.edge_q - 2 * EP), BF)
+    edge[d // 2] = jnp.concatenate([xt[m, :, 0:EP], xt[m, :, sz.tokens - EP :], lane_pad], axis=1)
+
+    def edge_chosen(up, down):
+        return jnp.concatenate([edge[up // 2][:, EP : 2 * EP], edge[down // 2][:, 0:EP], lane_pad], axis=1)
+
+    edge_at, edge_mid = dp_pick(edge, edge_chosen, s["edge_s"], s["edge_x"])
+
     for i, j, value in to_planes(lambda lo, hi: cot_ref[lo:hi, :]):
         dfm[plane(2 * i + j), :] = (value * token_mask(i, j)).astype(BF)
     dyh, dyh_g = s["dyh"], s["dyh_g"]
-    dyh[d, :, :D] = dfm[pl.ds(pl.multiple_of(PL * m + (KEYS - PB) * (m // 2), 16), 48), :]
-    dyh[d, :, D:] = jnp.zeros((48, W - D), BF)
-    dy_at, _, _ = dp_start(dyh)
+    dyh[d // 2, :, :D] = dfm[pl.ds(pl.multiple_of(PL * m + (KEYS - PB) * (m // 2), 16), 48), :]
+    dyh[d // 2, :, D:] = jnp.zeros((48, W - D), BF)
     x_mid()
 
     r2, c2 = iota((D, LANES), 0), iota((D, LANES), 1)
@@ -906,6 +930,85 @@
     nil = jnp.zeros((1, HF), F32)
     bkv = jnp.concatenate([nil, own_part(bv, HF)], axis=1)
     bkv5 = jnp.concatenate([nil, bv[:, last:]], axis=1)
+    w2 = w2_ref[...]
+    wr_t = s["wr_t"]
+    wr_t[...] = wr_ref[...].T
+
+    xm_r, n1_r = s["xm_r"], s["n1_r"]
+    x_at()
+    x_all = xt[...].reshape(D, sz.tokens)
+    for i, j, value in to_planes(lambda lo, hi: x_all[lo:hi, :]):
+        xm = value * token_mask(i, j)
+        xm_r[plane(2 * i + j), :] = xm.astype(BF)
+        xhat, _ = spread(xm)
+        n1_r[plane(2 * i + j), :] = (xhat * vec(ln1g_ref) + vec(ln1b_ref)).astype(BF)
+
+    kva, xr_r = s["kva"], s["xr_r"]
+    red = sum(nn(n1_r[plane(p), :], wr_t[D * p : D * (p + 1), :]) for p in range(4)) + vec(br_ref)
+    xhr, rsr = spread(red)
+    s["xhr_r"][...] = xhr
+    s["rsr_r"][...] = jnp.broadcast_to(rsr, (PL, LANES))
+    xr_r[...] = (xhr * vec(lnrg_ref) + vec(lnrb_ref)).astype(BF)
+    kva[d, 0:PL, :] = (nn(xr_r[...], wkv) + bkv).astype(BF)
+    quarter_rows = pl.ds(pl.multiple_of(sz.step * m, 16), sz.quarter)
+    kva[d, PL:, :] = (nn(xr_r[quarter_rows, :], wkv5) + bkv5).astype(BF)
+    _, _, kv_steps = dp_start(kva)
+
+    def dy_chosen(up, down):
+        return dyh[jnp.where(m >= 2, up, down) // 2]
+
+    dy_at, dy_mid = dp_pick(dyh, dy_chosen, s["dyh_s"], s["dyh_x"])
+
+    qa_r, qb_r, qc_r, qd_r = s["qa_r"], s["qb_r"], s["qc_r"], s["qd_r"]
+    Q = sz.queries
+
+    def feature_major(q_rows, own_r, last_r):
+        q2t = q_rows.T
+        nil = jnp.zeros((HF, q2t.shape[1]), F32)
+        own_r[...] = jnp.concatenate([q2t[0:HF], nil], axis=0).astype(BF)
+        last_r[...] = jnp.concatenate([q2t[HF:], nil], axis=0).astype(BF)
+
+    def query(rows):
+        return (nn(rows, wq2) + bq2).astype(BF).astype(F32) * HF ** (-0.5)
+
+    q2 = query(n1_r[...])
+    feature_major(to_queries([q2[plane(p)] for p in range(4)]), qa_r, qb_r)
+    half = jnp.zeros((HF, Q), F32)
+
+    e5buf, ebuf, ot_r = s["e5buf"], s["ebuf"], s["ot_r"]
+    limit5 = jnp.where(m == sz.n_mp - 1, KEYS - sz.step * m, sz.step)
+    pk, pk5 = iota((PL, 1), 0), iota((sz.quarter, 1), 0)
+
+    def attend(kv, q_r, bias, ebuf, o_r):
+        v = nn(kv, q_r[...]) + bias
+        top = jnp.max(v, axis=0, keepdims=True)
+        e = jnp.exp(v - top).astype(BF)
+        if ebuf is not None:
+            ebuf[...] = e
+        o_r[...] = tn(kv, e)[HF:]
+        return top, rowsum(e.astype(F32))
+
+    def biases(j):
+        return (
+            key_bias(pk, slot_ref[1, j]),
+            jnp.where(pk5 < limit5, key_bias(pk5 + sz.step * m, slot_ref[1, j]), NEG),
+        )
+
+    own, five, own_h, five_h = ([None] * sz.n_dp for _ in range(4))
+
+    def block(k):
+        j = dpx(k)
+        bias, bias5 = biases(j)
+        own[k] = attend(kva[j, 0:PL, :], qa_r, bias, ebuf.at[j], s["o_own"].at[k])
+        five[k] = attend(kva[j, PL:, :], qb_r, bias5, e5buf.at[j], s["o_five"].at[k])
+
+    def block_h(k):
+        j = dpx(k)
+        bias, bias5 = biases(j)
+        own_h[k] = attend(kva[j, 0:PL, :], qc_r, bias, None, s["oh_own"].at[k])
+        five_h[k] = attend(kva[j, PL:, :], qd_r, bias5, None, s["oh_five"].at[k])
+
+    block(0)
     rt, ct = iota((D, 4 * LANES), 0), iota((D, 4 * LANES), 1)
     lane4, head4 = ct & (LANES - 1), ct >> 7
     place_out = hot((lane4 < FS) & (rt == FS * head4 + lane4))
@@ -919,144 +1022,112 @@
     wq_cat[...] = nn(
         wq, hot(rt == jnp.where(lane4 < HF, HF * head4 + lane4, last + lane4 - HF))
     ).astype(BF)
-    w2 = w2_ref[...]
     w2_t[...] = w2.T
     wo = wo_ref[...]
     wo_cat[...] = jnp.concatenate(
         [b for h in range(4) for b in (wo[HF * h : HF * (h + 1)], wo[last:])], axis=0
     )
-    wr_t = s["wr_t"]
-    wr_t[...] = wr_ref[...].T
-
-    xm_r, n1_r = s["xm_r"], s["n1_r"]
-    x_at()
-    x_all = xt[...].reshape(D, sz.tokens)
-    for i, j, value in to_planes(lambda lo, hi: x_all[lo:hi, :]):
-        xm = value * token_mask(i, j)
-        xm_r[plane(2 * i + j), :] = xm.astype(BF)
-        xhat, _ = spread(xm)
-        n1_r[plane(2 * i + j), :] = (xhat * vec(ln1g_ref) + vec(ln1b_ref)).astype(BF)
-
-    kva, xr_r = s["kva"], s["xr_r"]
-    red = sum(nn(n1_r[plane(p), :], wr_t[D * p : D * (p + 1), :]) for p in range(4)) + vec(br_ref)
-    xhr, rsr = spread(red)
-    s["xhr_r"][...] = xhr
-    s["rsr_r"][...] = jnp.broadcast_to(rsr, (PL, LANES))
-    xr_r[...] = (xhr * vec(lnrg_ref) + vec(lnrb_ref)).astype(BF)
-    kva[d, 0:PL, :] = (nn(xr_r[...], wkv) + bkv).astype(BF)
-    quarter_rows = pl.ds(pl.multiple_of(sz.step * m, 16), sz.quarter)
-    kva[d, PL:, :] = (nn(xr_r[quarter_rows, :], wkv5) + bkv5).astype(BF)
-    kv_at, _, _ = dp_start(kva)
-
-    qa_r, qb_r = s["qa_r"], s["qb_r"]
-    Q = sz.queries
-    q2 = (nn(n1_r[...], wq2) + bq2).astype(BF).astype(F32) * HF ** (-0.5)
-    q2t = to_queries([q2[plane(p)] for p in range(4)]).T
-    half = jnp.zeros((HF, Q), F32)
-    qa_r[...] = jnp.concatenate([q2t[0:HF], half], axis=0).astype(BF)
-    qb_r[...] = jnp.concatenate([q2t[HF:], half], axis=0).astype(BF)
-
-    dy_at()
-    dyh_g[m] = dyh[jnp.where(m >= 2, above, below)]
-    dyg_at, dyg_mid = mp_start(dyh_g)
-
     dgx, dzx = s["dgx"], s["dzx"]
     for p in range(4):
         dgx[p, sz.top : sz.top + PL, :] = nt(dfm[plane(p), :], w2).astype(BF).astype(F32)
-    limit5 = jnp.where(m == sz.n_mp - 1, KEYS - sz.step * m, sz.step)
-    pk = iota((sz.quarter, 1), 0)
-    bias5 = jnp.concatenate(
-        [
-            jnp.where(pk < limit5, key_bias(pk + sz.step * m, tiles[k]), NEG)
-            for k in range(sz.n_dp)
-        ],
-        axis=0,
-    )
-    dyg_mid()
-    kv_at()
-
-    e5buf, ebuf, sbuf, row_r, ot_r = s["e5buf"], s["ebuf"], s["sbuf"], s["row_r"], s["ot_r"]
-    kv5 = kva[:, PL:, :].reshape(sz.n_dp * sz.quarter, LANES)
-    chunks = ((0, sz.edge_q, s["lse_a"], s["og_a"]), (sz.edge_q, sz.queries, s["lse_b"], s["og_b"]))
-    fives = []
-    for lo, hi, lse_r, _ in chunks:
-        s5 = nn(kv5, qb_r[:, lo:hi]) + bias5
-        m5 = jnp.max(s5, axis=0, keepdims=True)
-        e5 = jnp.exp(s5 - m5).astype(BF)
-        l5 = rowsum(e5.astype(F32))
-        e5buf[:, :, lo:hi] = e5.reshape(sz.n_dp, sz.quarter, hi - lo)
-        lse_r[m] = jnp.broadcast_to(m5 + jnp.log(l5), (8, hi - lo))
-        at = mp_scatter(
-            lambda h, r=lse_r: r.at[m], lambda k, r=lse_r: r.at[m], lambda k, r=lse_r: r.at[mpx(k)]
-        )
-        fives.append((m5, tn(kv5, e5), at))
-
-    pk = iota((PL, 1), 0)
+    edge_at()
+    up = jnp.where(
+        same_x(above), edge[above // 2][:, EP : 2 * EP].astype(F32), s["edge_x"][:, 0:EP].astype(F32)
+    )
+    down = jnp.where(
+        same_x(below), edge[below // 2][:, 0:EP].astype(F32), s["edge_x"][:, EP : 2 * EP].astype(F32)
+    )
+    edge_g[m] = jnp.concatenate([up, down, lane_pad.astype(F32)], axis=1).astype(BF)
+    edgeg_at, edgeg_mid = mp_start(edge_g)
+    kv_steps[3]()
+    block(1)
+    edgeg_mid()
+    kv_steps[0]()
+    block(2)
+    edgeg_at()
+
+    xh_r = s["xh_r"]
+    e_all = edge_g[...].reshape(D, sz.edge_q)
+    for n, ref in enumerate(lanes3):
+        ref[0 : sz.edge_q, :] = e_all[LANES * n : min(D, LANES * (n + 1))].astype(F32).T
+    rows = []
+    for i in range(2):
+        for j in range(2):
+            for a, first in ((-1, 0), (PA, EP)):
+                at = pl.ds(first + sz.cols * i + j, PB, stride=2)
+                value = jnp.concatenate([ref[at, :] for ref in lanes3], axis=1)
+                rows.append(value * row_mask(i, j, a))
+    xh = jnp.concatenate(rows, axis=0)
+    xh_r[...] = xh.astype(BF)
+    xhat, _ = spread(xh)
+    q2 = query((xhat * vec(ln1g_ref) + vec(ln1b_ref)).astype(BF))
+    q2 = jnp.concatenate([q2, jnp.zeros((sz.edge_q - sz.edge, LANES), F32)], axis=0)
+    feature_major(q2, qc_r, qd_r)
+    kv_steps[1]()
+    block(4)
+    kv_steps[2]()
+    block(6)
+    for k in (0, 1, 2, 4, 6):
+        block_h(k)
+    dy_mid()
+    for k, step in ((3, 4), (5, 5), (7, 6)):
+        kv_steps[step]()
+        block(k)
+        block_h(k)
+
+    def joined(parts, o_r):
+        top = functools.reduce(jnp.maximum, [t for t, _ in parts])
+        scale = [jnp.exp(t - top) for t, _ in parts]
+        total = sum(f * n for f, (_, n) in zip(scale, parts))
+        inv = 1.0 / total
+        scale = [f * inv for f in scale]
+        return top + jnp.log(total), scale, sum(f * o_r[k] for k, f in enumerate(scale))
+
+    lse_r, LR = s["lse_r"], (Q + sz.edge_q) // LANES
+    lse5, scale5, o5_t = joined(five, s["o_five"])
+    lse5h, _, o5h_t = joined(five_h, s["oh_five"])
+    flat = [lse5[:, LANES * n : LANES * (n + 1)] for n in range(Q // LANES)]
+    flat += [lse5h[:, LANES * n : LANES * (n + 1)] for n in range(sz.edge_q // LANES)]
+    lse_r[m] = jnp.concatenate(flat + [jnp.zeros((16 - LR, LANES), F32)], axis=0)
+    lse_at = mp_scatter(lambda h: lse_r.at[m], lambda k: lse_r.at[m], lambda k: lse_r.at[mpx(k)])
+    _, scale, o_t = joined(own, s["o_own"])
+    o2 = jnp.concatenate([o_t, o5_t], axis=0).T.astype(BF)
+    chunks = ((s["og_a"], s["ow_a"]), (s["og_b"], s["ow_b"]), (s["og_c"], s["ow_c"]))
     ogs = []
-    for (lo, hi, lse_r, og), (m5, o5t, lse_at) in zip(chunks, fives):
-
-        def score_step(j, top, lo=lo, hi=hi):
-            v = nn(kva[j, 0:PL, :], qa_r[:, lo:hi]) + key_bias(pk, slot_ref[1, j])
-            sbuf[j, :, lo:hi] = v
-            return jnp.maximum(top, jnp.max(v, axis=0, keepdims=True))
-
-        top = lax.fori_loop(0, sz.n_dp, score_step, jnp.full((1, hi - lo), NEG, F32))
-        if ogs:
-            ogs[0][1]()
-
-        def exp_step(j, total, lo=lo, hi=hi, top=top):
-            e = jnp.exp(sbuf[j, :, lo:hi] - top).astype(BF)
-            ebuf[j, :, lo:hi] = e
-            return total + rowsum(e.astype(F32))
-
-        total = lax.fori_loop(0, sz.n_dp, exp_step, jnp.zeros((1, hi - lo), F32))
-        ot = tn(
-            kva[:, 0:PL, :].reshape(sz.n_dp * PL, LANES),
-            ebuf[:, :, lo:hi].reshape(sz.n_dp * PL, hi - lo),
-        )
-        inv = 1.0 / total
-        lse_at()
-        lses = [lse_r[h][0:1] for h in range(4)]
-        lmax = jnp.maximum(jnp.maximum(lses[0], lses[1]), jnp.maximum(lses[2], lses[3]))
-        lse5 = lmax + jnp.log(sum(jnp.exp(v - lmax) for v in lses))
-        f5 = jnp.exp(m5 - lse5)
-        row_r[0:1, lo:hi] = inv
-        row_r[1:2, lo:hi] = f5
-        o2t = jnp.concatenate([ot[HF:] * inv, o5t[HF:] * f5], axis=0)
-        ot_r[:, lo:hi] = o2t
-        og[m] = o2t.T[0 : og.shape[1]].astype(BF)
+    for n in range(2):
+        og = chunks[n][0]
+        og[m] = o2[2 * KEYS * n : 2 * KEYS * (n + 1)]
         ogs.append(mp_start(og))
-
-    og_a, og_b = s["og_a"], s["og_b"]
-    hal, hal_g, h1_r, n2_r = s["hal"], s["hal_g"], s["h1_r"], s["n2_r"]
+    _, _, oh_t = joined(own_h, s["oh_own"])
+    s["og_c"][m] = jnp.concatenate([oh_t, o5h_t], axis=0).T[0 : sz.edge].astype(BF)
+    ogs.append(mp_start(s["og_c"]))
+
+    lse_at()
+    lse4 = [
+        jnp.concatenate([lse_r[h][n : n + 1] for n in range(LR)], axis=1) for h in range(4)
+    ]
+    top = functools.reduce(jnp.maximum, lse4)
+    whole = top + jnp.log(sum(jnp.exp(v - top) for v in lse4))
+    share_all = jnp.exp(jnp.concatenate(lse4 + [jnp.zeros((4, Q + sz.edge_q), F32)], axis=0) - whole).T
+    share = jnp.exp(lse5 - whole[:, 0:Q])
+
+    def weighed(n, first):
+        og, ow = chunks[n]
+        rows = og.shape[1]
+        lane = iota((rows, LANES), 1)
+        ogs[n][0]()
+        for h in range(4):
+            part = share_all[first : first + rows, h : h + 1]
+            ow[h] = (og[h].astype(F32) * jnp.where(lane < HF, 1.0, part)).astype(BF)
+        oc = jnp.concatenate([ow[h] for h in range(4)], axis=1)
+        return nn(oc, wo_cat[...]) + vec(bo_ref)
+
+    h1_r, n2_r = s["h1_r"], s["n2_r"]
 
     def second_norm(h1):
         xhat, _ = spread(h1)
         return (xhat * vec(ln2g_ref) + vec(ln2b_ref)).astype(BF)
 
-    ogs[0][0]()
-    border = pl.ds(pl.multiple_of(2 * PB * m, 16), 2 * PB)
-    oc = jnp.concatenate([og_a[h, border, :] for h in range(4)], axis=1)
-    xmine = plane_rows(xm_r, PL * m).astype(F32)
-    xmine = jnp.concatenate([xmine[0:PB], xmine[KEYS - PB : KEYS]], axis=0)
-    im, jm = m // 2, lax.rem(m, 2)
-    emask = jnp.concatenate([row_mask(im, jm, 0), row_mask(im, jm, PA - 1)], axis=0)
-    hal[d, :, :D] = second_norm(xmine + emask * (nn(oc, wo_cat[...]) + vec(bo_ref)))
-    hal[d, :, D:] = jnp.zeros((2 * PB, W - D), BF)
-    hal_at, hal_mid, hal_steps = dp_start(hal)
-    ogs[1][1]()
-
-    dyg_at()
-    for p in range(4):
-        i, j = p // 2, p % 2
-        start = sz.top - PB if i == 1 else sz.top + KEYS
-        rows = dyh_g[p][:, :D].astype(F32)[0:PB] * row_mask(i, j, -1 if i == 1 else PA)
-        dgx[p, start : start + PB, :] = nt(rows.astype(BF), w2).astype(BF).astype(F32)
-    ogs[1][0]()
-    mixed = []
-    for og in (og_a, og_b):
-        oc = jnp.concatenate([og[h] for h in range(4)], axis=1)
-        mixed.append(nn(oc, wo_cat[...]) + vec(bo_ref))
     w1, b1 = w1_ref[...], vec(b1_ref)
 
     def hidden(rows, mask):
@@ -1070,16 +1141,17 @@
         left[i, at, :] = jnp.where(b40 == 0, 0.0, pltpu.roll(src[2 * i + 1, at, :], 1, 0))
         right[i, at, :] = jnp.where(b40 == PB - 1, 0.0, pltpu.roll(src[2 * i, at, :], PB - 1, 0))
 
-    for p in range(4):
-        mask = token_mask(p // 2, p % 2)
-        h1 = xm_r[plane(p), :].astype(F32) + mask * from_queries(mixed[0], mixed[1], p)
-        h1_r[plane(p), :] = h1
-        n2_r[plane(p), :] = second_norm(h1)
-        ux[p, sz.top : sz.top + PL, :] = hidden(n2_r[plane(p), :], mask)
-    for i in range(2):
+    for n in range(2):
+        mixed = weighed(n, 2 * KEYS * n)
+        ogs[n + 1][1]()
+        for p in (2 * n, 2 * n + 1):
+            mask = token_mask(n, p % 2)
+            h1 = xm_r[plane(p), :].astype(F32) + mask * from_queries(mixed, p % 2)
+            h1_r[plane(p), :] = h1
+            n2_r[plane(p), :] = second_norm(h1)
+            ux[p, sz.top : sz.top + PL, :] = hidden(n2_r[plane(p), :], mask)
         for a in range(PA):
-            shift(ux, ul, ur, i, sz.top + PB * a)
-    hal_steps[0]()
+            shift(ux, ul, ur, n, sz.top + PB * a)
 
     wd_ref, bd_row = wd_ref.ready(), vec(bd_ref)
     g_r, du_r = s["g_r"], s["du_r"]
@@ -1130,31 +1202,32 @@
 
         return step
 
+    dy_at()
+    beside_j = jnp.where(m >= 2, above, below)
+    dyh_g[m] = jnp.where(
+        same_x(beside_j), dyh[beside_j // 2].astype(F32), s["dyh_x"][...].astype(F32)
+    ).astype(BF)
+    dyg_at, dyg_mid = mp_start(dyh_g)
+
     sums = tuple(jnp.zeros((8, C), F32) for _ in range(10))
     for i in range(2):
         for j in range(2):
             sums = lax.fori_loop(1 - i, PA - i, forward_step(i, j), sums)
-        hal_steps[1 + i]()
-    hal_at()
-    up_rows = hal[above].astype(F32)[PB:]
-    down_rows = hal[below].astype(F32)[0:PB]
-    hal_g[m] = jnp.concatenate([up_rows, down_rows], axis=0).astype(BF)
-    halg_at, _ = mp_start(hal_g)
-    for k in range(sz.n_dp):
-        e5buf[k] = (e5buf[k].astype(F32) * row_r[1:2, :]).astype(BF)
-    ogp = s["ogp"]
-    lane = iota((T, LANES), 1)
-    fifth = [sum(og[h].astype(F32) for h in range(4)) for og in (og_a, og_b)]
-    owns = [og[m].astype(F32) for og in (og_a, og_b)]
+    dyg_mid()
+    ot_r[...] = jnp.concatenate([o_t, o5_t * share], axis=0)
+    mixed = weighed(2, Q)
+    dyg_at()
     for p in range(4):
-        ogp[plane(p), :] = jnp.where(
-            lane[plane(p)] < HF, from_queries(*owns, p), from_queries(*fifth, p)
-        ).astype(BF)
-    halg_at()
+        i, j = p // 2, p % 2
+        start = sz.top - PB if i == 1 else sz.top + KEYS
+        rows = dyh_g[p][:, :D].astype(F32)[0:PB] * row_mask(i, j, -1 if i == 1 else PA)
+        dgx[p, start : start + PB, :] = nt(rows.astype(BF), w2).astype(BF).astype(F32)
+    xh = xh_r[...].astype(F32)
     for p in range(4):
         i, j = p // 2, p % 2
         mask = jnp.concatenate([row_mask(i, j, -1), row_mask(i, j, PA)], axis=0)
-        u = hidden(hal_g[p][:, :D], mask)
+        at = slice(2 * PB * p, 2 * PB * (p + 1))
+        u = hidden(second_norm(xh[at] + mask * mixed[at]), mask)
         ux[p, sz.top - PB : sz.top, :] = u[0:PB]
         ux[p, sz.top + KEYS : sz.top + KEYS + PB, :] = u[PB:]
     for i in range(2):
@@ -1198,6 +1271,19 @@
     for t in range(10):
         ve_s[t : t + 1, :C] = rowsum(sums[t])
     ve_s[10:11, :C] = rowsum(du_all.astype(F32))
+
+    for k in range(sz.n_dp):
+        j = dpx(k)
+        ebuf[j] = (ebuf[j].astype(F32) * scale[k]).astype(BF)
+        e5buf[j] = (e5buf[j].astype(F32) * (scale5[k] * share)).astype(BF)
+    ogp = s["ogp"]
+    lane = iota((PL, LANES), 1)
+    for n, (og, ow) in enumerate(chunks[:2]):
+        mine, fifth = og[m].astype(F32), sum(ow[h].astype(F32) for h in range(4))
+        for q in range(2):
+            ogp[plane(2 * n + q), :] = jnp.where(
+                lane < HF, from_queries(mine, q), from_queries(fifth, q)
+            ).astype(BF)
 
     xhat2, rstd2 = spread(plane_rows(h1_r, PL * m))
     dfp = plane_rows(dfm, PL * m).astype(F32)
@@ -1231,9 +1317,8 @@
     dr_r[m] = jnp.broadcast_to(rowsum(dot_t[HF:] * ot_r[HF:, :]), (8, Q))
     dr_at = mp_scatter(lambda h: dr_r.at[m], lambda k: dr_r.at[m], lambda k: dr_r.at[mpx(k)])
     dab_at, dab_mid = mp_start(dabg)
-    da_own = (dot_t[0:HF] * row_r[0:1, :]).astype(BF)
-    drow = rowsum(da_own.astype(F32) * ot_r[0:HF, :])
-    da_t = jnp.concatenate([half.astype(BF), da_own], axis=0)
+    drow = rowsum(dot_t[0:HF] * ot_r[0:HF, :])
+    da_t = jnp.concatenate([half, dot_t[0:HF]], axis=0).astype(BF)
     db_t = jnp.concatenate([half, dot_t[HF:]], axis=0).astype(BF)
     dqt, dqt5 = s["dqt"], s["dqt5"]
     dqt[...] = jnp.zeros_like(dqt)
@@ -1295,7 +1380,7 @@
     dq2 = (jnp.concatenate([dqt[0:HF], dqt5[0:HF]], axis=0) * HF ** (-0.5)).T
     dqs, dq_all = s["dqs"], s["dq_all"]
     for h in range(4):
-        dqs[h] = from_queries(dq2[: sz.edge_q], dq2[sz.edge_q :], h).astype(BF)
+        dqs[h] = from_queries(dq2, h).astype(BF)
     dq_at = mp_scatter(lambda h: dqs.at[h], lambda k: dq_all.at[m], lambda k: dq_all.at[mpx(k)])
     dq_all[m] = dqs[m]
     eg_ref[d] = e_at().astype(BF)
@@ -1359,7 +1444,7 @@
     vl_s[1:2, :D] = rowsum(dn1)
     vl_mid, vl_at = dp_total(vl_s, s["vl_n"], s["vl_p"])
     dxm = norm_back(dn1, vec(ln1g_ref), xhat1, rstd1)
-    gp = (token_mask(im, jm) * (s["dh1_r"][...] + dxm)).astype(BF)
+    gp = (token_mask(m // 2, lax.rem(m, 2)) * (s["dh1_r"][...] + dxm)).astype(BF)
     gpf = nn(gp, place_out).astype(BF)
     gps = s["gps"]
     for h in range(4):
@@ -1544,10 +1629,13 @@
     chunks = dict(e=(sz.echunk, W), l1=(sz.l1rows // N, LN), l2=(sz.l2rows // N, LN))
     shapes = {
         BF: dict(
-            xt=(4, sz.share, sz.tokens), dfm=(T, D), dyh=(N, 48, W), dyh_g=(4, 48, W), xm_r=(T, D), n1_r=(T, D),
+            xt=(4, sz.share, sz.tokens), dfm=(T, D), dyh=(4, 48, W), dyh_s=(48, W), dyh_x=(48, W), dyh_g=(4, 48, W),
+            edge=(4, sz.share, sz.edge_q), edge_s=(sz.share, sz.edge_q), edge_x=(sz.share, sz.edge_q),
+            edge_g=(4, sz.share, sz.edge_q), xh_r=(sz.edge, D), qc_r=(LN, sz.edge_q), qd_r=(LN, sz.edge_q), xm_r=(T, D), n1_r=(T, D),
             xr_r=(PL, D), kva=(N, sz.kvrows, LN), qa_r=(LN, Q), qb_r=(LN, Q), ebuf=(N, PL, Q),
-            e5buf=(N, sz.quarter, Q), og_a=(4, sz.edge, LN), og_b=(4, sz.inner, LN), n2_r=(T, D),
-            hal=(N, 2 * PB, W), hal_g=(4, 2 * PB, W), dub=(4, PL, C), dn2_s=(3, PL, D), dn2_n=(2, PL, D),
+            e5buf=(N, sz.quarter, Q), og_a=(4, 2 * sz.keys, LN), og_b=(4, 2 * sz.keys, LN), og_c=(4, sz.edge, LN),
+            ow_a=(4, 2 * sz.keys, LN), ow_b=(4, 2 * sz.keys, LN), ow_c=(4, sz.edge, LN), n2_r=(T, D),
+            dub=(4, PL, C), dn2_s=(3, PL, D), dn2_n=(2, PL, D),
             dn2_f=(PL, D), dos=(4, PL, LN), do_all=(4, PL, LN), dabg=(4, PL, W), ff_s=(3, sz.share, T), ff_n=(2, sz.share, T),
             ff_f=(sz.share, T), dk_x=(4, sz.kvrows, LN), dk_n=(4, sz.kvrows, LN), dk_o=(4, sz.kvrows, LN),
             dk_f=(4, sz.kvrows, LN), dkvg=(4, sz.kvrows, LN), dqs=(4, PL, LN), dq_all=(4, PL, LN),
@@ -1558,7 +1646,8 @@
         ),
         F32: dict(
             t0=(sz.tokens, LN), t1=(sz.tokens, LN), t2=(sz.tokens, D - 2 * LN), xhr_r=(PL, D), rsr_r=(PL, LN),
-            sbuf=(N, PL, Q), lse_a=(4, 8, sz.edge_q), lse_b=(4, 8, sz.inner_q), row_r=(8, Q), ot_r=(LN, Q),
+            o_own=(N, HF, Q), o_five=(N, HF, Q), oh_own=(N, HF, sz.edge_q), oh_five=(N, HF, sz.edge_q),
+            lse_r=(4, 16, LN), ot_r=(LN, Q),
             h1_r=(T, D), ux=(4, sz.ext, C), ul=(2, sz.ext, C), ur=(2, sz.ext, C), dgx=(4, sz.ext, C),
             dzx=(4, sz.ext, C), dzl=(2, sz.ext, C), dzr=(2, sz.ext, C), g_r=(4, PL, C), du_r=(4, PL, C),
             dh1_r=(PL, D), dr_r=(4, 8, Q), dqt=(LN, Q), dqt5=(LN, Q), ve_s=(16, W), ve_n=(16, W),

time: 125 us -> 119 us (0.952)
  Pallas kernels: 124 us -> 118 us
    pallas_call x1, Pallas kernels: 120 us -> 114 us  [on_device_fused(): pl.pallas_call(functools.partial(fused_body, sz, tuple(scratch)), out_sha...]
where the time goes in v4:
time: 119 us
  Pallas kernels  118 us (99%)
    pallas_call x1, Pallas kernels, on_device_fused(): pl.pallas_call(functools.partial(fused_body, sz, tuple(scratch)), out_sha...  114 us
    pallas_call x1, Pallas kernels, on_device_fused(): pl.pallas_call(functools.partial(unpack_body, sz), out_shape=outs, in_spe...  4.33 us

profile of v4, /device:TPU:0, one launch (start us, length us, event | category | flops | bytes accessed | tf_op | source)
XLA Modules:
  0.0 118.9 jit_solution(3253027848605520661)
XLA Ops:
  0.7 113.7 %fused_block.1 = (f32[832,128]{1,0:T(8,128)}, bf16[4,208,128]{2,1,0:T(8,128)(2,1)}, bf16[8,80,384]{2,1,0:T(8,128)(2,1)}, bf16[4,8,112,128]{3,2,1,0:T(8,128)(2,1)...) custom-call(s32[800]{0:T(1024)} %mask_ref.1, s32[2,8]{1,0:T(2,128)} %bitcast.10, ...), custom_call_target="tpu_custom_call" | custom-call | tf_op jit(solution)/shard_map/fused_block/pallas_call | solution.py:1666
  114.4 4.3 %unpack.1 = (bf16[80,800]{1,0:T(8,128)(2,1)}, f32[80,800]{1,0:T(8,128)}, f32[320]{0:T(512)}, f32[320]{0:T(512)}, f32[320,320]{1,0:T(8,128)}, /*index=5*/f32[320]...) custom-call(f32[832,128]{1,0:T(8,128)} %get-tuple-element.53.refs_0_, ...), custom_call_target="tpu_custom_call" | custom-call | tf_op jit(solution)/shard_map/unpack/pallas_call | solution.py:1684

commit v5 on v4

--- a/solution.py
+++ b/solution.py
@@ -480,7 +480,7 @@
 F32 = jnp.float32
 LANES = 128
 SIDE_SMALL = 64
-VMEM_MB = 56
+VMEM_MB = 52
 
 
 def nn(a, b):
@@ -544,7 +544,7 @@
         self.edge_q = -(-self.edge // LANES) * LANES
         self.queries = -(-4 * self.keys // LANES) * LANES
         self.echunk = (width + hidden) // n_dp
-        self.half = width - 2 * LANES
+        self.prows = -(-(2 * self.plane + self.plane // 2) // 16) * 16
         self.wrows = 2 * width + width // 2
         self.l2rows = -(-(self.wrows + self.share) // (16 * n_dp)) * 16 * n_dp
         self.orows = HEAD_FEATURES + HEAD_FEATURES // n_mp
@@ -574,14 +574,7 @@
     ins, refs = refs[:23], refs[23:]
     outs, refs = refs[:7], refs[7:]
     s = dict(zip(names, refs))
-    blk_ref, gp_ref, eg_ref, lg1_ref, lg2_ref, veg_ref, vlg_ref = (s["out%d" % i] for i in range(7))
-    stores = []
-
-    def store(i):
-        c = pltpu.make_async_copy(s["out%d" % i], outs[i], s["osem"].at[i])
-        c.start()
-        stores.append(c)
-
+    blk_ref, gp_ref, eg_ref, lg1_ref, lg2_ref, veg_ref, vlg_ref = outs
     D, HF, PB, PA, KEYS, PL, T = sz.width, HEAD_FEATURES, sz.pb, sz.pa, sz.keys, sz.plane, sz.all
     C, FS, W = sz.hidden, sz.share, sz.wide
     d = lax.axis_index("dp")
@@ -629,6 +622,10 @@
         c = copy(src, dst, sem, dev)
         c.start()
         pending.append(c)
+
+    def drain(keep=0):
+        while len(pending) > keep:
+            pending.pop(0).wait_send()
 
     def arrived(ref, sem):
         copy(ref, ref, sem, (d, m)).wait_recv()
@@ -931,6 +928,11 @@
     bkv = jnp.concatenate([nil, own_part(bv, HF)], axis=1)
     bkv5 = jnp.concatenate([nil, bv[:, last:]], axis=1)
     w2 = w2_ref[...]
+    wo_cat = s["wo_cat"]
+    wo = wo_ref[...]
+    wo_cat[...] = jnp.concatenate(
+        [b for h in range(4) for b in (wo[HF * h : HF * (h + 1)], wo[last:])], axis=0
+    )
     wr_t = s["wr_t"]
     wr_t[...] = wr_ref[...].T
 
@@ -953,6 +955,7 @@
     quarter_rows = pl.ds(pl.multiple_of(sz.step * m, 16), sz.quarter)
     kva[d, PL:, :] = (nn(xr_r[quarter_rows, :], wkv5) + bkv5).astype(BF)
     _, _, kv_steps = dp_start(kva)
+    edge_mid()
 
     def dy_chosen(up, down):
         return dyh[jnp.where(m >= 2, up, down) // 2]
@@ -979,57 +982,38 @@
     limit5 = jnp.where(m == sz.n_mp - 1, KEYS - sz.step * m, sz.step)
     pk, pk5 = iota((PL, 1), 0), iota((sz.quarter, 1), 0)
 
-    def attend(kv, q_r, bias, ebuf, o_r):
+    def attend(ks, rows, q_r, bias_of, ebuf, o_r):
+        js = [dpx(k) for k in ks]
+        n = rows.stop - rows.start
+        kv = jnp.concatenate([kva[j, rows, :] for j in js], axis=0)
+        bias = jnp.concatenate([bias_of(j) for j in js], axis=0)
         v = nn(kv, q_r[...]) + bias
         top = jnp.max(v, axis=0, keepdims=True)
         e = jnp.exp(v - top).astype(BF)
         if ebuf is not None:
-            ebuf[...] = e
-        o_r[...] = tn(kv, e)[HF:]
-        return top, rowsum(e.astype(F32))
-
-    def biases(j):
-        return (
-            key_bias(pk, slot_ref[1, j]),
-            jnp.where(pk5 < limit5, key_bias(pk5 + sz.step * m, slot_ref[1, j]), NEG),
-        )
-
-    own, five, own_h, five_h = ([None] * sz.n_dp for _ in range(4))
-
-    def block(k):
-        j = dpx(k)
-        bias, bias5 = biases(j)
-        own[k] = attend(kva[j, 0:PL, :], qa_r, bias, ebuf.at[j], s["o_own"].at[k])
-        five[k] = attend(kva[j, PL:, :], qb_r, bias5, e5buf.at[j], s["o_five"].at[k])
-
-    def block_h(k):
-        j = dpx(k)
-        bias, bias5 = biases(j)
-        own_h[k] = attend(kva[j, 0:PL, :], qc_r, bias, None, s["oh_own"].at[k])
-        five_h[k] = attend(kva[j, PL:, :], qd_r, bias5, None, s["oh_five"].at[k])
+            for q, j in enumerate(js):
+                ebuf[j] = e[n * q : n * (q + 1)]
+        o_r[ks[0]] = tn(kv, e)[HF:]
+        return ks, top, rowsum(e.astype(F32))
+
+    def bias_own(j):
+        return key_bias(pk, slot_ref[1, j])
+
+    def bias_last(j):
+        return jnp.where(pk5 < limit5, key_bias(pk5 + sz.step * m, slot_ref[1, j]), NEG)
+
+    own, five, own_h, five_h = [], [], [], []
+    ROWS, LAST = slice(0, PL), slice(PL, sz.kvrows)
+
+    def block(*ks):
+        own.append(attend(ks, ROWS, qa_r, bias_own, ebuf, s["o_own"]))
+        five.append(attend(ks, LAST, qb_r, bias_last, e5buf, s["o_five"]))
+
+    def block_h(*ks):
+        own_h.append(attend(ks, ROWS, qc_r, bias_own, None, s["oh_own"]))
+        five_h.append(attend(ks, LAST, qd_r, bias_last, None, s["oh_five"]))
 
     block(0)
-    rt, ct = iota((D, 4 * LANES), 0), iota((D, 4 * LANES), 1)
-    lane4, head4 = ct & (LANES - 1), ct >> 7
-    place_out = hot((lane4 < FS) & (rt == FS * head4 + lane4))
-    rk, ck = iota((D, 5 * LANES), 0), iota((D, 5 * LANES), 1)
-    lane5, head5 = ck & (LANES - 1), ck >> 7
-    w_all, wq_cat, w2_t, wo_cat = s["w_all"], s["wq_cat"], s["w2_t"], s["wo_cat"]
-    w_all[...] = (
-        nn(wk, hot((lane5 < HF) & (rk == HF * head5 + lane5)))
-        + nn(wv, hot((lane5 >= HF) & (rk == HF * head5 + lane5 - HF)))
-    ).astype(BF)
-    wq_cat[...] = nn(
-        wq, hot(rt == jnp.where(lane4 < HF, HF * head4 + lane4, last + lane4 - HF))
-    ).astype(BF)
-    w2_t[...] = w2.T
-    wo = wo_ref[...]
-    wo_cat[...] = jnp.concatenate(
-        [b for h in range(4) for b in (wo[HF * h : HF * (h + 1)], wo[last:])], axis=0
-    )
-    dgx, dzx = s["dgx"], s["dzx"]
-    for p in range(4):
-        dgx[p, sz.top : sz.top + PL, :] = nt(dfm[plane(p), :], w2).astype(BF).astype(F32)
     edge_at()
     up = jnp.where(
         same_x(above), edge[above // 2][:, EP : 2 * EP].astype(F32), s["edge_x"][:, 0:EP].astype(F32)
@@ -1040,10 +1024,12 @@
     edge_g[m] = jnp.concatenate([up, down, lane_pad.astype(F32)], axis=1).astype(BF)
     edgeg_at, edgeg_mid = mp_start(edge_g)
     kv_steps[3]()
-    block(1)
+    kv_steps[0]()
     edgeg_mid()
-    kv_steps[0]()
-    block(2)
+    block(1, 2)
+    kv_steps[1]()
+    kv_steps[2]()
+    block(4, 6)
     edgeg_at()
 
     xh_r = s["xh_r"]
@@ -1063,25 +1049,23 @@
     q2 = query((xhat * vec(ln1g_ref) + vec(ln1b_ref)).astype(BF))
     q2 = jnp.concatenate([q2, jnp.zeros((sz.edge_q - sz.edge, LANES), F32)], axis=0)
     feature_major(q2, qc_r, qd_r)
-    kv_steps[1]()
-    block(4)
-    kv_steps[2]()
-    block(6)
-    for k in (0, 1, 2, 4, 6):
-        block_h(k)
-    dy_mid()
-    for k, step in ((3, 4), (5, 5), (7, 6)):
-        kv_steps[step]()
-        block(k)
-        block_h(k)
+    block_h(0, 1, 2, 4, 6)
+    kv_steps[4]()
+    kv_steps[5]()
+    block(3, 5)
+    block_h(3, 5)
+    kv_steps[6]()
+    block(7)
+    block_h(7)
 
     def joined(parts, o_r):
-        top = functools.reduce(jnp.maximum, [t for t, _ in parts])
-        scale = [jnp.exp(t - top) for t, _ in parts]
-        total = sum(f * n for f, (_, n) in zip(scale, parts))
+        top = functools.reduce(jnp.maximum, [t for _, t, _ in parts])
+        scale = [jnp.exp(t - top) for _, t, _ in parts]
+        total = sum(f * n for f, (_, _, n) in zip(scale, parts))
         inv = 1.0 / total
         scale = [f * inv for f in scale]
-        return top + jnp.log(total), scale, sum(f * o_r[k] for k, f in enumerate(scale))
+        out = sum(f * o_r[ks[0]] for f, (ks, _, _) in zip(scale, parts))
+        return top + jnp.log(total), {k: f for f, (ks, _, _) in zip(scale, parts) for k in ks}, out
 
     lse_r, LR = s["lse_r"], (Q + sz.edge_q) // LANES
     lse5, scale5, o5_t = joined(five, s["o_five"])
@@ -1101,6 +1085,25 @@
     _, _, oh_t = joined(own_h, s["oh_own"])
     s["og_c"][m] = jnp.concatenate([oh_t, o5h_t], axis=0).T[0 : sz.edge].astype(BF)
     ogs.append(mp_start(s["og_c"]))
+    drain(12)
+    rt, ct = iota((D, 4 * LANES), 0), iota((D, 4 * LANES), 1)
+    lane4, head4 = ct & (LANES - 1), ct >> 7
+    place_out = hot((lane4 < FS) & (rt == FS * head4 + lane4))
+    rk, ck = iota((D, 5 * LANES), 0), iota((D, 5 * LANES), 1)
+    lane5, head5 = ck & (LANES - 1), ck >> 7
+    w_all, wq_cat, w2_t = s["w_all"], s["wq_cat"], s["w2_t"]
+    w_all[...] = (
+        nn(wk, hot((lane5 < HF) & (rk == HF * head5 + lane5)))
+        + nn(wv, hot((lane5 >= HF) & (rk == HF * head5 + lane5 - HF)))
+    ).astype(BF)
+    wq_cat[...] = nn(
+        wq, hot(rt == jnp.where(lane4 < HF, HF * head4 + lane4, last + lane4 - HF))
+    ).astype(BF)
+    w2_t[...] = w2.T
+    dgx, dzx = s["dgx"], s["dzx"]
+    for p in range(4):
+        dgx[p, sz.top : sz.top + PL, :] = nt(dfm[plane(p), :], w2).astype(BF).astype(F32)
+    dy_mid()
 
     lse_at()
     lse4 = [
@@ -1213,7 +1216,27 @@
     for i in range(2):
         for j in range(2):
             sums = lax.fori_loop(1 - i, PA - i, forward_step(i, j), sums)
+    for i in range(2):
+        for a in range(1, PA):
+            shift(dzx, dzl, dzr, i, sz.top + PB * (a - i))
+
+    def backward_step(i, j):
+        p = 2 * i + j
+
+        def step(a, carry):
+            start = sz.top + PB * a
+            du_r[p, pl.ds(pl.multiple_of(PB * a, 8), PB), :] = sum(
+                wd_ref[t : t + 1, :] * source((dzx, dzl, dzr), i, j, -di, -dj, start)
+                for t, (di, dj) in enumerate(TAPS)
+            )
+            return carry
+
+        return step
+
     dyg_mid()
+    for i in range(2):
+        for j in range(2):
+            lax.fori_loop(1, PA - 1, backward_step(i, j), 0)
     ot_r[...] = jnp.concatenate([o_t, o5_t * share], axis=0)
     mixed = weighed(2, Q)
     dyg_at()
@@ -1238,25 +1261,35 @@
             activation(i, j, sz.top - PB if i == 1 else sz.top + KEYS)
             sums = forward_step(i, j)((PA - 1) * i, sums)
     e_s, ve_s, vl_s = s["e_s"], s["ve_s"], s["vl_s"]
-    for i in range(2):
-        for a in range(PA + 1):
-            shift(dzx, dzl, dzr, i, sz.top + PB * (a - i))
+    shift(dzx, dzl, dzr, 0, sz.top)
+    shift(dzx, dzl, dzr, 0, sz.top + KEYS)
+    shift(dzx, dzl, dzr, 1, sz.top - PB)
+    shift(dzx, dzl, dzr, 1, sz.top + KEYS - PB)
     dub = s["dub"]
     for i in range(2):
         for j in range(2):
             p = 2 * i + j
-
-            def backward_step(a, carry, i=i, j=j, p=p):
-                start = sz.top + PB * a
-                du_r[p, pl.ds(pl.multiple_of(PB * a, 8), PB), :] = sum(
-                    wd_ref[t : t + 1, :] * source((dzx, dzl, dzr), i, j, -di, -dj, start)
-                    for t, (di, dj) in enumerate(TAPS)
-                )
-                return carry
-
-            lax.fori_loop(0, PA, backward_step, 0)
+            for a in (0, PA - 1):
+                backward_step(i, j)(a, 0)
             dub[p] = (du_r[p].astype(BF).astype(F32) * token_mask(i, j)).astype(BF)
-    dn2_mid, dn2_at = mp_sum(lambda h: nt(dub[h], w1), s["dn2_s"], s["dn2_n"], s["dn2_f"])
+    def packed(value):
+        n = value.shape[0] // 2
+        parts = [value[:, 0:LANES], value[:, LANES : 2 * LANES]]
+        parts.append(jnp.concatenate([value[0:n, 2 * LANES :], value[n:, 2 * LANES :]], axis=1))
+        return jnp.concatenate(parts, axis=0)
+
+    def unpacked(value, rows):
+        n = rows // 2
+        rest = value[2 * rows : 2 * rows + n]
+        rest = jnp.concatenate([rest[:, 0:HF], rest[:, HF:]], axis=0)
+        return jnp.concatenate([value[0:rows], value[rows : 2 * rows], rest], axis=1)
+
+    def dn2_block(h):
+        value = packed(nt(dub[h], w1))
+        rest = jnp.zeros((sz.prows - value.shape[0], LANES), F32)
+        return jnp.concatenate([value, rest], axis=0)
+
+    dn2_mid, dn2_at = mp_sum(dn2_block, s["dn2_s"], s["dn2_n"], s["dn2_f"])
     dn2_mid()
 
     gb = g_r[...].reshape(T, C).astype(BF)
@@ -1285,10 +1318,12 @@
                 lane < HF, from_queries(mine, q), from_queries(fifth, q)
             ).astype(BF)
 
+    drain(12)
+
     xhat2, rstd2 = spread(plane_rows(h1_r, PL * m))
     dfp = plane_rows(dfm, PL * m).astype(F32)
     ve_s[11:12, :D] = rowsum(dfp)
-    dn2 = dn2_at()
+    dn2 = unpacked(dn2_at(), PL)
     dh1 = dfp + norm_back(dn2, vec(ln2g_ref), xhat2, rstd2)
     dab = dh1.astype(BF)
     docat = nt(dab, wo_cat[...]).astype(BF)
@@ -1305,12 +1340,14 @@
     ve_s[15:16, :] = jnp.zeros((1, W), F32)
     ve_mid, ve_at = dp_total(ve_s, s["ve_n"], s["ve_p"])
     e_mid()
+    ve_mid()
 
     def ff_block(h):
         return nt(w2_t[pl.ds(pl.multiple_of(FS * h, 16), FS), :], gb)
 
     ff_mid, ff_at = mp_sum(ff_block, s["ff_s"], s["ff_n"], s["ff_f"])
 
+    drain(16)
     do_at()
     dr_r = s["dr_r"]
     dot_t = to_queries([do_all[p].astype(F32) for p in range(4)]).T
@@ -1325,55 +1362,62 @@
     dqt5[...] = jnp.zeros_like(dqt5)
     five_row = []
 
-    def own_keys(j):
-        kv, e = kva[j, 0:PL, :], ebuf[j]
-        ds = (e.astype(F32) * (nn(kv, da_t) - drow)).astype(BF)
-        dqt[...] += tn(kv, ds)
-        return nt(ds, qa_r[...]) + nt(e, da_t)
-
-    def last_keys(j):
-        kv, e = kva[j, PL:, :], e5buf[j]
-        ds = (e.astype(F32) * (nn(kv, db_t) - five_row[0])).astype(BF)
-        dqt5[...] += tn(kv, ds)
-        return nt(ds, qb_r[...]) + nt(e, db_t)
+    def key_grads(js, rows, ebuf, q_r, do_t, d_row, dq):
+        n = rows.stop - rows.start
+        kv = jnp.concatenate([kva[j, rows, :] for j in js], axis=0)
+        e = jnp.concatenate([ebuf[j] for j in js], axis=0)
+        ds = (e.astype(F32) * (nn(kv, do_t) - d_row)).astype(BF)
+        value = nt(ds, q_r[...]) + nt(e, do_t)
+        dq[...] += tn(kv, ds)
+        return [value[n * q : n * (q + 1)] for q in range(len(js))]
+
+    def own_keys(*ks):
+        return key_grads([dpx(k) for k in ks], ROWS, ebuf, qa_r, da_t, drow, dqt)
+
+    def last_keys(*ks):
+        return key_grads([dpx(k) for k in ks], LAST, e5buf, qb_r, db_t, five_row[0], dqt5)
 
     dk_x, dk_n, dk_o, dk_f = s["dk_x"], s["dk_n"], s["dk_o"], s["dk_f"]
+    dl_x, dl_n, dl_o, dl_f = s["dl_x"], s["dl_n"], s["dl_o"], s["dl_f"]
     dk_at = take(8)
-
-    def dk_across(kz, own):
-        dk_x[kz] = jnp.concatenate([own, last_keys(dpx(2 * kz + 1))], axis=0).astype(BF)
-        send(dk_x.at[kz], dk_n.at[kz], dk_at + kz, (dpx(1), m))
-
-    def dk_along(kz):
-        j = dpx(2 * kz)
-        value = jnp.concatenate([own_keys(j), last_keys(j)], axis=0)
+    dl_at = take(4)
+    for pair in ((2, 3), (1, 0)):
+        for kz, value in zip(pair, own_keys(*(2 * kz + 1 for kz in pair))):
+            dk_x[kz] = value.astype(BF)
+            send(dk_x.at[kz], dk_n.at[kz], dk_at + kz, (dpx(1), m))
+    dr_at()
+    five_row.append(sum(dr_r[h][0:1] for h in range(4)))
+    for kz, value in enumerate(last_keys(1, 3, 5, 7)):
+        dl_x[kz] = value.astype(BF)
+    send(dl_x, dl_n, dl_at, (dpx(1), m))
+    dab_mid()
+
+    def dk_along(kz, value):
         arrived(dk_n.at[kz], dk_at + kz)
         dk_o[kz] = (value + dk_n[kz].astype(F32)).astype(BF)
         send(dk_o.at[kz], dk_f.at[kz], dk_at + 4 + kz, (dpx(2 * kz), m))
 
-    own2 = own_keys(dpx(5))
-    own3 = own_keys(dpx(7))
-    dr_at()
-    five_row.append(sum(dr_r[h][0:1] for h in range(4)))
-    dk_across(2, own2)
-    dk_across(3, own3)
-    ve_mid()
-    dk_across(1, own_keys(dpx(3)))
-    dab_mid()
-    dk_across(0, own_keys(dpx(1)))
-    dk_along(2)
-    dk_along(3)
+    for kz, value in zip((2, 3), own_keys(4, 6)):
+        dk_along(kz, value)
     ff_mid()
-    dk_along(1)
-    dkv = jnp.concatenate([own_keys(d), last_keys(d)], axis=0)
+    value, dkv = own_keys(2, 0)
+    dk_along(1, value)
+    dkl, *values = last_keys(0, 2, 4, 6)
+    arrived(dl_n, dl_at)
+    for kz in (2, 3, 1):
+        dl_o[kz] = (values[kz - 1] + dl_n[kz].astype(F32)).astype(BF)
+        send(dl_o.at[kz], dl_f.at[kz], dl_at + kz, (dpx(2 * kz), m))
 
     def dk_finish():
         arrived(dk_n.at[0], dk_at)
-        total = dkv + dk_n[0].astype(F32)
+        total, last = dkv + dk_n[0].astype(F32), dkl + dl_n[0].astype(F32)
         for kz in (1, 2, 3):
             arrived(dk_f.at[kz], dk_at + 4 + kz)
             total = total + dk_f[kz].astype(F32)
-        return total
+        for kz in (1, 2, 3):
+            arrived(dl_f.at[kz], dl_at + kz)
+            last = last + dl_f[kz].astype(F32)
+        return jnp.concatenate([total, last], axis=0)
 
     dk_fin = handle(dk_finish)
 
@@ -1391,12 +1435,6 @@
     vl_s[...] = jnp.zeros_like(vl_s)
     vl_s[5:6, 0:LANES] = rowsum(dqp.astype(F32))
 
-    def packed(value):
-        n = value.shape[0] // 2
-        parts = [value[:, 0:LANES], value[:, LANES : 2 * LANES]]
-        parts.append(jnp.concatenate([value[0:n, 2 * LANES :], value[n:, 2 * LANES :]], axis=1))
-        return jnp.concatenate(parts, axis=0)
-
     def fill(ref, first, value):
         rest = jnp.zeros((ref.shape[0] - first - value.shape[0], LANES), F32)
         ref[first:, :] = jnp.concatenate([value, rest], axis=0).astype(BF)
@@ -1421,8 +1459,10 @@
     dq_cat = jnp.concatenate([dq_all[h] for h in range(4)], axis=1)
     dn1 = nt(dq_cat, wq_cat[...])
     xhat1, rstd1 = spread(plane_rows(xm_r, PL * m).astype(F32))
+    drain(12)
     dkv_mid()
     dkv_at()
+    l1_mid()
     rest = jnp.concatenate(
         [dkvg[h, PL : PL + sz.step, :] for h in range(3)] + [dkvg[3, PL:, :]], axis=0
     )
@@ -1433,7 +1473,6 @@
     l2_s[0 : sz.wrows, :] = packed(tn(drb, plane_rows(n1_r, PL * m))).astype(BF)
     fill(l2_s, sz.wrows, own_rows(tn(xr_r[...], rest), FS))
     l2_mid, l2_at = dp_sum(rows_of(l2_s, sz.l2rows // sz.n_dp), s["l2_n"], s["l2_o"], s["l2_f"])
-    l1_mid()
     vl_s[2:3, :D] = rowsum(dxr * xhr)
     vl_s[3:4, :D] = rowsum(dxr)
     vl_s[4:5, :D] = rowsum(drb.astype(F32))
@@ -1451,20 +1490,7 @@
         gps[h] = gpf[:, LANES * h : LANES * (h + 1)]
     gp_at = mp_scatter(lambda h: gps.at[h], lambda k: gp_ref.at[m], lambda k: gp_ref.at[mpx(k)])
     gp_ref[m] = gps[m]
-    eg_mid()
-
-    ff = ff_at().T
-    ff = jnp.concatenate([ff, jnp.zeros((T, LANES - FS), F32)], axis=1)
-    sel = hot((c2 < FS) & (r2 == FS * m + c2))
-    b2q = jnp.concatenate(
-        [own_part(vec(b2_ref), FS), jnp.zeros((1, LANES - FS), F32)], axis=1
-    )
-    for p in range(4):
-        h1 = h1_r[plane(p), :]
-        hi = h1.astype(BF)
-        h1q = nn(hi, sel) + nn((h1 - hi.astype(F32)).astype(BF), sel)
-        blk_ref[plane(p), :] = h1q + token_mask(p // 2, p % 2) * (ff[plane(p)] + b2q)
-    store(0)
+
     veg_ref[m] = ve_at()
     veg_at, _ = mp_start(veg_ref)
 
@@ -1497,11 +1523,25 @@
 
         return near, mid, relays, handle(finish)
 
+    drain(12)
     lg1_ref[m, d] = l1_at().astype(BF)
     near1, mid1, relays1, lg1_at = gather(lg1_ref)
     l2_mid()
     vl_mid()
+    eg_mid()
+    ff = ff_at().T
+    ff = jnp.concatenate([ff, jnp.zeros((T, LANES - FS), F32)], axis=1)
+    sel = hot((c2 < FS) & (r2 == FS * m + c2))
+    b2q = jnp.concatenate(
+        [own_part(vec(b2_ref), FS), jnp.zeros((1, LANES - FS), F32)], axis=1
+    )
+    for p in range(4):
+        h1 = h1_r[plane(p), :]
+        hi = h1.astype(BF)
+        h1q = nn(hi, sel) + nn((h1 - hi.astype(F32)).astype(BF), sel)
+        blk_ref[plane(p), :] = h1q + token_mask(p // 2, p % 2) * (ff[plane(p)] + b2q)
     mid1()
+    drain(24)
     lg2_ref[m, d] = l2_at().astype(BF)
     near2, mid2, relays2, lg2_at = gather(lg2_ref)
     near1()
@@ -1509,43 +1549,43 @@
     vlg_at, _ = mp_start(vlg_ref)
     for r in relays1[:4]:
         r()
+    drain(16)
     mid2()
     for r in relays1[4:]:
         r()
+    drain(24)
     near2()
+    drain(16)
     for r in relays2:
         r()
+        drain(16)
     eg_at()
-    store(2)
     gp_at()
-    store(1)
     veg_at()
-    store(5)
     lg1_at()
-    store(3)
     vlg_at()
-    store(6)
     lg2_at()
-    store(4)
-    for c in pending:
-        c.wait_send()
-    for c in stores:
-        c.wait()
+    drain()
 
 
 def unpack_body(sz, *refs):
     srcs, refs = refs[:7], refs[7:]
+    dsts, refs = refs[:23], refs[23:]
     (
         out_ref, gpix_ref, ln1g_ref, ln1b_ref, gwq_ref, gbq_ref, gwk_ref, gwv_ref, gbv_ref, gwr_ref, gbr_ref,
         lnrg_ref, lnrb_ref, gwo_ref, gbo_ref, ln2g_ref, ln2b_ref, gw1_ref, gb1_ref, gwd_ref, gbd_ref,
         gw2_ref, gb2_ref,
-    ), refs = refs[:23], refs[23:]
-    out32, gp32, sem = refs[7:]
-    order = (5, 6, 0, 1, 2, 3, 4)
-    loads = [None] * 7
-    for i in order:
-        loads[i] = Load(srcs[i], refs[i], sem.at[i])
-    blk_ref, gp_ref, eg_ref, lg1_ref, lg2_ref, veg_ref, vlg_ref = loads
+    ), outs, refs = refs[:23], refs[:23], refs[23:]
+    out32, gp32, osem = refs
+    stores = []
+
+    def store(*which):
+        for i in which:
+            c = pltpu.make_async_copy(outs[i], dsts[i], osem.at[i])
+            c.start()
+            stores.append(c)
+
+    blk_ref, gp_ref, eg_ref, lg1_ref, lg2_ref, veg_ref, vlg_ref = srcs
     D, HF, PB, PA, PL = sz.width, HEAD_FEATURES, sz.pb, sz.pa, sz.plane
     C, FS = sz.hidden, sz.share
     m = lax.axis_index("mp")
@@ -1575,6 +1615,7 @@
 
     gbq_ref[...] = head_row(5)
     gbv_ref[...] = head_row(6)
+    store(2, 3, 5, 8, 10, 11, 12, 14, 15, 16, 18, 19, 20, 22)
     for i in range(2):
         for j in range(2):
             p = 2 * i + j
@@ -1584,9 +1625,11 @@
                 gp32[at, :] = gp_ref[p].astype(F32)[PB * a : PB * (a + 1), 0:FS]
     out_ref[...] = out32[...].T.astype(BF)
     gpix_ref[...] = gp32[...].T
+    store(0, 1)
     eg = eg_ref[...].reshape(D + C, sz.wide)
     gw1_ref[...] = eg[0:D, :C].astype(F32)
     gw2_ref[...] = eg[D:, :D].astype(F32)
+    store(17, 21)
 
     def unpacked(value):
         n = value.shape[0] * 2 // 5
@@ -1601,12 +1644,17 @@
     gwq_ref[...] = jnp.concatenate([lg1[h][0:D, 0:HF] for h in range(4)] + [fifth], axis=1)
     gwk_ref[...] = jnp.concatenate([lg1[h][D : 2 * D, 0:HF] for h in range(4)] + [tail[:, 0:HF]], axis=1)
     gwv_ref[...] = jnp.concatenate([lg1[h][D : 2 * D, HF:] for h in range(4)] + [tail[:, HF:]], axis=1)
+    store(4, 6, 7)
     gwr_ref[...] = jnp.concatenate([unpacked(lg2[h][0 : sz.wrows]) for h in range(4)], axis=1)
+    store(9)
     n = HF // 4
     for h in range(4):
         wo = unpacked(lg1[h][2 * D : 2 * D + 5 * sz.orows // 2])
         gwo_ref[HF * h : HF * (h + 1), :] = wo[0:HF]
         gwo_ref[4 * HF + n * h : 4 * HF + n * (h + 1), :] = wo[HF:]
+    store(13)
+    for c in stores:
+        c.wait()
 
 
 def on_device_fused(*args):
@@ -1635,10 +1683,9 @@
             xr_r=(PL, D), kva=(N, sz.kvrows, LN), qa_r=(LN, Q), qb_r=(LN, Q), ebuf=(N, PL, Q),
             e5buf=(N, sz.quarter, Q), og_a=(4, 2 * sz.keys, LN), og_b=(4, 2 * sz.keys, LN), og_c=(4, sz.edge, LN),
             ow_a=(4, 2 * sz.keys, LN), ow_b=(4, 2 * sz.keys, LN), ow_c=(4, sz.edge, LN), n2_r=(T, D),
-            dub=(4, PL, C), dn2_s=(3, PL, D), dn2_n=(2, PL, D),
-            dn2_f=(PL, D), dos=(4, PL, LN), do_all=(4, PL, LN), dabg=(4, PL, W), ff_s=(3, sz.share, T), ff_n=(2, sz.share, T),
-            ff_f=(sz.share, T), dk_x=(4, sz.kvrows, LN), dk_n=(4, sz.kvrows, LN), dk_o=(4, sz.kvrows, LN),
-            dk_f=(4, sz.kvrows, LN), dkvg=(4, sz.kvrows, LN), dqs=(4, PL, LN), dq_all=(4, PL, LN),
+            dub=(4, PL, C), dn2_s=(3, sz.prows, LN), dn2_n=(2, sz.prows, LN),
+            dn2_f=(sz.prows, LN), dos=(4, PL, LN), do_all=(4, PL, LN), dabg=(4, PL, W), ff_s=(3, sz.share, T), ff_n=(2, sz.share, T),
+            ff_f=(sz.share, T), **{"dk_" + k: (4, PL, LN) for k in "xnof"}, **{"dl_" + k: (4, sz.quarter, LN) for k in "xnof"}, dkvg=(4, sz.kvrows, LN), dqs=(4, PL, LN), dq_all=(4, PL, LN),
             e_s=(D + C, W), gps=(4, PL, LN), wr_t=(4 * D, D), ogp=(T, LN),
             w2_t=(D, C), w_all=(D, 5 * LN), wq_cat=(D, 4 * LN), wo_cat=(4 * LN, D), l1_s=(sz.l1rows, LN),
             l2_s=(sz.l2rows, LN),
@@ -1659,21 +1706,18 @@
         scratch["in%d" % i] = pltpu.VMEM(ins[i].shape, ins[i].dtype)
     scratch["ssem"] = pltpu.SemaphoreType.DMA((200,))
     scratch["rsem"] = pltpu.SemaphoreType.DMA((200,))
-    for i, v in enumerate(mids):
-        scratch["out%d" % i] = pltpu.VMEM(v.shape, v.dtype)
-    scratch["osem"] = pltpu.SemaphoreType.DMA((len(mids),))
     scratch["isem"] = pltpu.SemaphoreType.DMA((len(ins),))
     mid = pl.pallas_call(
         functools.partial(fused_body, sz, tuple(scratch)),
-        out_shape=mids,
+        out_shape=[pltpu.VMEM(v.shape, v.dtype) for v in mids],
         in_specs=[sm, sm] + [hbm] * len(ins),
-        out_specs=[hbm] * len(mids),
+        out_specs=[vm] * len(mids),
         scratch_shapes=list(scratch.values()),
         compiler_params=pltpu.CompilerParams(
             collective_id=0, has_side_effects=True, vmem_limit_bytes=VMEM_MB * 2**20
         ),
         name="fused_block",
-    )(pixel_mask, tile_slot.T, *ins)
+    )(pixel_mask, tile_slot.T, *(pltpu.with_memory_space_constraint(v, pltpu.HBM) for v in ins))
     outs = [
         S((sz.share, sz.tokens), BF), S((sz.share, sz.tokens), F32), S((D,), F32), S((D,), F32), S((D, D), F32),
         S((D,), F32), S((D, D), F32), S((D, D), F32), S((D,), F32), S((D, 4 * D), F32), S((D,), F32), S((D,), F32),
@@ -1684,12 +1728,12 @@
         pl.pallas_call(
             functools.partial(unpack_body, sz),
             out_shape=outs,
-            in_specs=[hbm] * len(mids),
-            out_specs=[vm] * len(outs),
-            scratch_shapes=[pltpu.VMEM(v.shape, v.dtype) for v in mids]
+            in_specs=[vm] * len(mids),
+            out_specs=[hbm] * len(outs),
+            scratch_shapes=[pltpu.VMEM(v.shape, v.dtype) for v in outs]
             + [pltpu.VMEM((sz.tokens, sz.share), F32)] * 2
-            + [pltpu.SemaphoreType.DMA((len(mids),))],
-            compiler_params=pltpu.CompilerParams(vmem_limit_bytes=60 * 2**20),
+            + [pltpu.SemaphoreType.DMA((len(outs),))],
+            compiler_params=pltpu.CompilerParams(vmem_limit_bytes=40 * 2**20),
             name="unpack",
         )(*mid)
     )

time: 119 us -> 113 us (0.950)
  Pallas kernels: 118 us -> 112 us
    pallas_call x1, Pallas kernels: 114 us -> 109 us  [on_device_fused(): pl.pallas_call(functools.partial(fused_body, sz, tuple(scratch)), out_sha...]
    pallas_call x1, Pallas kernels: 4.33 us -> 3.08 us  [on_device_fused(): pl.pallas_call(functools.partial(unpack_body, sz), out_shape=outs, in_spe...]
where the time goes in v5:
time: 113 us
  Pallas kernels  112 us (99%)
    pallas_call x1, Pallas kernels, on_device_fused(): pl.pallas_call(functools.partial(fused_body, sz, tuple(scratch)), out_sha...  109 us
    pallas_call x1, Pallas kernels, on_device_fused(): pl.pallas_call(functools.partial(unpack_body, sz), out_shape=outs, in_spe...  3.08 us

profile of v5, /device:TPU:0, one launch (start us, length us, event | category | flops | bytes accessed | tf_op | source)
XLA Modules:
  0.0 112.7 jit_solution(8384544438947103068)
XLA Ops:
  0.7 108.7 %fused_block.1 = (f32[832,128]{1,0:T(8,128)S(1)}, bf16[4,208,128]{2,1,0:T(8,128)(2,1)S(1)}, bf16[8,80,384]{2,1,0:T(8,128)(2,1)S(1)}, bf16[4,8,112,128]{3,2,1,0:T...) custom-call(s32[800]{0:T(1024)} %mask_ref.1, ...), custom_call_target="tpu_custom_call" | custom-call | tf_op jit(solution)/shard_map/fused_block/pallas_call | solution.py:1710
  109.4 3.1 %unpack.1 = (bf16[80,800]{1,0:T(8,128)(2,1)}, f32[80,800]{1,0:T(8,128)}, f32[320]{0:T(512)}, f32[320]{0:T(512)}, f32[320,320]{1,0:T(8,128)}, /*index=5*/f32[320]...) custom-call(f32[832,128]{1,0:T(8,128)S(1)} %get-tuple-element.53.ref, ...), custom_call_target="tpu_custom_call" | custom-call | tf_op jit(solution)/shard_map/unpack/pallas_call | solution.py:1728

commit v6 on v5

--- a/solution.py
+++ b/solution.py
@@ -733,10 +733,10 @@
 
     def mp_sum(block, out, near, far):
         base = take(3)
+        out[1] = block(mpx(3)).astype(BF)
+        send(out.at[1], near.at[1], base + 1, (d, mpx(1)))
         out[0] = block(mpx(1)).astype(BF)
         send(out.at[0], near.at[0], base, (d, mpx(1)))
-        out[1] = block(mpx(3)).astype(BF)
-        send(out.at[1], near.at[1], base + 1, (d, mpx(1)))
 
         def middle():
             value = block(mpx(2))
@@ -960,8 +960,6 @@
     def dy_chosen(up, down):
         return dyh[jnp.where(m >= 2, up, down) // 2]
 
-    dy_at, dy_mid = dp_pick(dyh, dy_chosen, s["dyh_s"], s["dyh_x"])
-
     qa_r, qb_r, qc_r, qd_r = s["qa_r"], s["qb_r"], s["qc_r"], s["qd_r"]
     Q = sz.queries
 
@@ -1027,9 +1025,6 @@
     kv_steps[0]()
     edgeg_mid()
     block(1, 2)
-    kv_steps[1]()
-    kv_steps[2]()
-    block(4, 6)
     edgeg_at()
 
     xh_r = s["xh_r"]
@@ -1049,7 +1044,12 @@
     q2 = query((xhat * vec(ln1g_ref) + vec(ln1b_ref)).astype(BF))
     q2 = jnp.concatenate([q2, jnp.zeros((sz.edge_q - sz.edge, LANES), F32)], axis=0)
     feature_major(q2, qc_r, qd_r)
-    block_h(0, 1, 2, 4, 6)
+    kv_steps[1]()
+    block_h(0, 1, 2)
+    kv_steps[2]()
+    dy_at, dy_mid = dp_pick(dyh, dy_chosen, s["dyh_s"], s["dyh_x"])
+    block(4, 6)
+    block_h(4, 6)
     kv_steps[4]()
     kv_steps[5]()
     block(3, 5)
@@ -1340,7 +1340,6 @@
     ve_s[15:16, :] = jnp.zeros((1, W), F32)
     ve_mid, ve_at = dp_total(ve_s, s["ve_n"], s["ve_p"])
     e_mid()
-    ve_mid()
 
     def ff_block(h):
         return nt(w2_t[pl.ds(pl.multiple_of(FS * h, 16), FS), :], gb)
@@ -1349,11 +1348,13 @@
 
     drain(16)
     do_at()
+    ve_mid()
     dr_r = s["dr_r"]
     dot_t = to_queries([do_all[p].astype(F32) for p in range(4)]).T
-    dr_r[m] = jnp.broadcast_to(rowsum(dot_t[HF:] * ot_r[HF:, :]), (8, Q))
+    d_row = rowsum(dot_t[HF:] * ot_r[HF:, :])
+    d_row = [d_row[:, LANES * n : LANES * (n + 1)] for n in range(Q // LANES)]
+    dr_r[m] = jnp.concatenate(d_row + [jnp.zeros((8 - len(d_row), LANES), F32)], axis=0)
     dr_at = mp_scatter(lambda h: dr_r.at[m], lambda k: dr_r.at[m], lambda k: dr_r.at[mpx(k)])
-    dab_at, dab_mid = mp_start(dabg)
     drow = rowsum(dot_t[0:HF] * ot_r[0:HF, :])
     da_t = jnp.concatenate([half, dot_t[0:HF]], axis=0).astype(BF)
     db_t = jnp.concatenate([half, dot_t[HF:]], axis=0).astype(BF)
@@ -1386,11 +1387,12 @@
             dk_x[kz] = value.astype(BF)
             send(dk_x.at[kz], dk_n.at[kz], dk_at + kz, (dpx(1), m))
     dr_at()
-    five_row.append(sum(dr_r[h][0:1] for h in range(4)))
+    dab_at, dab_mid = mp_start(dabg)
+    d_sum = sum(dr_r[h] for h in range(4))
+    five_row.append(jnp.concatenate([d_sum[n : n + 1] for n in range(Q // LANES)], axis=1))
     for kz, value in enumerate(last_keys(1, 3, 5, 7)):
         dl_x[kz] = value.astype(BF)
     send(dl_x, dl_n, dl_at, (dpx(1), m))
-    dab_mid()
 
     def dk_along(kz, value):
         arrived(dk_n.at[kz], dk_at + kz)
@@ -1399,14 +1401,15 @@
 
     for kz, value in zip((2, 3), own_keys(4, 6)):
         dk_along(kz, value)
-    ff_mid()
     value, dkv = own_keys(2, 0)
     dk_along(1, value)
+    dab_mid()
     dkl, *values = last_keys(0, 2, 4, 6)
     arrived(dl_n, dl_at)
     for kz in (2, 3, 1):
         dl_o[kz] = (values[kz - 1] + dl_n[kz].astype(F32)).astype(BF)
         send(dl_o.at[kz], dl_f.at[kz], dl_at + kz, (dpx(2 * kz), m))
+    ff_mid()
 
     def dk_finish():
         arrived(dk_n.at[0], dk_at)
@@ -1425,10 +1428,6 @@
     dqs, dq_all = s["dqs"], s["dq_all"]
     for h in range(4):
         dqs[h] = from_queries(dq2, h).astype(BF)
-    dq_at = mp_scatter(lambda h: dqs.at[h], lambda k: dq_all.at[m], lambda k: dq_all.at[mpx(k)])
-    dq_all[m] = dqs[m]
-    eg_ref[d] = e_at().astype(BF)
-    eg_at, eg_mid, _ = dp_start(eg_ref)
     l1_s, l2_s = s["l1_s"], s["l2_s"]
     dqp = dqs[...].reshape(T, LANES)
     l1_s[0:D, :] = tn(n1_r[...], dqp).astype(BF)
@@ -1452,13 +1451,14 @@
     dkv_at, dkv_mid = mp_start(dkvg)
     l1_s[D : 2 * D, :] = tn(xr_r[...], dkvb[0:PL]).astype(BF)
     l1_mid, l1_at = dp_sum(rows_of(l1_s, sz.l1rows // sz.n_dp), s["l1_n"], s["l1_o"], s["l1_f"])
+    eg_ref[d] = e_at().astype(BF)
+    eg_at, eg_mid, _ = dp_start(eg_ref)
     vl_s[6:7, 0:LANES] = jnp.concatenate(
         [rowsum(dkvb[0:PL].astype(F32))[:, HF:], rowsum(dkvb[PL:].astype(F32))[:, HF:]], axis=1
     )
-    dq_at()
-    dq_cat = jnp.concatenate([dq_all[h] for h in range(4)], axis=1)
-    dn1 = nt(dq_cat, wq_cat[...])
-    xhat1, rstd1 = spread(plane_rows(xm_r, PL * m).astype(F32))
+    dkv_mid()
+    dq_at = mp_scatter(lambda h: dqs.at[h], lambda k: dq_all.at[m], lambda k: dq_all.at[mpx(k)])
+    dq_all[m] = dqs[m]
     drain(12)
     dkv_mid()
     dkv_at()
@@ -1478,6 +1478,10 @@
     vl_s[4:5, :D] = rowsum(drb.astype(F32))
 
     wr_m = wr_t[pl.ds(pl.multiple_of(D * m, 16), D), :]
+    dq_at()
+    dq_cat = jnp.concatenate([dq_all[h] for h in range(4)], axis=1)
+    dn1 = nt(dq_cat, wq_cat[...])
+    xhat1, rstd1 = spread(plane_rows(xm_r, PL * m).astype(F32))
     dn1 = dn1 + nt(drb, wr_m)
     vl_s[0:1, :D] = rowsum(dn1 * xhat1)
     vl_s[1:2, :D] = rowsum(dn1)
@@ -1524,11 +1528,11 @@
         return near, mid, relays, handle(finish)
 
     drain(12)
+    eg_mid()
     lg1_ref[m, d] = l1_at().astype(BF)
     near1, mid1, relays1, lg1_at = gather(lg1_ref)
     l2_mid()
     vl_mid()
-    eg_mid()
     ff = ff_at().T
     ff = jnp.concatenate([ff, jnp.zeros((T, LANES - FS), F32)], axis=1)
     sel = hot((c2 < FS) & (r2 == FS * m + c2))
@@ -1697,7 +1701,7 @@
             lse_r=(4, 16, LN), ot_r=(LN, Q),
             h1_r=(T, D), ux=(4, sz.ext, C), ul=(2, sz.ext, C), ur=(2, sz.ext, C), dgx=(4, sz.ext, C),
             dzx=(4, sz.ext, C), dzl=(2, sz.ext, C), dzr=(2, sz.ext, C), g_r=(4, PL, C), du_r=(4, PL, C),
-            dh1_r=(PL, D), dr_r=(4, 8, Q), dqt=(LN, Q), dqt5=(LN, Q), ve_s=(16, W), ve_n=(16, W),
+            dh1_r=(PL, D), dr_r=(4, 8, LN), dqt=(LN, Q), dqt5=(LN, Q), ve_s=(16, W), ve_n=(16, W),
             ve_p=(4, 16, W), vl_s=(8, W), vl_n=(8, W), vl_p=(4, 8, W),
         ),
     }

time: 113 us -> 107 us (0.947)
  Pallas kernels: 112 us -> 106 us
    pallas_call x1, Pallas kernels: 109 us -> 103 us  [on_device_fused(): pl.pallas_call(functools.partial(fused_body, sz, tuple(scratch)), out_sha...]
where the time goes in v6:
time: 107 us
  Pallas kernels  106 us (99%)
    pallas_call x1, Pallas kernels, on_device_fused(): pl.pallas_call(functools.partial(fused_body, sz, tuple(scratch)), out_sha...  103 us
    pallas_call x1, Pallas kernels, on_device_fused(): pl.pallas_call(functools.partial(unpack_body, sz), out_shape=outs, in_spe...  3.08 us

profile of v6, /device:TPU:0, one launch (start us, length us, event | category | flops | bytes accessed | tf_op | source)
XLA Modules:
  0.0 107.2 jit_solution(9465135985804319539)
XLA Ops:
  0.7 103.2 %fused_block.1 = (f32[832,128]{1,0:T(8,128)S(1)}, bf16[4,208,128]{2,1,0:T(8,128)(2,1)S(1)}, bf16[8,80,384]{2,1,0:T(8,128)(2,1)S(1)}, bf16[4,8,112,128]{3,2,1,0:T...) custom-call(s32[800]{0:T(1024)} %mask_ref.1, ...), custom_call_target="tpu_custom_call" | custom-call | tf_op jit(solution)/shard_map/fused_block/pallas_call | solution.py:1714
  103.9 3.1 %unpack.1 = (bf16[80,800]{1,0:T(8,128)(2,1)}, f32[80,800]{1,0:T(8,128)}, f32[320]{0:T(512)}, f32[320]{0:T(512)}, f32[320,320]{1,0:T(8,128)}, /*index=5*/f32[320]...) custom-call(f32[832,128]{1,0:T(8,128)S(1)} %get-tuple-element.53.ref, ...), custom_call_target="tpu_custom_call" | custom-call | tf_op jit(solution)/shard_map/unpack/pallas_call | solution.py:1732

commit v7 on v6

--- a/solution.py
+++ b/solution.py
@@ -661,6 +661,10 @@
 
         return handle(finish), mid
 
+    def mp_direct(buf):
+        at = mp_scatter(lambda h: buf.at[m], lambda k: buf.at[m], lambda k: buf.at[mpx(k)])
+        return at, lambda: None
+
     def dp_start(buf, each=lambda k: None):
         base = take(7)
         for kz in (3, 2, 1):
@@ -938,6 +942,11 @@
 
     xm_r, n1_r = s["xm_r"], s["n1_r"]
     x_at()
+
+    def dy_chosen(up, down):
+        return dyh[jnp.where(m >= 2, up, down) // 2]
+    dy_at, dy_mid = dp_pick(dyh, dy_chosen, s["dyh_s"], s["dyh_x"])
+
     x_all = xt[...].reshape(D, sz.tokens)
     for i, j, value in to_planes(lambda lo, hi: x_all[lo:hi, :]):
         xm = value * token_mask(i, j)
@@ -956,9 +965,6 @@
     kva[d, PL:, :] = (nn(xr_r[quarter_rows, :], wkv5) + bkv5).astype(BF)
     _, _, kv_steps = dp_start(kva)
     edge_mid()
-
-    def dy_chosen(up, down):
-        return dyh[jnp.where(m >= 2, up, down) // 2]
 
     qa_r, qb_r, qc_r, qd_r = s["qa_r"], s["qb_r"], s["qc_r"], s["qd_r"]
     Q = sz.queries
@@ -1020,11 +1026,12 @@
         same_x(below), edge[below // 2][:, 0:EP].astype(F32), s["edge_x"][:, EP : 2 * EP].astype(F32)
     )
     edge_g[m] = jnp.concatenate([up, down, lane_pad.astype(F32)], axis=1).astype(BF)
-    edgeg_at, edgeg_mid = mp_start(edge_g)
+    edgeg_at, edgeg_mid = mp_direct(edge_g)
     kv_steps[3]()
     kv_steps[0]()
     edgeg_mid()
     block(1, 2)
+    dy_mid()
     edgeg_at()
 
     xh_r = s["xh_r"]
@@ -1047,13 +1054,19 @@
     kv_steps[1]()
     block_h(0, 1, 2)
     kv_steps[2]()
-    dy_at, dy_mid = dp_pick(dyh, dy_chosen, s["dyh_s"], s["dyh_x"])
     block(4, 6)
     block_h(4, 6)
+    dy_at()
+    beside_j = jnp.where(m >= 2, above, below)
+    dyh_g[m] = jnp.where(
+        same_x(beside_j), dyh[beside_j // 2].astype(F32), s["dyh_x"][...].astype(F32)
+    ).astype(BF)
+    dyg_at, dyg_mid = mp_direct(dyh_g)
     kv_steps[4]()
     kv_steps[5]()
     block(3, 5)
     block_h(3, 5)
+    dyg_mid()
     kv_steps[6]()
     block(7)
     block_h(7)
@@ -1103,7 +1116,6 @@
     dgx, dzx = s["dgx"], s["dzx"]
     for p in range(4):
         dgx[p, sz.top : sz.top + PL, :] = nt(dfm[plane(p), :], w2).astype(BF).astype(F32)
-    dy_mid()
 
     lse_at()
     lse4 = [
@@ -1204,13 +1216,6 @@
             return tuple(new) + (acc[9] + fold(dz),)
 
         return step
-
-    dy_at()
-    beside_j = jnp.where(m >= 2, above, below)
-    dyh_g[m] = jnp.where(
-        same_x(beside_j), dyh[beside_j // 2].astype(F32), s["dyh_x"][...].astype(F32)
-    ).astype(BF)
-    dyg_at, dyg_mid = mp_start(dyh_g)
 
     sums = tuple(jnp.zeros((8, C), F32) for _ in range(10))
     for i in range(2):
@@ -1448,7 +1453,7 @@
     dkvb = dk_fin().astype(BF)
     dkvg = s["dkvg"]
     dkvg[m] = dkvb
-    dkv_at, dkv_mid = mp_start(dkvg)
+    dkv_at, dkv_mid = mp_direct(dkvg)
     l1_s[D : 2 * D, :] = tn(xr_r[...], dkvb[0:PL]).astype(BF)
     l1_mid, l1_at = dp_sum(rows_of(l1_s, sz.l1rows // sz.n_dp), s["l1_n"], s["l1_o"], s["l1_f"])
     eg_ref[d] = e_at().astype(BF)
@@ -1496,7 +1501,7 @@
     gp_ref[m] = gps[m]
 
     veg_ref[m] = ve_at()
-    veg_at, _ = mp_start(veg_ref)
+    veg_at, _ = mp_direct(veg_ref)
 
     def gather(buf):
         base = take(3 * sz.n_dp)
@@ -1532,7 +1537,6 @@
     lg1_ref[m, d] = l1_at().astype(BF)
     near1, mid1, relays1, lg1_at = gather(lg1_ref)
     l2_mid()
-    vl_mid()
     ff = ff_at().T
     ff = jnp.concatenate([ff, jnp.zeros((T, LANES - FS), F32)], axis=1)
     sel = hot((c2 < FS) & (r2 == FS * m + c2))
@@ -1546,11 +1550,12 @@
         blk_ref[plane(p), :] = h1q + token_mask(p // 2, p % 2) * (ff[plane(p)] + b2q)
     mid1()
     drain(24)
+    vl_mid()
     lg2_ref[m, d] = l2_at().astype(BF)
     near2, mid2, relays2, lg2_at = gather(lg2_ref)
     near1()
     vlg_ref[m] = vl_at()
-    vlg_at, _ = mp_start(vlg_ref)
+    vlg_at, _ = mp_direct(vlg_ref)
     for r in relays1[:4]:
         r()
     drain(16)

time: 107 us -> 105 us (0.981)
  Pallas kernels: 106 us -> 104 us
    pallas_call x1, Pallas kernels: 103 us -> 101 us  [on_device_fused(): pl.pallas_call(functools.partial(fused_body, sz, tuple(scratch)), out_sha...]
where the time goes in v7:
time: 105 us
  Pallas kernels  104 us (99%)
    pallas_call x1, Pallas kernels, on_device_fused(): pl.pallas_call(functools.partial(fused_body, sz, tuple(scratch)), out_sha...  101 us
    pallas_call x1, Pallas kernels, on_device_fused(): pl.pallas_call(functools.partial(unpack_body, sz), out_shape=outs, in_spe...  3.08 us

profile of v7, /device:TPU:0, one launch (start us, length us, event | category | flops | bytes accessed | tf_op | source)
XLA Modules:
  0.0 105.2 jit_solution(16303108071284975653)
XLA Ops:
  0.7 101.3 %fused_block.1 = (f32[832,128]{1,0:T(8,128)S(1)}, bf16[4,208,128]{2,1,0:T(8,128)(2,1)S(1)}, bf16[8,80,384]{2,1,0:T(8,128)(2,1)S(1)}, bf16[4,8,112,128]{3,2,1,0:T...) custom-call(s32[800]{0:T(1024)} %mask_ref.1, ...), custom_call_target="tpu_custom_call" | custom-call | tf_op jit(solution)/shard_map/fused_block/pallas_call | solution.py:1719
  102.0 3.1 %unpack.1 = (bf16[80,800]{1,0:T(8,128)(2,1)}, f32[80,800]{1,0:T(8,128)}, f32[320]{0:T(512)}, f32[320]{0:T(512)}, f32[320,320]{1,0:T(8,128)}, /*index=5*/f32[320]...) custom-call(f32[832,128]{1,0:T(8,128)S(1)} %get-tuple-element.53.ref, ...), custom_call_target="tpu_custom_call" | custom-call | tf_op jit(solution)/shard_map/unpack/pallas_call | solution.py:1737
